TPU v7x, 32 devices: a whole 2x2x4 slice. The times are simulated.
32 devices in a mesh: dp: 16 (over z, x, core), tensor: 2 (over y).
Axes of the slice: x: 2, y: 2, z: 4, core: 2. Of those that a mesh axis runs over, the one named last changes fastest.
Arguments:
- frames_in: bfloat16 [16, 256, 1536], P('dp', 'tensor'), may hold values from -6 to 6
- lengths: int32 [16], P('dp'), may hold values from 85 to 256, as said below
- ln_gain: float32 [1536], replicated, may hold values from 0.5 to 2
- ln_bias: float32 [1536], replicated, may hold values from -3 to 3
- glu_weight: bfloat16 [2, 1536, 1536], P(None, 'tensor'), may hold values from -0.15625 to 0.15625
- conv_kernel: bfloat16 [32, 1536], P(None, 'tensor'), may hold values from -1 to 1
- bn_gain: float32 [1536], P('tensor'), may hold values from 0.5 to 2
- bn_bias: float32 [1536], P('tensor'), may hold values from -3 to 3
- out_weight: bfloat16 [1536, 1536], P('tensor'), may hold values from -0.15625 to 0.15625
Outputs:
- frames_out: bfloat16 [16, 256, 1536], P('dp', 'tensor')
Inputs may be any that keep to these rules, and one draw needn't show every extreme that they name: `lengths`: each span's length lies between 85 and 256; some span is full in every draw.
All inputs are finite; a program needn't handle non-finite values.
Results may differ from a plain program's by a relative error of at most 0.0095.
Values may be sent and summed in bfloat16 or wider, within the bound.
No kernel may reach another device: no remote copies, remote signals or barrier semaphores. Data moves between devices by JAX's collectives and lax.ppermute only.
A program may use at most 64 MiB of HBM per device.

v0:
```python
import jax
import jax.numpy as jnp
from jax import lax
from jax.sharding import PartitionSpec as P

KERNEL = 32


def layer_norm(rows, gain, bias):
    values = rows.astype(jnp.float32)
    center = jnp.mean(values, axis=-1, keepdims=True)
    spread = jnp.mean((values - center) ** 2, axis=-1, keepdims=True)
    return ((values - center) * lax.rsqrt(spread + 1e-05) * gain + bias).astype(jnp.bfloat16)


def contract_last(left, right):
    return lax.dot_general(
        left, right, (((1,), (1,)), ((), ())), preferred_element_type=jnp.float32
    )


def keep_same(stacked):
    return stacked


def batch_stats(conv, weight_rows, own_count, reduce_fn, spread_fn, bn_gain, bn_bias):
    local_sums = reduce_fn(jnp.sum(conv * weight_rows, axis=0)[None])[0]
    sums, count = lax.psum((local_sums, own_count), "dp")
    mean = sums / count
    mean_wide = spread_fn(mean[None])[0]
    local_squares = reduce_fn(jnp.sum(((conv - mean_wide) * weight_rows) ** 2, axis=0)[None])[0]
    squares = lax.psum(local_squares, "dp")
    var = squares / count
    scale = lax.rsqrt(var + 1e-05) * bn_gain
    wide = spread_fn(jnp.stack([scale, bn_bias]))
    return (mean_wide, wide[0], wide[1])


def per_device(
    frames_in, lengths, ln_gain, ln_bias, glu_weight, conv_kernel, bn_gain, bn_bias, out_weight
):
    rows = frames_in[0]
    width = rows.shape[1]
    chans = glu_weight.shape[1]
    normed = layer_norm(rows, ln_gain, ln_bias)
    own_count = lengths[0].astype(jnp.float32)
    taps = conv_kernel.astype(jnp.float32)
    w_glu = glu_weight.reshape(2 * chans, width)
    proj = contract_last(lax.all_gather(normed, "tensor", axis=0, tiled=True), w_glu)
    glu = (proj[:, :chans] * jax.nn.sigmoid(proj[:, chans:])).astype(jnp.bfloat16)
    total_rows = glu.shape[0]
    valid = jnp.arange(total_rows, dtype=jnp.int32) < lengths[0]
    glu = jnp.where(valid[:, None], glu, jnp.zeros_like(glu)).astype(jnp.float32)
    padded = jnp.pad(glu, ((15, KERNEL - 16), (0, 0)))
    conv = jnp.zeros_like(glu)
    for k in range(KERNEL):
        conv = conv + padded[k : k + total_rows] * taps[k]
    weight_rows = valid.astype(jnp.float32)[:, None]
    mean, scale, shift = batch_stats(
        conv, weight_rows, own_count, keep_same, keep_same, bn_gain, bn_bias
    )
    z = (conv - mean) * scale + shift
    act = (z * jax.nn.sigmoid(z)).astype(jnp.bfloat16)
    partial_cols = contract_last(lax.all_gather(act, "tensor", axis=1, tiled=True), out_weight)
    branch = lax.all_to_all(partial_cols, "tensor", split_axis=0, concat_axis=1, tiled=True)
    return (rows.astype(jnp.float32) + branch).astype(jnp.bfloat16)[None]


def solution(mesh):
    return jax.shard_map(
        per_device,
        mesh=mesh,
        in_specs=(
            P("dp", "tensor", None),
            P("dp"),
            P(),
            P(),
            P(None, "tensor", None),
            P(None, "tensor"),
            P("tensor"),
            P("tensor"),
            P("tensor", None),
        ),
        out_specs=P("dp", "tensor", None),
        check_vma=False,
    )
```

profile of v0, /device:TPU:0, one launch (start us, length us, event | category | flops | bytes accessed | tf_op | source)
XLA Modules:
  0.0 120.0 jit_solution(18058220420627045888)
XLA Ops:
  0.0 0.0 copy-start
  0.0 1.0 convert_element_type.44
  1.0 0.1 slice_reduce_fusion.30
  1.1 0.2 slice_reduce_fusion.31
  1.9 1.1 convert_reduce_fusion
  3.0 1.2 %fusion.65 = f32[128]{0:T(128)S(1)} fusion(bf16[1,128,1536]{2,1,0:T(8,128)(2,1)} %param.9, f32[128]{0:T(128)S(1)} %broadcast_multiply_fusion), kind=kLoop, calls=%fused_computation.99 | loop fusion | flops 786304 | bytes 394240 | tf_op jit(solution)/shard_map/reduce_sum | solution.py:12
  4.3 1.3 %fusion.68 = bf16[128,1536]{1,0:T(8,128)(2,1)S(1)} fusion(bf16[1,128,1536]{2,1,0:T(8,128)(2,1)} %param.9, f32[1536]{0:T(1024)} %param.12, f32[1536]{0:T(1024)} %param.11, f32[128]{0:T(128)S(1)} %add_rsqrt_fusion, f32[128]{0:T(128)S(1)} %broadcast_multiply_fusion), kind=kLoop, calls=%fused_computation.102 | loop fusion | flops 1179648 | bytes 799744 | tf_op jit(solution)/shard_map/convert_element_type | solution.py:13
  5.6 12.8 %all_gather.6 = bf16[256,1536]{1,0:T(8,128)(2,1)S(1)} all-gather(bf16[128,1536]{1,0:T(8,128)(2,1)S(1)} %fusion.68), channel_id=1, replica_groups=mesh['dp'=16,'tensor'=2] {'tensor'}, dimensions={0}, use_global_device_ids=true | all-gather | bytes 1179648 | tf_op jit(solution)/shard_map/all_gather | solution.py:49
  18.4 3.7 %fusion.77 = f32[256,1536]{1,0:T(8,128)S(1)} fusion(bf16[256,1536]{1,0:T(8,128)(2,1)S(1)} %all_gather.6, bf16[1536,1536]{1,0:T(8,128)(2,1)} %bitcast.28), kind=kOutput, calls=%fused_computation.152 | convolution fusion | flops 1207959552 | bytes 7077888 | tf_op jit(solution)/shard_map/dot_general | solution.py:17
  22.1 0.0 copy-start.3
  22.1 0.0 copy-start.2
  22.2 0.2 select_convert_fusion
  22.4 3.3 %multiply_reduce_fusion.1 = (f32[768]{0:T(1024)S(1)}, f32[256,768]{1,0:T(8,128)S(1)}) fusion(f32[256]{0:T(256)S(1)} %get-tuple-element.42, f32[768]{0:T(1024)S(1)} %get-tuple-element.6, f32[768]{0:T(1024)S(1)} %get-tuple-element.7, f32[768]{0:T(1024)S(1)} %get-tuple-element.8, f32[768]{0:T(1024)S(1)} %get-tuple-element.9, f32[768]{0:T(1024)S(1)} %get-tuple-element.10, ...), kind=kLoop, calls=%fused_computation.111 | loop fusion | flops 12778752 | bytes 1675264 | tf_op jit(solution)/shard_map/reduce_sum | solution.py:27
  25.6 33.8 %all-reduce.1 = (f32[768]{0:T(1024)S(1)}, f32[]{:T(128)}) all-reduce(f32[768]{0:T(1024)S(1)} %get-tuple-element.39, f32[]{:T(128)S(6)} %convert_element_type.46), channel_id=1, replica_groups=mesh['dp'=16,'tensor'=2] {'dp'}, use_global_device_ids=true, to_apply=%region_3.4 | all-reduce | flops 769 | bytes 6152 | tf_op jit(solution)/shard_map/psum | solution.py:28
  59.5 0.6 broadcast_divide_fusion
  60.1 0.2 multiply_reduce_fusion
  60.3 29.5 %psum.23 = f32[768]{0:T(1024)S(1)} all-reduce(f32[768]{0:T(1024)S(1)} %multiply_reduce_fusion), channel_id=1, replica_groups=mesh['dp'=16,'tensor'=2] {'dp'}, use_global_device_ids=true, to_apply=%region_6.7 | all-reduce | flops 768 | bytes 6144 | tf_op jit(solution)/shard_map/psum | solution.py:32
  89.8 0.0 copy-done.3
  89.8 0.7 rsqrt_multiply_fusion
  90.5 0.0 copy-done.2
  90.5 0.2 multiply_convert_fusion
  90.7 11.6 %all_gather.7 = bf16[256,1536]{1,0:T(8,128)(2,1)S(1)} all-gather(bf16[256,768]{1,0:T(8,128)(2,1)S(1)} %multiply_convert_fusion), channel_id=1, replica_groups=mesh['dp'=16,'tensor'=2] {'tensor'}, dimensions={1}, use_global_device_ids=true | all-gather | bytes 1179648 | tf_op jit(solution)/shard_map/all_gather | solution.py:64
  102.3 0.0 copy-done
  102.3 0.8 fusion.78
  103.1 0.0 copy-start.1
  103.1 12.8 %all_to_all.19 = f32[2,128,768]{2,1,0:T(8,128)S(1)} all-to-all(f32[2,128,768]{2,1,0:T(8,128)S(1)} %bitcast.27), channel_id=1, replica_groups=mesh['dp'=16,'tensor'=2] {'tensor'}, dimensions={0} | all-to-all | bytes 1572864 | tf_op jit(solution)/shard_map/all_to_all | solution.py:65
  115.9 0.6 copy.10
  116.5 1.5 %all_to_all.17 = f32[1,128,1536]{2,1,0:T(8,128)} reshape(f32[128,2,768]{2,1,0:T(2,128)S(1)} %copy.10) | data formatting | bytes 1572864 | tf_op jit(solution)/shard_map/all_to_all | solution.py:65
  118.0 0.0 copy-done.1
  118.0 1.9 %fusion.69 = bf16[1,128,1536]{2,1,0:T(8,128)(2,1)} fusion(f32[1,128,1536]{2,1,0:T(8,128)} %all_to_all.17, bf16[1,128,1536]{2,1,0:T(8,128)(2,1)S(1)} %copy-done.1), kind=kLoop, calls=%fused_computation.103 | loop fusion | flops 589824 | bytes 1572864 | tf_op jit(solution)/shard_map/convert_element_type | solution.py:66
  (3 shorter events, 0.0 us)
Async XLA Ops:
  0.0 102.3 %copy-start = (bf16[768,1536]{1,0:T(8,128)(2,1)S(1)}, bf16[768,1536]{1,0:T(8,128)(2,1)}, u32[]{:S(2)}) copy-start(bf16[768,1536]{1,0:T(8,128)(2,1)} %param.17) | copy-start | bytes 7077892
  22.1 67.7 %copy-start.3 = (f32[768]{0:T(1024)S(1)}, f32[768]{0:T(1024)}, u32[]{:S(2)}) copy-start(f32[768]{0:T(1024)} %param.15) | copy-start | bytes 9220
  22.1 68.3 %copy-start.2 = (f32[768]{0:T(1024)S(1)}, f32[768]{0:T(1024)}, u32[]{:S(2)}) copy-start(f32[768]{0:T(1024)} %param.16) | copy-start | bytes 9220
  103.1 14.9 %copy-start.1 = (bf16[1,128,1536]{2,1,0:T(8,128)(2,1)S(1)}, bf16[1,128,1536]{2,1,0:T(8,128)(2,1)}, u32[]{:S(2)}) copy-start(bf16[1,128,1536]{2,1,0:T(8,128)(2,1)} %param.9) | copy-start | bytes 1179652
where the time goes:
time: 120 us
  blocking collectives  100 us (83%)
  other arithmetic  11.8 us (10%)
  matrix products  4.56 us (4%)
  local copies, waits for them, and re-layouts  2.41 us (2%)
    psum x1, blocking collectives, batch_stats(): sums, count = lax.psum((local_sums, own_count), 'dp')  33.8 us
    psum x1, blocking collectives, batch_stats(): squares = lax.psum(local_squares, 'dp')  29.5 us
    all_to_all x1, blocking collectives, per_device(): lax.all_to_all(partial_cols, 'tensor', split_axis=0, concat_axis=1, tiled...  12.8 us
    all_gather x1, blocking collectives, per_device(): lax.all_gather(normed, 'tensor', axis=0, tiled=True)  12.8 us
    all_gather x1, blocking collectives, per_device(): lax.all_gather(act, 'tensor', axis=1, tiled=True)  11.6 us
    dot_general x2, matrix products, contract_last(): lax.dot_general(left, right, (((1,), (1,)), ((), ())), preferred_element_...  4.56 us
    reduce_sum x1, other arithmetic, batch_stats(): local_sums = reduce_fn(jnp.sum(conv * weight_rows, axis=0)[None])[0]  3.26 us

commit v1 on v0

v1 whole, which is shorter than its diff:
```python
import functools

import jax
import jax.numpy as jnp
from jax import lax
from jax.experimental import pallas as pl
from jax.experimental.pallas import tpu as pltpu
from jax.sharding import PartitionSpec as P

KERNEL = 32
HEAD = 16
LANES = 128
F32 = jnp.float32
BF16 = jnp.bfloat16

VMEM = pl.BlockSpec(memory_space=pltpu.VMEM)
SMEM = pl.BlockSpec(memory_space=pltpu.SMEM)


def contract_last(left, right):
    return lax.dot_general(
        left, right, (((1,), (1,)), ((), ())), preferred_element_type=F32
    )


def layer_norm(rows, gain, bias):
    values = rows.astype(F32)
    center = jnp.mean(values, axis=-1, keepdims=True)
    values = values - center
    spread = jnp.mean(values * values, axis=-1, keepdims=True)
    return (values * lax.rsqrt(spread + 1e-05) * gain + bias).astype(BF16)


def swish(z):
    return z * jax.nn.sigmoid(z)


def cuts(width, most):
    step = most if width % most == 0 else width
    return [slice(at, at + step) for at in range(0, width, step)]


def glu_of(normed, weight_ref, cut, keep):
    value = contract_last(normed, weight_ref[0, cut, :])
    gate = contract_last(normed, weight_ref[1, cut, :])
    glu = (value * jax.nn.sigmoid(gate)).astype(BF16)
    return jnp.where(keep, glu.astype(F32), 0.0)


def own_rows_valid(first, rows, length):
    index = first + lax.broadcasted_iota(jnp.int32, (rows, 1), 0)
    return index < length


def glu_kernel(shift, parts, where_ref, rows_ref, gain_ref, bias_ref, weight_ref, glu_ref):
    rows, chans = glu_ref.shape
    first = lax.rem(where_ref[0] + shift, parts) * rows
    keep = own_rows_valid(first, rows, where_ref[1])
    normed = layer_norm(rows_ref[...], gain_ref[...], bias_ref[...])
    for cut in cuts(chans, 256):
        glu_ref[:, cut] = glu_of(normed, weight_ref, cut, keep).astype(BF16)


def conv_rows(padded_ref, taps_ref, at, rows, cut):
    total = jnp.zeros((rows, cut.stop - cut.start), F32)
    for offset in range(8):
        last = 4 if offset == 0 else 3
        seen = padded_ref[at + offset : at + offset + rows + 8 * last, cut]
        for step in range(last + 1):
            tap = 8 * step + offset - 1
            if tap >= 0:
                total += seen[8 * step : 8 * step + rows] * taps_ref[tap : tap + 1, cut]
    return total


def fill_ends(padded_ref, cut):
    total = padded_ref.shape[0]
    width = cut.stop - cut.start
    padded_ref[0:HEAD, cut] = jnp.zeros((HEAD, width), F32)
    padded_ref[total - HEAD : total, cut] = jnp.zeros((HEAD, width), F32)


def place_block(padded_ref, block, slot, rows, cut):
    at = pl.multiple_of(HEAD + slot * rows, 16)
    padded_ref[pl.ds(at, rows), cut] = block


def last_block_kernel(
    parts, where_ref, rows_ref, gain_ref, bias_ref, weight_ref, early_ref, taps_ref,
    glu_ref, conv_ref, sums_ref, padded_ref,
):
    rows, chans = glu_ref.shape
    total_rows = conv_ref.shape[0]
    own, length = where_ref[0], where_ref[1]
    slot = lax.rem(own + parts - 1, parts)
    keep = own_rows_valid(slot * rows, rows, length)
    count = length.astype(F32)
    normed = layer_norm(rows_ref[...], gain_ref[...], bias_ref[...])
    valid = own_rows_valid(0, total_rows, length).astype(F32)
    for wide in cuts(chans, 256):
        glu = glu_of(normed, weight_ref, wide, keep)
        glu_ref[:, wide] = glu.astype(BF16)
        fill_ends(padded_ref, wide)
        place_block(padded_ref, glu, slot, rows, wide)
        for shift in range(parts - 1):
            place = lax.rem(own + shift, parts)
            place_block(padded_ref, early_ref[shift, :, wide].astype(F32), place, rows, wide)
        span = wide.stop - wide.start
        for narrow in cuts(span, LANES):
            cut = slice(wide.start + narrow.start, wide.start + narrow.stop)
            sums = jnp.zeros((1, cut.stop - cut.start), F32)
            for at in range(0, total_rows, rows):
                conv = conv_rows(padded_ref, taps_ref, at, rows, cut)
                conv_ref[at : at + rows, cut] = conv
                sums += jnp.sum(conv * valid[at : at + rows], axis=0, keepdims=True)
            mean = sums / count
            squares = jnp.zeros_like(sums)
            for at in range(0, total_rows, rows):
                off = (conv_ref[at : at + rows, cut] - mean) * valid[at : at + rows]
                squares += jnp.sum(off * off, axis=0, keepdims=True)
            sums_ref[:, cut] = sums
            sums_ref[:, chans + cut.start : chans + cut.stop] = squares
    sums_ref[:, 2 * chans :] = jnp.full((1, LANES), count, F32)


def conv_kernel_of_peer(shift, parts, where_ref, early_ref, late_ref, taps_ref, conv_ref, padded_ref):
    rows, chans = late_ref.shape
    total_rows = conv_ref.shape[0]
    peer = lax.rem(where_ref[0] + shift, parts)
    for cut in cuts(chans, LANES):
        fill_ends(padded_ref, cut)
        for step in range(parts - 1):
            block = early_ref[step, :, cut].astype(F32)
            place_block(padded_ref, block, lax.rem(peer + step, parts), rows, cut)
        block = late_ref[:, cut].astype(F32)
        place_block(padded_ref, block, lax.rem(peer + parts - 1, parts), rows, cut)
        for at in range(0, total_rows, rows):
            conv_ref[at : at + rows, cut] = conv_rows(padded_ref, taps_ref, at, rows, cut)


def scale_and_shift(stats_ref, place, chans):
    seen = stats_ref[:, pl.ds(place, 1), :, :]
    sums = seen[..., :chans]
    squares = seen[..., chans : 2 * chans]
    counts = seen[..., 2 * chans : 2 * chans + 1]
    count = jnp.sum(counts, axis=0)[0]
    mean = jnp.sum(sums, axis=0)[0] / count
    off = sums / counts - mean
    var = jnp.sum(squares + counts * off * off, axis=0)[0] / count
    return mean, lax.rsqrt(var + 1e-05)


def branch_rows(parts, own, slot, rows, stats_ref, conv_refs, norm_refs, weight_ref):
    chans = conv_refs[0].shape[1]
    total = None
    for shift in range(parts):
        place = lax.rem(own + shift, parts)
        mean, scale = scale_and_shift(stats_ref, place, chans)
        scale = scale * norm_refs[shift][0:1, :]
        conv = conv_refs[shift][pl.ds(pl.multiple_of(slot * rows, 16), rows), :]
        z = (conv - mean) * scale + norm_refs[shift][1:2, :]
        term = contract_last(swish(z).astype(BF16), weight_ref[place])
        total = term if total is None else total + term
    return total


def sent_kernel(parts, where_ref, stats_ref, weight_ref, *refs):
    conv_refs, norm_refs, out_ref = refs[:parts], refs[parts:-1], refs[-1]
    own = where_ref[0]
    rows = out_ref.shape[1]
    for shift in range(1, parts):
        slot = lax.rem(own + shift, parts)
        branch = branch_rows(parts, own, slot, rows, stats_ref, conv_refs, norm_refs, weight_ref)
        out_ref[shift - 1] = branch.astype(BF16)


def kept_kernel(parts, where_ref, stats_ref, weight_ref, *refs):
    conv_refs, norm_refs, out_ref = refs[:parts], refs[parts:-1], refs[-1]
    own = where_ref[0]
    rows = out_ref.shape[0]
    out_ref[...] = branch_rows(parts, own, own, rows, stats_ref, conv_refs, norm_refs, weight_ref)


def finish_kernel(parts, where_ref, rows_ref, kept_ref, *refs):
    got_refs, out_ref = refs[:-1], refs[-1]
    own = where_ref[0]
    cols = kept_ref.shape[1]
    for shift in range(parts):
        branch = kept_ref[...] if shift == 0 else got_refs[shift - 1][...].astype(F32)
        place = lax.rem(own + shift, parts)
        if cols % LANES == 0:
            at = pl.ds(pl.multiple_of(place * cols, LANES), cols)
            out_ref[:, at] = (rows_ref[:, at].astype(F32) + branch).astype(BF16)
        else:
            for block in range(parts):

                @pl.when(place == block)
                def _():
                    cut = slice(block * cols, (block + 1) * cols)
                    out_ref[:, cut] = (rows_ref[:, cut].astype(F32) + branch).astype(BF16)


def shape(dims, kind):
    return jax.ShapeDtypeStruct(dims, kind)


def call(kernel, out, operands, scratch=(), flops=0, name=None):
    single = not isinstance(out, (tuple, list))
    outs = [out] if single else list(out)
    moved = sum(x.size * x.dtype.itemsize for x in list(operands) + outs)
    result = pl.pallas_call(
        kernel,
        out_shape=tuple(outs),
        in_specs=[SMEM] + [VMEM] * (len(operands) - 1),
        out_specs=tuple([VMEM] * len(outs)),
        scratch_shapes=list(scratch),
        compiler_params=pltpu.CompilerParams(vmem_limit_bytes=32 * 1024 * 1024),
        cost_estimate=pl.CostEstimate(flops=flops, bytes_accessed=moved, transcendentals=0),
        name=name,
    )(*operands)
    return result[0] if single else result


def per_device(
    parts, devices, frames_in, lengths, ln_gain, ln_bias, glu_weight, conv_kernel, bn_gain, bn_bias,
    out_weight,
):
    rows = frames_in[0]
    span, width = rows.shape
    chans = glu_weight.shape[1]
    cols = out_weight.shape[0]
    total_rows = span * parts
    own = lax.axis_index("tensor").astype(jnp.int32)
    where = jnp.stack([own, lengths[0]])

    def from_peer(value, shift):
        pairs = [((at + shift) % parts, at) for at in range(parts)]
        return lax.ppermute(value, "tensor", pairs)

    gain, bias = ln_gain[None], ln_bias[None]
    small = jnp.concatenate([conv_kernel.astype(F32), bn_gain[None], bn_bias[None]])
    frames = [rows] + [from_peer(rows, shift) for shift in range(1, parts)]
    smalls = [small] + [from_peer(small, shift) for shift in range(1, parts)]
    taps = [each[:KERNEL] for each in smalls]
    norms = [each[KERNEL:] for each in smalls]
    weight = out_weight.reshape(cols, parts, chans).transpose(1, 0, 2)

    glu_flops = 4 * span * width * chans
    early = jnp.stack([
        call(
            functools.partial(glu_kernel, shift, parts),
            shape((span, chans), BF16),
            (where, frames[shift], gain, bias, glu_weight),
            flops=glu_flops,
            name="glu",
        )
        for shift in range(parts - 1)
    ])
    padded = pltpu.VMEM((total_rows + 2 * HEAD, chans), F32)
    late, conv, sums = call(
        functools.partial(last_block_kernel, parts),
        (
            shape((span, chans), BF16),
            shape((total_rows, chans), F32),
            shape((1, 2 * chans + LANES), F32),
        ),
        (where, frames[-1], gain, bias, glu_weight, early, taps[0]),
        scratch=(padded,),
        flops=glu_flops + 2 * KERNEL * total_rows * chans,
        name="glu_conv_sums",
    )
    spread = jnp.broadcast_to(sums[None], (devices,) + sums.shape)
    stats = lax.all_to_all(spread, ("dp", "tensor"), split_axis=0, concat_axis=0, tiled=True)
    stats = stats.reshape((devices // parts, parts) + sums.shape)

    convs = [conv]
    for shift in range(1, parts):
        convs.append(
            call(
                functools.partial(conv_kernel_of_peer, shift, parts),
                shape((total_rows, chans), F32),
                (where, from_peer(early, shift), from_peer(late, shift), taps[shift]),
                scratch=(padded,),
                flops=2 * KERNEL * total_rows * chans,
                name="conv_of_peer",
            )
        )
    operands = (where, stats, weight, *convs, *norms)
    branch_flops = 2 * span * width * cols
    sent = call(
        functools.partial(sent_kernel, parts),
        shape((parts - 1, span, cols), BF16),
        operands,
        flops=branch_flops * (parts - 1),
        name="branch_sent",
    )
    got = [from_peer(sent[parts - shift - 1], shift) for shift in range(1, parts)]
    kept = call(
        functools.partial(kept_kernel, parts),
        shape((span, cols), F32),
        operands,
        flops=branch_flops,
        name="branch_kept",
    )
    out = call(
        functools.partial(finish_kernel, parts),
        shape((span, width), BF16),
        (where, rows, kept, *got),
        name="residual",
    )
    return out[None]


def solution(mesh):
    sizes = dict(mesh.shape)
    body = functools.partial(per_device, sizes["tensor"], sizes["tensor"] * sizes["dp"])
    return jax.shard_map(
        body,
        mesh=mesh,
        in_specs=(
            P("dp", "tensor", None),
            P("dp"),
            P(),
            P(),
            P(None, "tensor", None),
            P(None, "tensor"),
            P("tensor"),
            P("tensor"),
            P("tensor", None),
        ),
        out_specs=P("dp", "tensor", None),
        check_vma=False,
    )
```

time: 120 us -> 63.4 us (0.53)
  blocking collectives: 100 us -> 0 us
  local copies, waits for them, and re-layouts: 2.41 us -> 22.6 us
  Pallas kernels: 0 us -> 16.1 us
  starting transfers between devices: 0 us -> 14.4 us
  other arithmetic: 11.8 us -> 1.52 us
  waiting for transfers between devices: 0 us -> 7.17 us
  matrix products: 4.56 us -> 0 us
    psum x2 -> x0, blocking collectives: 63.3 us -> none  [the longest x1 33.8 us: batch_stats(): sums, count = lax.psum((local_sums, own_count), 'dp')]
    all_gather x2 -> x0, blocking collectives: 24.3 us -> none  [the longest x1 12.8 us: per_device(): lax.all_gather(normed, 'tensor', axis=0, tiled=True)]
    pallas_call x0 -> x6, Pallas kernels: none -> 16.1 us  [call(): pl.pallas_call(kernel, out_shape=tuple(outs), in_specs=[SMEM] + [VMEM] *...]
    unnamed x8 -> x35, local copies, waits for them, and re-layouts: 0.02 us -> 15.4 us
    all_to_all x1 -> x0, blocking collectives: 12.8 us -> none  [per_device(): lax.all_to_all(partial_cols, 'tensor', split_axis=0, concat_axis=1, tiled...]
    ppermute x0 -> x5, starting transfers between devices: none -> 8.14 us  [from_peer(): return lax.ppermute(value, 'tensor', pairs)]
    ppermute x0 -> x5, waiting for transfers between devices: none -> 7.16 us  [from_peer(): return lax.ppermute(value, 'tensor', pairs)]
    all_to_all x0 -> x1, starting transfers between devices: none -> 6.25 us  [per_device(): lax.all_to_all(spread, ('dp', 'tensor'), split_axis=0, concat_axis=0, til...]
  transfers between devices with their start and end apart: 0 -> 6, of which waited for: 0 -> 3; matrix products, arithmetic and copies ran while one was open for 0% -> 20% of each run, Pallas kernels for 0% -> 12%
where the time goes in v1:
time: 63.4 us; the launch traced here: 62.6 us
  local copies, waits for them, and re-layouts  22.6 us (36%)
  Pallas kernels  16.1 us (25%)
  starting transfers between devices  14.4 us (23%)
  waiting for transfers between devices  7.17 us (11%)
  other arithmetic  1.52 us (2%)
  between operations  0.78 us (1%)
    pallas_call x6, Pallas kernels, call(): pl.pallas_call(kernel, out_shape=tuple(outs), in_specs=[SMEM] + [VMEM] *...  16.1 us
    unnamed x35, local copies, waits for them, and re-layouts  15.4 us
    ppermute x5, starting transfers between devices, from_peer(): return lax.ppermute(value, 'tensor', pairs)  8.14 us
    ppermute x5, waiting for transfers between devices, from_peer(): return lax.ppermute(value, 'tensor', pairs)  7.16 us
    all_to_all x1, starting transfers between devices, per_device(): lax.all_to_all(spread, ('dp', 'tensor'), split_axis=0, concat_axis=0, til...  6.25 us
    reshape x1, local copies, waits for them, and re-layouts, per_device(): weight = out_weight.reshape(cols, parts, chans).transpose(1, 0, 2)  2.84 us
    broadcast_in_dim x2, local copies, waits for them, and re-layouts, per_device(): gain, bias = (ln_gain[None], ln_bias[None])  1.4 us
    slice x1, local copies, waits for them, and re-layouts, per_device(): norms = [each[KERNEL:] for each in smalls]  1.33 us
  transfers between devices with their start and end apart: 6, of which 3 were waited for; matrix products, arithmetic and copies ran while one was open for 20% of the time, Pallas kernels for 12%

profile of v1, /device:TPU:0, one launch (start us, length us, event | category | flops | bytes accessed | tf_op | source)
XLA Modules:
  0.0 62.6 jit_solution(5724296824642422601)
XLA Ops:
  0.0 3.0 %collective-permute-start = (bf16[128,1536]{1,0:T(8,128)(2,1)}, bf16[128,1536]{1,0:T(8,128)(2,1)S(1)}, u32[]{:S(2)}, u32[]{:S(2)}) collective-permute-start(bf16[128,1536]{1,0:T(8,128)(2,1)} %bitcast.12), channel_id=1, source_target_pairs={{1,0},{0,1},{3,2},{2,3},{5,4},{4,5},{7,6},{6,7},{9,8},{8,9},{11,10... | collective-permute-start | bytes 1179656 | tf_op jit(solution)/shard_map/ppermute | solution.py:238
  3.6 0.7 %broadcast_in_dim.23.gain_ref = f32[1,1536]{1,0:T(1,128)S(1)} reshape(f32[1536]{0:T(1024)} %param.11) | data formatting | bytes 12288 | tf_op jit(solution)/shard_map/broadcast_in_dim | solution.py:240
  4.3 0.7 %broadcast_in_dim.24.bias_ref = f32[1,1536]{1,0:T(1,128)S(1)} reshape(f32[1536]{0:T(1024)} %param.12) | data formatting | bytes 12288 | tf_op jit(solution)/shard_map/broadcast_in_dim | solution.py:240
  5.0 0.8 %convert_element_type.3.taps_ref = f32[32,768]{1,0:T(8,128)S(1)} convert(bf16[32,768]{1,0:T(8,128)(2,1)} %param.14) | non-fusion elementwise | flops 24576 | bytes 147456 | tf_op jit(solution)/shard_map/convert_element_type | solution.py:241
  5.9 2.3 %copy-done = bf16[2,768,1536]{2,1,0:T(8,128)(2,1)S(1)} copy-done((bf16[2,768,1536]{2,1,0:T(8,128)(2,1)S(1)}, bf16[2,768,1536]{2,1,0:T(8,128)(2,1)}, u32[]{:S(2)}) %copy-start) | copy-done | bytes 4718616
  8.2 1.0 %copy-done.4 = bf16[1,128,1536]{2,1,0:T(8,128)(2,1)S(1)} copy-done((bf16[1,128,1536]{2,1,0:T(8,128)(2,1)S(1)}, bf16[1,128,1536]{2,1,0:T(8,128)(2,1)}, u32[]{:S(2)}) %copy-start.4) | copy-done | bytes 393240
  9.2 2.4 %glu.1 = bf16[128,768]{1,0:T(8,128)(2,1)S(1)} custom-call(s32[2]{0:T(128)S(1)} %pad_add_fusion.where_ref, bf16[128,1536]{1,0:T(8,128)(2,1)S(1)} %bitcast.13, f32[1,1536]{1,0:T(1,128)S(1)} %broadcast_in_dim.23.gain_ref, f32[1,1536]{1,0:T(1,128)S(1)} %broadcast_in_dim.24.bias_ref, bf16[2,768,1536]{2,1,0:T(8,128)(2,1)S(1)} %copy-done), custom_call_target="tpu_custom_call" | custom-call | flops 603979776 | bytes 5320712 | tf_op jit(solution)/shard_map/glu/pallas_call | solution.py:211
  12.3 5.3 %glu_conv_sums.1 = (bf16[128,768]{1,0:T(8,128)(2,1)S(1)}, f32[256,768]{1,0:T(8,128)S(1)}, f32[1,1664]{1,0:T(1,128)S(1)}) custom-call(s32[2]{0:T(128)S(1)} %pad_add_fusion.where_ref, bf16[128,1536]{1,0:T(8,128)(2,1)S(1)} %collective-permute-done.rows_ref, f32[1,1536]{1,0:T(1,128)S(1)} %broadcast_in_dim.23.gain_ref, f32[1,1536]{1,0:T(1,128)S(1)} %broadcast_in_dim.24.bias_ref, ...), custom_call_target="tpu_custom_call" | custom-call | flops 616562688 | bytes 6408712 | tf_op jit(solution)/shard_map/glu_conv_sums/pallas_call | solution.py:211
  17.6 0.9 %copy-done.2 = f32[256,768]{1,0:T(8,128)} copy-done((f32[256,768]{1,0:T(8,128)}, f32[256,768]{1,0:T(8,128)S(1)}, u32[]{:S(2)}) %copy-start.2) | copy-done | bytes 786456
  18.5 0.8 %broadcast_in_dim.26 = f32[32,1,1664]{2,1,0:T(1,128)} broadcast(f32[1664]{0:T(1024)S(1)} %reduce), dimensions={2} | broadcast | bytes 219648 | tf_op jit(solution)/shard_map/broadcast_in_dim | solution.py:272
  19.3 6.3 %all-to-all-start = ((f32[32,1,1664]{2,1,0:T(1,128)}), f32[32,1,1664]{2,1,0:T(1,128)S(1)}, u32[]{:S(2)}, u32[]{:S(2)}) async-start(f32[32,1,1664]{2,1,0:T(1,128)} %broadcast_in_dim.26), calls=%async_computation | async-start | bytes 425984 | tf_op jit(solution)/shard_map/all_to_all | solution.py:273
  25.6 1.7 %collective-permute-start.1 = (bf16[1,128,768]{2,1,0:T(8,128)(2,1)S(1)}, bf16[1,128,768]{2,1,0:T(8,128)(2,1)S(1)}, u32[]{:S(2)}, u32[]{:S(2)}) collective-permute-start(bf16[1,128,768]{2,1,0:T(8,128)(2,1)S(1)} %bitcast.16), channel_id=1, source_target_pairs={{1,0},{0,1},{3,2},{2,3},{5,4},{4,5},{7,6},{6,7},{9,8},{8,9},{11,10... | collective-permute-start | bytes 589832 | tf_op jit(solution)/shard_map/ppermute | solution.py:238
  27.8 1.7 %collective-permute-start.3 = (f32[34,768]{1,0:T(8,128)S(1)}, f32[34,768]{1,0:T(8,128)}, u32[]{:S(2)}, u32[]{:S(2)}) collective-permute-start(f32[34,768]{1,0:T(8,128)S(1)} %pad_maximum_fusion), channel_id=1, source_target_pairs={{1,0},{0,1},{3,2},{2,3},{5,4},{4,5},{7,6},{6,7},{9,8},{8,9},{11,10... | collective-permute-start | bytes 313352 | tf_op jit(solution)/shard_map/ppermute | solution.py:238
  29.4 4.3 %copy.10 = bf16[768,1536]{0,1:T(8,128)(2,1)} copy(bf16[768,1536]{1,0:T(8,128)(2,1)} %param.17) | data formatting | bytes 4718592 | tf_op args[8]
  33.7 2.8 %copy.11 = bf16[768,2,768]{2,0,1:T(8,128)(2,1)S(1)} copy(bf16[768,2,768]{0,2,1:T(8,128)(2,1)} %bitcast.18) | data formatting | bytes 4718592 | tf_op jit(solution)/shard_map/reshape | solution.py:246
  37.1 4.5 %collective-permute-done.3 = f32[34,768]{1,0:T(8,128)} collective-permute-done((f32[34,768]{1,0:T(8,128)S(1)}, f32[34,768]{1,0:T(8,128)}, u32[]{:S(2)}, u32[]{:S(2)}) %collective-permute-start.3) | collective-permute-done | bytes 104480 | tf_op jit(solution)/shard_map/ppermute | solution.py:238
  41.7 0.9 %slice.10.taps_ref = f32[32,768]{1,0:T(8,128)S(1)} slice(f32[34,768]{1,0:T(8,128)} %collective-permute-done.3), slice={[0:32], [0:768]} | slice | bytes 196608 | tf_op jit(solution)/shard_map/slice | solution.py:244
  42.6 1.3 %slice.11.refs_3_ = f32[2,768]{1,0:T(2,128)} slice(f32[34,768]{1,0:T(8,128)} %collective-permute-done.3), slice={[32:34], [0:768]} | slice | bytes 12288 | tf_op jit(solution)/shard_map/slice | solution.py:245
  44.6 0.9 %copy-done.7 = bf16[128,768]{1,0:T(8,128)(2,1)S(1)} copy-done((bf16[128,768]{1,0:T(8,128)(2,1)S(1)}, bf16[128,768]{1,0:T(8,128)(2,1)}, u32[]{:S(2)}) %copy-start.7) | copy-done | bytes 196632
  45.5 0.7 %copy-done.13 = s32[2]{0:T(128)S(1)} copy-done((s32[2]{0:T(128)S(1)}, s32[2]{0:T(128)}, u32[]{:S(2)}) %copy-start.13) | copy-done | bytes 32
  46.2 3.7 %conv_of_peer.1.refs_1_ = f32[256,768]{1,0:T(8,128)S(1)} custom-call(s32[2]{0:T(128)S(1)} %copy-done.13, bf16[1,128,768]{2,1,0:T(8,128)(2,1)S(1)} %collective-permute-done.1.early_ref, bf16[128,768]{1,0:T(8,128)(2,1)S(1)} %copy-done.7, f32[32,768]{1,0:T(8,128)S(1)} %slice.10.taps_ref), custom_call_target="tpu_custom_call" | custom-call | flops 12582912 | bytes 1277960 | tf_op jit(solution)/shard_map/conv_of_peer/pallas_call | solution.py:211
  50.0 1.1 %copy-done.3 = f32[256,768]{1,0:T(8,128)S(1)} copy-done((f32[256,768]{1,0:T(8,128)S(1)}, f32[256,768]{1,0:T(8,128)}, u32[]{:S(2)}) %copy-start.3) | copy-done | bytes 786456
  51.1 0.7 %copy-done.8 = f32[2,768]{1,0:T(2,128)S(1)} copy-done((f32[2,768]{1,0:T(2,128)S(1)}, f32[2,768]{1,0:T(2,128)}, u32[]{:S(2)}) %copy-start.8) | copy-done | bytes 6168
  51.8 0.7 %copy-done.10 = f32[2,768]{1,0:T(2,128)S(1)} copy-done((f32[2,768]{1,0:T(2,128)S(1)}, f32[2,768]{1,0:T(2,128)}, u32[]{:S(2)}) %copy-start.10) | copy-done | bytes 6168
  52.5 0.7 %copy-done.14 = s32[2]{0:T(128)S(1)} copy-done((s32[2]{0:T(128)S(1)}, s32[2]{0:T(128)}, u32[]{:S(2)}) %copy-start.14) | copy-done | bytes 32
  53.2 1.6 %branch_sent.1 = bf16[1,128,768]{2,1,0:T(8,128)(2,1)S(1)} custom-call(s32[2]{0:T(128)S(1)} %copy-done.14, f32[16,2,1,1664]{3,2,1,0:T(1,128)S(1)} %bitcast.10, bf16[2,768,768]{2,1,0:T(8,128)(2,1)S(1)} %bitcast.8, f32[256,768]{1,0:T(8,128)S(1)} %copy-done.3, f32[256,768]{1,0:T(8,128)S(1)} %conv_of_peer.1.refs_1_, f32[2,768]{1,0:T(2,128)S(1)} %copy-done.8, ...), custom_call_target="tpu_custom_call" | custom-call | flops 301989888 | bytes 4354056 | tf_op jit(solution)/shard_map/branch_sent/pallas_call | solution.py:211
  54.8 1.4 %collective-permute-start.4 = (bf16[128,768]{1,0:T(8,128)(2,1)S(1)}, bf16[128,768]{1,0:T(8,128)(2,1)S(1)}, u32[]{:S(2)}, u32[]{:S(2)}) collective-permute-start(bf16[128,768]{1,0:T(8,128)(2,1)S(1)} %bitcast.17), channel_id=1, source_target_pairs={{1,0},{0,1},{3,2},{2,3},{5,4},{4,5},{7,6},{6,7},{9,8},{8,9},{11,10... | collective-permute-start | bytes 589832 | tf_op jit(solution)/shard_map/ppermute | solution.py:238
  56.2 0.7 %copy-done.9 = f32[2,768]{1,0:T(2,128)S(1)} copy-done((f32[2,768]{1,0:T(2,128)S(1)}, f32[2,768]{1,0:T(2,128)}, u32[]{:S(2)}) %copy-start.9) | copy-done | bytes 6168
  56.9 0.7 %copy-done.11 = f32[2,768]{1,0:T(2,128)S(1)} copy-done((f32[2,768]{1,0:T(2,128)S(1)}, f32[2,768]{1,0:T(2,128)}, u32[]{:S(2)}) %copy-start.11) | copy-done | bytes 6168
  57.6 1.6 %branch_kept.1.kept_ref = f32[128,768]{1,0:T(8,128)S(1)} custom-call(s32[2]{0:T(128)S(1)} %copy-done.14, f32[16,2,1,1664]{3,2,1,0:T(1,128)S(1)} %bitcast.11, bf16[2,768,768]{2,1,0:T(8,128)(2,1)S(1)} %bitcast.9, f32[256,768]{1,0:T(8,128)S(1)} %copy-done.3, f32[256,768]{1,0:T(8,128)S(1)} %conv_of_peer.1.refs_1_, f32[2,768]{1,0:T(2,128)S(1)} %copy-done.9, ...), custom_call_target="tpu_custom_call" | custom-call | flops 301989888 | bytes 4550664 | tf_op jit(solution)/shard_map/branch_kept/pallas_call | solution.py:211
  59.2 2.0 %collective-permute-done.4.refs_0_ = bf16[128,768]{1,0:T(8,128)(2,1)S(1)} collective-permute-done((bf16[128,768]{1,0:T(8,128)(2,1)S(1)}, bf16[128,768]{1,0:T(8,128)(2,1)S(1)}, u32[]{:S(2)}, u32[]{:S(2)}) %collective-permute-start.4) | collective-permute-done | bytes 196640 | tf_op jit(solution)/shard_map/ppermute | solution.py:238
  61.2 1.4 %residual.1 = bf16[128,1536]{1,0:T(8,128)(2,1)} custom-call(s32[2]{0:T(128)S(1)} %copy-done.14, bf16[128,1536]{1,0:T(8,128)(2,1)S(1)} %bitcast.14, f32[128,768]{1,0:T(8,128)S(1)} %branch_kept.1.kept_ref, bf16[128,768]{1,0:T(8,128)(2,1)S(1)} %collective-permute-done.4.refs_0_), custom_call_target="tpu_custom_call" | custom-call | bytes 1376264 | tf_op jit(solution)/shard_map/residual/pallas_call | solution.py:211
  (34 shorter events, 2.6 us)
Async XLA Ops:
  0.0 12.3 %collective-permute-start = (bf16[128,1536]{1,0:T(8,128)(2,1)}, bf16[128,1536]{1,0:T(8,128)(2,1)S(1)}, u32[]{:S(2)}, u32[]{:S(2)}) collective-permute-start(bf16[128,1536]{1,0:T(8,128)(2,1)} %bitcast.12), channel_id=1, source_target_pairs={{1,0},{0,1},{3,2},{2,3},{5,4},{4,5},{7,6},{6,7},{9,8},{8,9},{11,10... | collective-permute-start | bytes 1179656 | tf_op jit(solution)/shard_map/ppermute | solution.py:238
  5.9 2.3 %copy-start = (bf16[2,768,1536]{2,1,0:T(8,128)(2,1)S(1)}, bf16[2,768,1536]{2,1,0:T(8,128)(2,1)}, u32[]{:S(2)}) copy-start(bf16[2,768,1536]{2,1,0:T(8,128)(2,1)} %weight_ref.3) | copy-start | bytes 14155780
  8.2 1.0 %copy-start.4 = (bf16[1,128,1536]{2,1,0:T(8,128)(2,1)S(1)}, bf16[1,128,1536]{2,1,0:T(8,128)(2,1)}, u32[]{:S(2)}) copy-start(bf16[1,128,1536]{2,1,0:T(8,128)(2,1)} %param.9) | copy-start | bytes 1179652
  9.2 3.1 %copy-start.12 = (s32[2]{0:T(128)}, s32[2]{0:T(128)S(1)}, u32[]{:S(2)}) copy-start(s32[2]{0:T(128)S(1)} %pad_add_fusion.where_ref) | copy-start | bytes 28
  9.2 3.1 %copy-start.1 = (bf16[2,768,1536]{2,1,0:T(8,128)(2,1)S(1)}, bf16[2,768,1536]{2,1,0:T(8,128)(2,1)}, u32[]{:S(2)}) copy-start(bf16[2,768,1536]{2,1,0:T(8,128)(2,1)} %weight_ref.3) | copy-start | bytes 14155780
  12.3 14.9 %copy-start.15 = (f32[768]{0:T(1024)S(1)}, f32[768]{0:T(1024)}, u32[]{:S(2)}) copy-start(f32[768]{0:T(1024)} %param.16) | copy-start | bytes 9220
  12.3 14.9 %copy-start.16 = (f32[768]{0:T(1024)S(1)}, f32[768]{0:T(1024)}, u32[]{:S(2)}) copy-start(f32[768]{0:T(1024)} %param.15) | copy-start | bytes 9220
  17.6 0.9 %copy-start.2 = (f32[256,768]{1,0:T(8,128)}, f32[256,768]{1,0:T(8,128)S(1)}, u32[]{:S(2)}) copy-start(f32[256,768]{1,0:T(8,128)S(1)} %get-tuple-element.9.refs_0_) | copy-start | bytes 2359300
  19.3 30.7 %all-to-all-start = ((f32[32,1,1664]{2,1,0:T(1,128)}), f32[32,1,1664]{2,1,0:T(1,128)S(1)}, u32[]{:S(2)}, u32[]{:S(2)}) async-start(f32[32,1,1664]{2,1,0:T(1,128)} %broadcast_in_dim.26), calls=%async_computation | async-start | bytes 425984 | tf_op jit(solution)/shard_map/all_to_all | solution.py:273
  25.6 18.4 %collective-permute-start.1 = (bf16[1,128,768]{2,1,0:T(8,128)(2,1)S(1)}, bf16[1,128,768]{2,1,0:T(8,128)(2,1)S(1)}, u32[]{:S(2)}, u32[]{:S(2)}) collective-permute-start(bf16[1,128,768]{2,1,0:T(8,128)(2,1)S(1)} %bitcast.16), channel_id=1, source_target_pairs={{1,0},{0,1},{3,2},{2,3},{5,4},{4,5},{7,6},{6,7},{9,8},{8,9},{11,10... | collective-permute-start | bytes 589832 | tf_op jit(solution)/shard_map/ppermute | solution.py:238
  27.3 16.7 %collective-permute-start.2 = (bf16[128,768]{1,0:T(8,128)(2,1)S(1)}, bf16[128,768]{1,0:T(8,128)(2,1)S(1)}, u32[]{:S(2)}, u32[]{:S(2)}) collective-permute-start(bf16[128,768]{1,0:T(8,128)(2,1)S(1)} %get-tuple-element.10), channel_id=1, source_target_pairs={{1,0},{0,1},{3,2},{2,3},{5,4},{4,5},{7,6},{6,7},{9,8},{8,9},{11,10... | collective-permute-start | bytes 589832 | tf_op jit(solution)/shard_map/ppermute | solution.py:238
  27.8 13.9 %collective-permute-start.3 = (f32[34,768]{1,0:T(8,128)S(1)}, f32[34,768]{1,0:T(8,128)}, u32[]{:S(2)}, u32[]{:S(2)}) collective-permute-start(f32[34,768]{1,0:T(8,128)S(1)} %pad_maximum_fusion), channel_id=1, source_target_pairs={{1,0},{0,1},{3,2},{2,3},{5,4},{4,5},{7,6},{6,7},{9,8},{8,9},{11,10... | collective-permute-start | bytes 313352 | tf_op jit(solution)/shard_map/ppermute | solution.py:238
  43.9 0.7 %copy-start.6 = (bf16[128,768]{1,0:T(8,128)(2,1)}, bf16[128,768]{1,0:T(8,128)(2,1)S(1)}, u32[]{:S(2)}) copy-start(bf16[128,768]{1,0:T(8,128)(2,1)S(1)} %collective-permute-done.2.late_ref) | copy-start | bytes 589828
  44.6 0.9 %copy-start.7 = (bf16[128,768]{1,0:T(8,128)(2,1)S(1)}, bf16[128,768]{1,0:T(8,128)(2,1)}, u32[]{:S(2)}) copy-start(bf16[128,768]{1,0:T(8,128)(2,1)} %copy-done.6) | copy-start | bytes 589828
  45.5 0.7 %copy-start.13 = (s32[2]{0:T(128)S(1)}, s32[2]{0:T(128)}, u32[]{:S(2)}) copy-start(s32[2]{0:T(128)} %copy-done.12) | copy-start | bytes 28
  50.0 1.1 %copy-start.3 = (f32[256,768]{1,0:T(8,128)S(1)}, f32[256,768]{1,0:T(8,128)}, u32[]{:S(2)}) copy-start(f32[256,768]{1,0:T(8,128)} %copy-done.2) | copy-start | bytes 2359300
  51.1 0.7 %copy-start.8 = (f32[2,768]{1,0:T(2,128)S(1)}, f32[2,768]{1,0:T(2,128)}, u32[]{:S(2)}) copy-start(f32[2,768]{1,0:T(2,128)} %pad_maximum_fusion.1.refs_2_) | copy-start | bytes 18436
  51.8 0.7 %copy-start.10 = (f32[2,768]{1,0:T(2,128)S(1)}, f32[2,768]{1,0:T(2,128)}, u32[]{:S(2)}) copy-start(f32[2,768]{1,0:T(2,128)} %slice.11.refs_3_) | copy-start | bytes 18436
  52.5 0.7 %copy-start.14 = (s32[2]{0:T(128)S(1)}, s32[2]{0:T(128)}, u32[]{:S(2)}) copy-start(s32[2]{0:T(128)} %copy-done.12) | copy-start | bytes 28
  54.8 6.4 %copy-start.5 = (bf16[1,128,1536]{2,1,0:T(8,128)(2,1)S(1)}, bf16[1,128,1536]{2,1,0:T(8,128)(2,1)}, u32[]{:S(2)}) copy-start(bf16[1,128,1536]{2,1,0:T(8,128)(2,1)} %param.9) | copy-start | bytes 1179652
  54.8 6.3 %collective-permute-start.4 = (bf16[128,768]{1,0:T(8,128)(2,1)S(1)}, bf16[128,768]{1,0:T(8,128)(2,1)S(1)}, u32[]{:S(2)}, u32[]{:S(2)}) collective-permute-start(bf16[128,768]{1,0:T(8,128)(2,1)S(1)} %bitcast.17), channel_id=1, source_target_pairs={{1,0},{0,1},{3,2},{2,3},{5,4},{4,5},{7,6},{6,7},{9,8},{8,9},{11,10... | collective-permute-start | bytes 589832 | tf_op jit(solution)/shard_map/ppermute | solution.py:238
  56.2 0.7 %copy-start.9 = (f32[2,768]{1,0:T(2,128)S(1)}, f32[2,768]{1,0:T(2,128)}, u32[]{:S(2)}) copy-start(f32[2,768]{1,0:T(2,128)} %pad_maximum_fusion.1.refs_2_) | copy-start | bytes 18436
  56.9 0.7 %copy-start.11 = (f32[2,768]{1,0:T(2,128)S(1)}, f32[2,768]{1,0:T(2,128)}, u32[]{:S(2)}) copy-start(f32[2,768]{1,0:T(2,128)} %slice.11.refs_3_) | copy-start | bytes 18436

commit v2 on v0

v2 whole, which is shorter than its diff:
```python
import functools

import jax
import jax.numpy as jnp
from jax import lax
from jax.experimental import pallas as pl
from jax.experimental.pallas import tpu as pltpu
from jax.sharding import PartitionSpec as P

KERNEL = 32
LANES = 128
HALO = 16
REACH = 32
EXTRA = 48
F32 = jnp.float32
BF16 = jnp.bfloat16

VMEM = pl.BlockSpec(memory_space=pltpu.VMEM)
SMEM = pl.BlockSpec(memory_space=pltpu.SMEM)
HBM = pl.BlockSpec(memory_space=pl.ANY)


def contract_last(left, right):
    return lax.dot_general(
        left, right, (((1,), (1,)), ((), ())), preferred_element_type=F32
    )


def layer_norm(rows, gain, bias):
    values = rows.astype(F32)
    center = jnp.mean(values, axis=-1, keepdims=True)
    values = values - center
    spread = jnp.mean(values * values, axis=-1, keepdims=True)
    return (values * lax.rsqrt(spread + 1e-05) * gain + bias).astype(BF16)


def swish(z):
    return z * jax.nn.sigmoid(z)


def cuts(width, most):
    step = most if width % most == 0 else LANES
    return [slice(at, at + step) for at in range(0, width, step)]


def valid_rows(first, rows, length):
    index = first + lax.broadcasted_iota(jnp.int32, (rows, 1), 0)
    return index < length


def glu_of(normed, weight_ref, cut, keep):
    value = contract_last(normed, weight_ref[0, cut, :])
    gate = contract_last(normed, weight_ref[1, cut, :])
    glu = (value * jax.nn.sigmoid(gate)).astype(BF16)
    return jnp.where(keep, glu.astype(F32), 0.0)


def three_parts(vector):
    parts = []
    for _ in range(3):
        part = vector.astype(BF16).astype(F32)
        parts.append(part)
        vector = vector - part
    return parts


def clear_ends(edge_ref):
    tiles, total, _ = edge_ref.shape
    zeros = jnp.zeros((REACH, LANES), F32)
    for tile in range(tiles):
        edge_ref[tile, 0:REACH, :] = zeros
        edge_ref[tile, total - REACH : total, :] = zeros


def add_block_conv(block, tile, edge_ref, taps_ref, sums_ref, first, fresh):
    rows = block.shape[0]
    edge_ref[tile, REACH : REACH + rows, :] = block
    count = (rows + 2 * HALO) // 8
    cut = slice(tile * LANES, (tile + 1) * LANES)
    total = [None] * count
    if not fresh:
        total = [sums_ref[tile, pl.ds(first + at, 8, stride=count), :] for at in range(count)]
    for seen in range(1, count + KERNEL):
        values = edge_ref[tile, pl.ds(seen, 8, stride=count), :]
        for at in range(count):
            tap = seen - at - 1
            if 0 <= tap < KERNEL:
                term = values * taps_ref[tap : tap + 1, cut]
                total[at] = term if total[at] is None else total[at] + term
    for at in range(count):
        sums_ref[tile, pl.ds(first + at, 8, stride=count), :] = total[at]


def first_block_kernel(
    parts, lengths_ref, frames_ref, vectors_ref, taps_ref, weight_ref,
    pack_ref, sums_ref, held_ref,
    rows_ref, wide_taps_ref, edge_ref, rows_sem, weight_sems,
):
    rows, width = rows_ref.shape
    chans = held_ref.shape[1]
    own = lax.axis_index("tensor")
    rows_copy = pltpu.make_async_copy(frames_ref.at[0], rows_ref, rows_sem)
    rows_copy.start()
    pieces = cuts(chans, 256)
    copies = []
    for at, cut in enumerate(pieces):
        for side in range(2):
            place = (side, pl.ds(cut.start, cut.stop - cut.start))
            copy = pltpu.make_async_copy(
                weight_ref.at[place], held_ref.at[place], weight_sems.at[at, side]
            )
            copy.start()
            copies.append(copy)
    clear_ends(edge_ref)
    taps = taps_ref[...]
    wide_taps_ref[...] = taps.astype(F32)
    gain, bias = vectors_ref[:, :width], vectors_ref[:, width : 2 * width]
    norms = [vectors_ref[:, 2 * width + at * chans : 2 * width + (at + 1) * chans] for at in range(2)]
    extra = three_parts(norms[0]) + three_parts(norms[1])
    extra.append(jnp.zeros((EXTRA - KERNEL - len(extra), chans), F32))
    pack_ref[rows : rows + KERNEL, :] = taps
    pack_ref[rows + KERNEL :, :] = jnp.concatenate(extra).astype(BF16)
    keep = valid_rows(own * rows, rows, lengths_ref[0])
    rows_copy.wait()
    normed = layer_norm(rows_ref[...], gain, bias)
    for at, cut in enumerate(pieces):
        copies[2 * at].wait()
        copies[2 * at + 1].wait()
        glu = glu_of(normed, held_ref, cut, keep)
        pack_ref[0:rows, cut] = glu.astype(BF16)
        for tile in range(cut.start // LANES, cut.stop // LANES):
            seen = slice(tile * LANES - cut.start, (tile + 1) * LANES - cut.start)
            add_block_conv(glu[:, seen], tile, edge_ref, wide_taps_ref, sums_ref, 0, True)


def middle_block_kernel(shift, parts, lengths_ref, rows_ref, vectors_ref, weight_ref, glu_ref):
    rows, chans = glu_ref.shape
    width = rows_ref.shape[1]
    first = lax.rem(lax.axis_index("tensor") + shift, parts) * rows
    keep = valid_rows(first, rows, lengths_ref[0])
    gain, bias = vectors_ref[:, :width], vectors_ref[:, width : 2 * width]
    normed = layer_norm(rows_ref[...], gain, bias)
    for cut in cuts(chans, 256):
        glu_ref[:, cut] = glu_of(normed, weight_ref, cut, keep).astype(BF16)


def last_block_kernel(
    parts, lengths_ref, rows_ref, vectors_ref, taps_ref, weight_ref, first_sums_ref, *refs
):
    middle_refs = refs[: parts - 2]
    glu_ref, conv_ref, spread_ref, wide_taps_ref, edge_ref, sums_ref, stats_ref, conv_sem = refs[parts - 2 :]
    rows, chans = glu_ref.shape
    width = rows_ref.shape[1]
    tiles = chans // LANES
    total_rows = parts * rows
    own = lax.axis_index("tensor")
    slot = lax.rem(own + parts - 1, parts)
    length = lengths_ref[0]
    count = length.astype(F32)
    keep = valid_rows(slot * rows, rows, length)
    valid = valid_rows(0, total_rows, length).astype(F32)
    clear_ends(edge_ref)
    wide_taps_ref[...] = taps_ref[...].astype(F32)
    reach = rows + 2 * HALO
    zeros = jnp.zeros((total_rows + 2 * HALO, LANES), F32)
    for tile in range(tiles):
        sums_ref[tile] = zeros
        sums_ref[tile, pl.ds(pl.multiple_of(own * rows, rows), reach), :] = first_sums_ref[tile]
    gain, bias = vectors_ref[:, :width], vectors_ref[:, width : 2 * width]
    normed = layer_norm(rows_ref[...], gain, bias)
    copies = []
    for cut in cuts(chans, 256):
        glu = glu_of(normed, weight_ref, cut, keep)
        glu_ref[:, cut] = glu.astype(BF16)
        for tile in range(cut.start // LANES, cut.stop // LANES):
            seen = slice(tile * LANES - cut.start, (tile + 1) * LANES - cut.start)
            lanes = slice(tile * LANES, (tile + 1) * LANES)
            for at, middle in enumerate(middle_refs):
                first = pl.multiple_of(lax.rem(own + at + 1, parts) * rows, rows)
                block = middle[:, lanes].astype(F32)
                add_block_conv(block, tile, edge_ref, wide_taps_ref, sums_ref, first, False)
            first = pl.multiple_of(slot * rows, rows)
            add_block_conv(glu[:, seen], tile, edge_ref, wide_taps_ref, sums_ref, first, False)
            copy = pltpu.make_async_copy(
                sums_ref.at[tile, pl.ds(HALO, total_rows)], conv_ref.at[tile], conv_sem.at[tile]
            )
            copy.start()
            copies.append(copy)
            conv = sums_ref[tile, HALO : HALO + total_rows, :]
            sums = jnp.sum(conv * valid, axis=0, keepdims=True)
            off = (conv - sums / count) * valid
            stats_ref[:, lanes] = sums
            stats_ref[:, chans + lanes.start : chans + lanes.stop] = jnp.sum(
                off * off, axis=0, keepdims=True
            )
    stats_ref[:, 2 * chans :] = jnp.full((1, LANES), count, F32)
    stats = stats_ref[...]
    for at in range(spread_ref.shape[0]):
        spread_ref[at] = stats
    for copy in copies:
        copy.wait()


def peer_conv_kernel(parts, vectors_ref, conv_ref, weight_ref, *refs):
    packs, middles, lates = refs[: parts - 1], refs[parts - 1 : (parts - 1) ** 2], refs[(parts - 1) ** 2 :]
    lates, (convs_ref, norms_ref, held_ref) = lates[: parts - 1], lates[parts - 1 : parts + 2]
    wide_taps_ref, edge_ref, sums_ref, conv_sem, weight_sem = refs[-5:]
    rows, chans = lates[0].shape
    tiles = chans // LANES
    total_rows = parts * rows
    conv_copy = pltpu.make_async_copy(conv_ref, convs_ref.at[0], conv_sem)
    conv_copy.start()
    weight_copy = pltpu.make_async_copy(weight_ref, held_ref, weight_sem)
    weight_copy.start()
    own = lax.axis_index("tensor")
    clear_ends(edge_ref)
    skip = vectors_ref.shape[1] - 2 * chans
    norms_ref[0, 0:1, :] = vectors_ref[:, skip : skip + chans]
    norms_ref[0, 1:2, :] = vectors_ref[:, skip + chans :]
    zeros = jnp.zeros((total_rows + 2 * HALO, LANES), F32)
    for shift in range(1, parts):
        peer = lax.rem(own + shift, parts)
        pack = packs[shift - 1]
        wide_taps_ref[...] = pack[rows : rows + KERNEL, :].astype(F32)
        extra = pack[rows + KERNEL :, :].astype(F32)
        norms_ref[shift, 0:1, :] = extra[0:1] + (extra[1:2] + extra[2:3])
        norms_ref[shift, 1:2, :] = extra[3:4] + (extra[4:5] + extra[5:6])
        mine = middles[(shift - 1) * (parts - 2) : shift * (parts - 2)]
        blocks = [pack] + list(mine) + [lates[shift - 1]]
        for tile in range(tiles):
            lanes = slice(tile * LANES, (tile + 1) * LANES)
            sums_ref[tile] = zeros
            for step, block in enumerate(blocks):
                first = pl.multiple_of(lax.rem(peer + step, parts) * rows, rows)
                values = block[0:rows, lanes].astype(F32)
                add_block_conv(values, tile, edge_ref, wide_taps_ref, sums_ref, first, False)
            convs_ref[shift, tile] = sums_ref[tile, HALO : HALO + total_rows, :]
    conv_copy.wait()
    weight_copy.wait()


def branch_rows(parts, slot, rows, stats_ref, convs_ref, norms_ref, weight_ref):
    chans = norms_ref.shape[2]
    own = lax.axis_index("tensor")
    first = pl.multiple_of(slot * rows, rows)
    total = None
    for shift in range(parts):
        place = lax.rem(own + shift, parts)
        seen = stats_ref[:, pl.ds(place, 1), :, :]
        counts = seen[..., 2 * chans : 2 * chans + 1]
        sums = seen[..., :chans]
        count = jnp.sum(counts, axis=0)[0]
        mean = jnp.sum(sums, axis=0)[0] / count
        off = sums / counts - mean
        var = jnp.sum(seen[..., chans : 2 * chans] + counts * off * off, axis=0)[0] / count
        scale = lax.rsqrt(var + 1e-05) * norms_ref[shift, 0:1, :]
        bias = norms_ref[shift, 1:2, :]
        acts = []
        for tile in range(chans // LANES):
            lanes = slice(tile * LANES, (tile + 1) * LANES)
            conv = convs_ref[shift, tile, pl.ds(first, rows), :]
            z = (conv - mean[:, lanes]) * scale[:, lanes] + bias[:, lanes]
            acts.append(swish(z).astype(BF16))
        if weight_ref.ndim == 3:
            weight = weight_ref[place]
        else:
            weight = weight_ref[:, pl.ds(pl.multiple_of(place * chans, LANES), chans)]
        term = contract_last(jnp.concatenate(acts, axis=1), weight)
        total = term if total is None else total + term
    return total


def sent_kernel(parts, stats_ref, convs_ref, norms_ref, weight_ref, out_ref):
    own = lax.axis_index("tensor")
    rows = out_ref.shape[1]
    for shift in range(1, parts):
        slot = lax.rem(own + shift, parts)
        branch = branch_rows(parts, slot, rows, stats_ref, convs_ref, norms_ref, weight_ref)
        out_ref[shift - 1] = branch.astype(BF16)


def columns(ref, place, cols):
    if len(ref.shape) == 3:
        return ref.at[place]
    return ref.at[:, pl.ds(pl.multiple_of(place * cols, LANES), cols)]


def kept_kernel(
    parts, stats_ref, convs_ref, norms_ref, weight_ref, frames_ref,
    out_ref, base_ref, mine_ref, frames_sems, out_sem,
):
    own = lax.axis_index("tensor")
    rows, cols = mine_ref.shape
    copies = []
    for shift in range(parts):
        target = mine_ref if shift == 0 else base_ref.at[shift - 1]
        source = columns(frames_ref, lax.rem(own + shift, parts), cols)
        copy = pltpu.make_async_copy(source, target, frames_sems.at[shift])
        copy.start()
        copies.append(copy)
    branch = branch_rows(parts, own, rows, stats_ref, convs_ref, norms_ref, weight_ref)
    for copy in copies:
        copy.wait()
    mine_ref[...] = (mine_ref[...].astype(F32) + branch).astype(BF16)
    out_copy = pltpu.make_async_copy(mine_ref, columns(out_ref, own, cols), out_sem)
    out_copy.start()
    out_copy.wait()


def finish_kernel(parts, filled_ref, base_ref, *refs):
    got_refs, (out_ref, done_ref, out_sems) = refs[: parts - 1], refs[parts - 1 :]
    own = lax.axis_index("tensor")
    cols = base_ref.shape[2]
    copies = []
    for shift in range(1, parts):
        branch = got_refs[shift - 1][...].astype(F32)
        done_ref[shift - 1] = (base_ref[shift - 1].astype(F32) + branch).astype(BF16)
        target = columns(out_ref, lax.rem(own + shift, parts), cols)
        copy = pltpu.make_async_copy(done_ref.at[shift - 1], target, out_sems.at[shift - 1])
        copy.start()
        copies.append(copy)
    for copy in copies:
        copy.wait()


def shape(dims, kind):
    return jax.ShapeDtypeStruct(dims, kind)


def call(kernel, outs, in_specs, operands, out_specs=None, scratch=(), flops=0, name=None, aliases=None):
    moved = sum(x.size * x.dtype.itemsize for x in list(operands) + list(outs))
    return pl.pallas_call(
        kernel,
        out_shape=tuple(outs),
        in_specs=list(in_specs),
        out_specs=tuple(out_specs or [VMEM] * len(outs)),
        scratch_shapes=list(scratch),
        input_output_aliases=aliases or {},
        compiler_params=pltpu.CompilerParams(vmem_limit_bytes=24 * 1024 * 1024),
        cost_estimate=pl.CostEstimate(flops=flops, bytes_accessed=moved, transcendentals=0),
        name=name,
    )(*operands)


def per_device(
    parts, devices, frames_in, lengths, ln_gain, ln_bias, glu_weight, conv_kernel, bn_gain, bn_bias,
    out_weight,
):
    _, span, width = frames_in.shape
    given = glu_weight.shape[1]
    cols = out_weight.shape[0]
    spare = -given % LANES
    if spare:
        glu_weight = jnp.pad(glu_weight, ((0, 0), (0, spare), (0, 0)))
        conv_kernel = jnp.pad(conv_kernel, ((0, 0), (0, spare)))
        bn_gain, bn_bias = jnp.pad(bn_gain, (0, spare)), jnp.pad(bn_bias, (0, spare))
        out_weight = out_weight.reshape(cols, parts, given).transpose(1, 0, 2)
        out_weight = jnp.pad(out_weight, ((0, 0), (0, 0), (0, spare)))
    chans = given + spare
    tiles = chans // LANES
    total_rows = span * parts

    def from_peer(value, shift):
        pairs = [((at + shift) % parts, at) for at in range(parts)]
        return lax.ppermute(value, "tensor", pairs)

    vectors = jnp.concatenate([ln_gain, ln_bias, bn_gain, bn_bias])[None]
    frames = [from_peer(frames_in[0], shift) for shift in range(1, parts)]

    glu_flops = 4 * span * width * chans
    wide_taps = pltpu.VMEM((KERNEL, chans), F32)
    edge = pltpu.VMEM((tiles, span + 2 * REACH, LANES), F32)
    sums = pltpu.VMEM((tiles, total_rows + 2 * HALO, LANES), F32)
    pack, first_sums, held = call(
        functools.partial(first_block_kernel, parts),
        (
            shape((span + EXTRA, chans), BF16),
            shape((tiles, span + 2 * HALO, LANES), F32),
            shape((2, chans, width), BF16),
        ),
        [SMEM, HBM, VMEM, VMEM, HBM],
        (lengths, frames_in, vectors, conv_kernel, glu_weight),
        scratch=(
            pltpu.VMEM((span, width), BF16),
            wide_taps,
            edge,
            pltpu.SemaphoreType.DMA,
            pltpu.SemaphoreType.DMA((len(cuts(chans, 256)), 2)),
        ),
        flops=glu_flops,
        name="first_block",
    )
    middle = [
        call(
            functools.partial(middle_block_kernel, shift, parts),
            (shape((span, chans), BF16),),
            [SMEM, VMEM, VMEM, VMEM],
            (lengths, frames[shift - 1], vectors, held),
            flops=glu_flops,
            name="middle_block",
        )[0]
        for shift in range(1, parts - 1)
    ]
    late, conv, spread = call(
        functools.partial(last_block_kernel, parts),
        (
            shape((span, chans), BF16),
            shape((tiles, total_rows, LANES), F32),
            shape((devices, 1, 2 * chans + LANES), F32),
        ),
        [SMEM] + [VMEM] * (5 + len(middle)),
        (lengths, frames[-1], vectors, conv_kernel, held, first_sums, *middle),
        out_specs=(VMEM, HBM, VMEM),
        scratch=(
            wide_taps,
            edge,
            sums,
            pltpu.VMEM((1, 2 * chans + LANES), F32),
            pltpu.SemaphoreType.DMA((tiles,)),
        ),
        flops=glu_flops,
        name="last_block",
    )
    stats = lax.all_to_all(spread, ("dp", "tensor"), split_axis=0, concat_axis=0, tiled=True)
    stats = stats.reshape((devices // parts, parts) + spread.shape[1:])

    shifts = range(1, parts)
    packs = [from_peer(pack, shift) for shift in shifts]
    middles = [from_peer(each, shift) for shift in shifts for each in middle]
    lates = [from_peer(late, shift) for shift in shifts]
    convs, norms, weight = call(
        functools.partial(peer_conv_kernel, parts),
        (
            shape((parts, tiles, total_rows, LANES), F32),
            shape((parts, 2, chans), F32),
            shape(out_weight.shape, BF16),
        ),
        [VMEM, HBM, HBM] + [VMEM] * (len(packs) + len(middles) + len(lates)),
        (vectors, conv, out_weight, *packs, *middles, *lates),
        scratch=(wide_taps, edge, sums, pltpu.SemaphoreType.DMA, pltpu.SemaphoreType.DMA),
        flops=2 * KERNEL * total_rows * chans,
        name="peer_conv",
    )
    operands = (stats, convs, norms, weight)
    branch_flops = 2 * span * width * cols
    (sent,) = call(
        functools.partial(sent_kernel, parts),
        (shape((parts - 1, span, cols), BF16),),
        [VMEM] * 4,
        operands,
        flops=branch_flops * (parts - 1),
        name="branch_sent",
    )
    got = [from_peer(sent[parts - shift - 1], shift) for shift in shifts]
    whole = cols % LANES == 0
    rows = frames_in[0]
    if not whole:
        rows = rows.reshape(span, parts, cols).transpose(1, 0, 2)
    filled, base = call(
        functools.partial(kept_kernel, parts),
        (shape(rows.shape, BF16), shape((parts - 1, span, cols), BF16)),
        [VMEM] * 4 + [HBM],
        (*operands, rows),
        out_specs=(HBM, VMEM),
        scratch=(
            pltpu.VMEM((span, cols), BF16),
            pltpu.SemaphoreType.DMA((parts,)),
            pltpu.SemaphoreType.DMA,
        ),
        flops=branch_flops,
        name="branch_kept",
    )
    (out,) = call(
        functools.partial(finish_kernel, parts),
        (shape(rows.shape, BF16),),
        [HBM] + [VMEM] * parts,
        (filled, base, *got),
        out_specs=(HBM,),
        scratch=(
            pltpu.VMEM((parts - 1, span, cols), BF16),
            pltpu.SemaphoreType.DMA((parts - 1,)),
        ),
        aliases={0: 0},
        name="residual",
    )
    if not whole:
        out = out.transpose(1, 0, 2).reshape(span, width)
    return out[None]


def solution(mesh):
    sizes = dict(mesh.shape)
    body = functools.partial(per_device, sizes["tensor"], sizes["tensor"] * sizes["dp"])
    return jax.shard_map(
        body,
        mesh=mesh,
        in_specs=(
            P("dp", "tensor", None),
            P("dp"),
            P(),
            P(),
            P(None, "tensor", None),
            P(None, "tensor"),
            P("tensor"),
            P("tensor"),
            P("tensor", None),
        ),
        out_specs=P("dp", "tensor", None),
        check_vma=False,
    )
```

time: 120 us -> 56.4 us (0.47)
  blocking collectives: 100 us -> 0 us
  waiting for transfers between devices: 0 us -> 16.4 us
  Pallas kernels: 0 us -> 15.3 us
  starting transfers between devices: 0 us -> 12.3 us
  other arithmetic: 11.8 us -> 0.76 us
  local copies, waits for them, and re-layouts: 2.41 us -> 10.4 us
  matrix products: 4.56 us -> 0 us
    psum x2 -> x0, blocking collectives: 63.3 us -> none  [the longest x1 33.8 us: batch_stats(): sums, count = lax.psum((local_sums, own_count), 'dp')]
    all_gather x2 -> x0, blocking collectives: 24.3 us -> none  [the longest x1 12.8 us: per_device(): lax.all_gather(normed, 'tensor', axis=0, tiled=True)]
    ppermute x0 -> x4, waiting for transfers between devices: none -> 16.4 us  [from_peer(): return lax.ppermute(value, 'tensor', pairs)]
    pallas_call x0 -> x6, Pallas kernels: none -> 15.3 us  [call(): pl.pallas_call(kernel, out_shape=tuple(outs), in_specs=list(in_specs), ou...]
    all_to_all x1 -> x0, blocking collectives: 12.8 us -> none  [per_device(): lax.all_to_all(partial_cols, 'tensor', split_axis=0, concat_axis=1, tiled...]
    unnamed x8 -> x20, local copies, waits for them, and re-layouts: 0.02 us -> 10.4 us
    ppermute x0 -> x4, starting transfers between devices: none -> 6.39 us  [from_peer(): return lax.ppermute(value, 'tensor', pairs)]
    all_to_all x0 -> x1, starting transfers between devices: none -> 5.87 us  [per_device(): lax.all_to_all(spread, ('dp', 'tensor'), split_axis=0, concat_axis=0, til...]
  transfers between devices with their start and end apart: 0 -> 5, of which waited for: 0 -> 3; matrix products, arithmetic and copies ran while one was open for 0% -> 1% of each run, Pallas kernels for 0% -> 15%
where the time goes in v2:
time: 56.4 us; the launch traced here: 55.9 us
  waiting for transfers between devices  16.4 us (29%)
  Pallas kernels  15.3 us (27%)
  starting transfers between devices  12.3 us (22%)
  local copies, waits for them, and re-layouts  10.4 us (18%)
  other arithmetic  0.76 us (1%)
  between operations  0.75 us (1%)
    ppermute x4, waiting for transfers between devices, from_peer(): return lax.ppermute(value, 'tensor', pairs)  16.4 us
    pallas_call x6, Pallas kernels, call(): pl.pallas_call(kernel, out_shape=tuple(outs), in_specs=list(in_specs), ou...  15.3 us
    unnamed x20, local copies, waits for them, and re-layouts  10.4 us
    ppermute x4, starting transfers between devices, from_peer(): return lax.ppermute(value, 'tensor', pairs)  6.39 us
    all_to_all x1, starting transfers between devices, per_device(): lax.all_to_all(spread, ('dp', 'tensor'), split_axis=0, concat_axis=0, til...  5.87 us
  transfers between devices with their start and end apart: 5, of which 3 were waited for; matrix products, arithmetic and copies ran while one was open for 1% of the time, Pallas kernels for 15%

profile of v2, /device:TPU:0, one launch (start us, length us, event | category | flops | bytes accessed | tf_op | source)
XLA Modules:
  0.0 55.9 jit_solution(5228122797756225774)
XLA Ops:
  0.0 3.0 %collective-permute-start = (bf16[128,1536]{1,0:T(8,128)(2,1)}, bf16[128,1536]{1,0:T(8,128)(2,1)S(1)}, u32[]{:S(2)}, u32[]{:S(2)}) collective-permute-start(bf16[128,1536]{1,0:T(8,128)(2,1)} %bitcast.6), channel_id=1, source_target_pairs={{1,0},{0,1},{3,2},{2,3},{5,4},{4,5},{7,6},{6,7},{9,8},{8,9},{11,10... | collective-permute-start | bytes 1179656 | tf_op jit(solution)/shard_map/ppermute | solution.py:365
  3.6 0.8 %pad_maximum_fusion = f32[4608]{0:T(1024)S(1)} fusion(f32[768]{0:T(1024)} %param.16, f32[768]{0:T(1024)} %param.15, f32[1536]{0:T(1024)} %param.12, f32[1536]{0:T(1024)} %param.11), kind=kLoop, calls=%fused_computation | loop fusion | flops 13824 | bytes 36864 | tf_op jit(solution)/shard_map/concatenate | solution.py:367
  4.4 0.0 copy-start.3
  4.4 2.3 %copy-done.3 = bf16[2,768,1536]{2,1,0:T(8,128)(2,1)S(1)} copy-done((bf16[2,768,1536]{2,1,0:T(8,128)(2,1)S(1)}, bf16[2,768,1536]{2,1,0:T(8,128)(2,1)}, u32[]{:S(2)}) %copy-start.3) | copy-done | bytes 4718616
  6.7 0.0 copy-start.5
  6.7 1.0 %copy-done.5 = bf16[1,128,1536]{2,1,0:T(8,128)(2,1)S(1)} copy-done((bf16[1,128,1536]{2,1,0:T(8,128)(2,1)S(1)}, bf16[1,128,1536]{2,1,0:T(8,128)(2,1)}, u32[]{:S(2)}) %copy-start.5) | copy-done | bytes 393240
  7.7 0.0 copy-start.9
  7.7 0.8 %copy-done.9 = bf16[32,768]{1,0:T(8,128)(2,1)S(1)} copy-done((bf16[32,768]{1,0:T(8,128)(2,1)S(1)}, bf16[32,768]{1,0:T(8,128)(2,1)}, u32[]{:S(2)}) %copy-start.9) | copy-done | bytes 49176
  8.5 3.9 %first_block.1 = (bf16[176,768]{1,0:T(8,128)(2,1)S(1)}, f32[6,160,128]{2,1,0:T(8,128)S(1)}, bf16[2,768,1536]{2,1,0:T(8,128)(2,1)S(1)}) custom-call(s32[1]{0:T(128)S(6)} %copy.12.lengths_ref, bf16[1,128,1536]{2,1,0:T(8,128)(2,1)S(1)} %copy-done.5, f32[1,4608]{1,0:T(1,128)S(1)} %broadcast_in_dim.6.vectors_ref, bf16[32,768]{1,0:T(8,128)(2,1)S(1)} %copy-done.9, ...), custom_call_target="tpu_custom_call" | custom-call | flops 603979776 | bytes 10659844 | tf_op jit(solution)/shard_map/first_block/pallas_call | solution.py:332
  12.5 0.0 collective-permute-done.rows_ref
  12.5 5.2 %last_block.1 = (bf16[128,768]{1,0:T(8,128)(2,1)S(1)}, f32[6,256,128]{2,1,0:T(8,128)S(1)}, f32[32,1,1664]{2,1,0:T(1,128)}) custom-call(s32[1]{0:T(128)S(6)} %copy.12.lengths_ref, bf16[128,1536]{1,0:T(8,128)(2,1)S(1)} %collective-permute-done.rows_ref, f32[1,4608]{1,0:T(1,128)S(1)} %broadcast_in_dim.6.vectors_ref, bf16[32,768]{1,0:T(8,128)(2,1)S(1)} %copy-done.9, ...), custom_call_target="tpu_custom_call" | custom-call | flops 603979776 | bytes 6866948 | tf_op jit(solution)/shard_map/last_block/pallas_call | solution.py:332
  17.7 0.0 copy-start.7
  17.7 0.9 %copy-done.7 = f32[6,256,128]{2,1,0:T(8,128)} copy-done((f32[6,256,128]{2,1,0:T(8,128)}, f32[6,256,128]{2,1,0:T(8,128)S(1)}, u32[]{:S(2)}) %copy-start.7) | copy-done | bytes 786456
  18.6 5.9 %all-to-all-start = ((f32[32,1,1664]{2,1,0:T(1,128)}), f32[32,1,1664]{2,1,0:T(1,128)S(1)}, u32[]{:S(2)}, u32[]{:S(2)}) async-start(f32[32,1,1664]{2,1,0:T(1,128)} %get-tuple-element.18), calls=%async_computation | async-start | bytes 425984 | tf_op jit(solution)/shard_map/all_to_all | solution.py:424
  24.5 1.8 %collective-permute-start.1 = (bf16[176,768]{1,0:T(8,128)(2,1)S(1)}, bf16[176,768]{1,0:T(8,128)(2,1)S(1)}, u32[]{:S(2)}, u32[]{:S(2)}) collective-permute-start(bf16[176,768]{1,0:T(8,128)(2,1)S(1)} %get-tuple-element.20), channel_id=1, source_target_pairs={{1,0},{0,1},{3,2},{2,3},{5,4},{4,5},{7,6},{6,7},{9,8},{8,9},{11,10... | collective-permute-start | bytes 811016 | tf_op jit(solution)/shard_map/ppermute | solution.py:365
  26.3 0.3 collective-permute-start.2
  26.6 9.3 %collective-permute-done.1.refs_0_ = bf16[176,768]{1,0:T(8,128)(2,1)S(1)} collective-permute-done((bf16[176,768]{1,0:T(8,128)(2,1)S(1)}, bf16[176,768]{1,0:T(8,128)(2,1)S(1)}, u32[]{:S(2)}, u32[]{:S(2)}) %collective-permute-start.1) | collective-permute-done | bytes 270368 | tf_op jit(solution)/shard_map/ppermute | solution.py:365
  35.8 3.8 %collective-permute-done.2.refs_1_ = bf16[128,768]{1,0:T(8,128)(2,1)S(1)} collective-permute-done((bf16[128,768]{1,0:T(8,128)(2,1)S(1)}, bf16[128,768]{1,0:T(8,128)(2,1)S(1)}, u32[]{:S(2)}, u32[]{:S(2)}) %collective-permute-start.2) | collective-permute-done | bytes 196640 | tf_op jit(solution)/shard_map/ppermute | solution.py:365
  39.6 1.7 %copy-done.4 = bf16[768,1536]{1,0:T(8,128)(2,1)S(1)} copy-done((bf16[768,1536]{1,0:T(8,128)(2,1)S(1)}, bf16[768,1536]{1,0:T(8,128)(2,1)}, u32[]{:S(2)}) %copy-start.4) | copy-done | bytes 2359320
  41.3 1.1 %copy-done.8 = f32[6,256,128]{2,1,0:T(8,128)S(1)} copy-done((f32[6,256,128]{2,1,0:T(8,128)S(1)}, f32[6,256,128]{2,1,0:T(8,128)}, u32[]{:S(2)}) %copy-start.8) | copy-done | bytes 786456
  42.4 2.5 %peer_conv.1 = (f32[2,6,256,128]{3,2,1,0:T(8,128)S(1)}, f32[2,2,768]{2,1,0:T(2,128)S(1)}, bf16[768,1536]{1,0:T(8,128)(2,1)S(1)}) custom-call(f32[1,4608]{1,0:T(1,128)S(1)} %broadcast_in_dim.6.vectors_ref, f32[6,256,128]{2,1,0:T(8,128)S(1)} %copy-done.8, bf16[768,1536]{1,0:T(8,128)(2,1)S(1)} %copy-done.4, ...), custom_call_target="tpu_custom_call" | custom-call | flops 12582912 | bytes 7575552 | tf_op jit(solution)/shard_map/peer_conv/pallas_call | solution.py:332
  44.9 0.0 copy-start
  44.9 1.2 %copy-done = f32[2,6,256,128]{3,2,1,0:T(8,128)} copy-done((f32[2,6,256,128]{3,2,1,0:T(8,128)}, f32[2,6,256,128]{3,2,1,0:T(8,128)S(1)}, u32[]{:S(2)}) %copy-start) | copy-done | bytes 1572888
  46.1 0.0 all-to-all-done
  46.1 1.4 %copy-done.1 = f32[2,6,256,128]{3,2,1,0:T(8,128)S(1)} copy-done((f32[2,6,256,128]{3,2,1,0:T(8,128)S(1)}, f32[2,6,256,128]{3,2,1,0:T(8,128)}, u32[]{:S(2)}) %copy-start.1) | copy-done | bytes 1572888
  47.5 1.1 %branch_sent.1 = bf16[1,128,768]{2,1,0:T(8,128)(2,1)S(1)} custom-call(f32[16,2,1,1664]{3,2,1,0:T(1,128)S(1)} %bitcast.4, f32[2,6,256,128]{3,2,1,0:T(8,128)S(1)} %copy-done.1, f32[2,2,768]{2,1,0:T(2,128)S(1)} %get-tuple-element.23.norms_ref, bf16[768,1536]{1,0:T(8,128)(2,1)S(1)} %get-tuple-element.24.weight_ref), custom_call_target="tpu_custom_call" | custom-call | flops 301989888 | bytes 4354048 | tf_op jit(solution)/shard_map/branch_sent/pallas_call | solution.py:332
  48.6 1.3 %collective-permute-start.3 = (bf16[128,768]{1,0:T(8,128)(2,1)S(1)}, bf16[128,768]{1,0:T(8,128)(2,1)S(1)}, u32[]{:S(2)}, u32[]{:S(2)}) collective-permute-start(bf16[128,768]{1,0:T(8,128)(2,1)S(1)} %bitcast.8), channel_id=1, source_target_pairs={{1,0},{0,1},{3,2},{2,3},{5,4},{4,5},{7,6},{6,7},{9,8},{8,9},{11,10... | collective-permute-start | bytes 589832 | tf_op jit(solution)/shard_map/ppermute | solution.py:365
  49.9 0.0 copy-done.6
  50.0 0.0 copy-done.2
  50.0 1.9 %branch_kept.1 = (bf16[128,1536]{1,0:T(8,128)(2,1)}, bf16[1,128,768]{2,1,0:T(8,128)(2,1)S(1)}) custom-call(f32[16,2,1,1664]{3,2,1,0:T(1,128)S(1)} %bitcast.5, f32[2,6,256,128]{3,2,1,0:T(8,128)S(1)} %copy-done.2, f32[2,2,768]{2,1,0:T(2,128)S(1)} %get-tuple-element.23.norms_ref, bf16[768,1536]{1,0:T(8,128)(2,1)S(1)} %get-tuple-element.24.weight_ref, ...), custom_call_target="tpu_custom_call" | custom-call | flops 301989888 | bytes 5140480 | tf_op jit(solution)/shard_map/branch_kept/pallas_call | solution.py:332
  51.8 3.3 %collective-permute-done.3.refs_0_ = bf16[128,768]{1,0:T(8,128)(2,1)S(1)} collective-permute-done((bf16[128,768]{1,0:T(8,128)(2,1)S(1)}, bf16[128,768]{1,0:T(8,128)(2,1)S(1)}, u32[]{:S(2)}, u32[]{:S(2)}) %collective-permute-start.3) | collective-permute-done | bytes 196640 | tf_op jit(solution)/shard_map/ppermute | solution.py:365
  55.2 0.7 %residual.1 = bf16[128,1536]{1,0:T(8,128)(2,1)} custom-call(bf16[128,1536]{1,0:T(8,128)(2,1)} %get-tuple-element.25.filled_ref, bf16[1,128,768]{2,1,0:T(8,128)(2,1)S(1)} %get-tuple-element.26.base_ref, bf16[128,768]{1,0:T(8,128)(2,1)S(1)} %collective-permute-done.3.refs_0_), custom_call_target="tpu_custom_call", output_to_operand_aliasing={{}: (0, {})} | custom-call | bytes 1179648 | tf_op jit(solution)/shard_map/residual/pallas_call | solution.py:332
  (6 shorter events, 0.0 us)
Async XLA Ops:
  0.0 12.5 %collective-permute-start = (bf16[128,1536]{1,0:T(8,128)(2,1)}, bf16[128,1536]{1,0:T(8,128)(2,1)S(1)}, u32[]{:S(2)}, u32[]{:S(2)}) collective-permute-start(bf16[128,1536]{1,0:T(8,128)(2,1)} %bitcast.6), channel_id=1, source_target_pairs={{1,0},{0,1},{3,2},{2,3},{5,4},{4,5},{7,6},{6,7},{9,8},{8,9},{11,10... | collective-permute-start | bytes 1179656 | tf_op jit(solution)/shard_map/ppermute | solution.py:365
  4.4 2.3 %copy-start.3 = (bf16[2,768,1536]{2,1,0:T(8,128)(2,1)S(1)}, bf16[2,768,1536]{2,1,0:T(8,128)(2,1)}, u32[]{:S(2)}) copy-start(bf16[2,768,1536]{2,1,0:T(8,128)(2,1)} %weight_ref.2) | copy-start | bytes 14155780
  6.7 1.0 %copy-start.5 = (bf16[1,128,1536]{2,1,0:T(8,128)(2,1)S(1)}, bf16[1,128,1536]{2,1,0:T(8,128)(2,1)}, u32[]{:S(2)}) copy-start(bf16[1,128,1536]{2,1,0:T(8,128)(2,1)} %frames_ref.1) | copy-start | bytes 1179652
  7.7 0.8 %copy-start.9 = (bf16[32,768]{1,0:T(8,128)(2,1)S(1)}, bf16[32,768]{1,0:T(8,128)(2,1)}, u32[]{:S(2)}) copy-start(bf16[32,768]{1,0:T(8,128)(2,1)} %taps_ref.3) | copy-start | bytes 147460
  17.7 0.9 %copy-start.7 = (f32[6,256,128]{2,1,0:T(8,128)}, f32[6,256,128]{2,1,0:T(8,128)S(1)}, u32[]{:S(2)}) copy-start(f32[6,256,128]{2,1,0:T(8,128)S(1)} %get-tuple-element.19.conv_ref) | copy-start | bytes 2359300
  18.6 27.5 %all-to-all-start = ((f32[32,1,1664]{2,1,0:T(1,128)}), f32[32,1,1664]{2,1,0:T(1,128)S(1)}, u32[]{:S(2)}, u32[]{:S(2)}) async-start(f32[32,1,1664]{2,1,0:T(1,128)} %get-tuple-element.18), calls=%async_computation | async-start | bytes 425984 | tf_op jit(solution)/shard_map/all_to_all | solution.py:424
  24.5 11.4 %collective-permute-start.1 = (bf16[176,768]{1,0:T(8,128)(2,1)S(1)}, bf16[176,768]{1,0:T(8,128)(2,1)S(1)}, u32[]{:S(2)}, u32[]{:S(2)}) collective-permute-start(bf16[176,768]{1,0:T(8,128)(2,1)S(1)} %get-tuple-element.20), channel_id=1, source_target_pairs={{1,0},{0,1},{3,2},{2,3},{5,4},{4,5},{7,6},{6,7},{9,8},{8,9},{11,10... | collective-permute-start | bytes 811016 | tf_op jit(solution)/shard_map/ppermute | solution.py:365
  26.3 13.3 %collective-permute-start.2 = (bf16[128,768]{1,0:T(8,128)(2,1)S(1)}, bf16[128,768]{1,0:T(8,128)(2,1)S(1)}, u32[]{:S(2)}, u32[]{:S(2)}) collective-permute-start(bf16[128,768]{1,0:T(8,128)(2,1)S(1)} %get-tuple-element.21), channel_id=1, source_target_pairs={{1,0},{0,1},{3,2},{2,3},{5,4},{4,5},{7,6},{6,7},{9,8},{8,9},{11,10... | collective-permute-start | bytes 589832 | tf_op jit(solution)/shard_map/ppermute | solution.py:365
  39.6 1.7 %copy-start.4 = (bf16[768,1536]{1,0:T(8,128)(2,1)S(1)}, bf16[768,1536]{1,0:T(8,128)(2,1)}, u32[]{:S(2)}) copy-start(bf16[768,1536]{1,0:T(8,128)(2,1)} %weight_ref.3) | copy-start | bytes 7077892
  41.3 1.1 %copy-start.8 = (f32[6,256,128]{2,1,0:T(8,128)S(1)}, f32[6,256,128]{2,1,0:T(8,128)}, u32[]{:S(2)}) copy-start(f32[6,256,128]{2,1,0:T(8,128)} %copy-done.7) | copy-start | bytes 2359300
  42.4 7.5 %copy-start.6 = (bf16[1,128,1536]{2,1,0:T(8,128)(2,1)S(1)}, bf16[1,128,1536]{2,1,0:T(8,128)(2,1)}, u32[]{:S(2)}) copy-start(bf16[1,128,1536]{2,1,0:T(8,128)(2,1)} %frames_ref.1) | copy-start | bytes 1179652
  44.9 1.2 %copy-start = (f32[2,6,256,128]{3,2,1,0:T(8,128)}, f32[2,6,256,128]{3,2,1,0:T(8,128)S(1)}, u32[]{:S(2)}) copy-start(f32[2,6,256,128]{3,2,1,0:T(8,128)S(1)} %get-tuple-element.22.convs_ref) | copy-start | bytes 4718596
  46.1 1.4 %copy-start.1 = (f32[2,6,256,128]{3,2,1,0:T(8,128)S(1)}, f32[2,6,256,128]{3,2,1,0:T(8,128)}, u32[]{:S(2)}) copy-start(f32[2,6,256,128]{3,2,1,0:T(8,128)} %copy-done) | copy-start | bytes 4718596
  47.5 2.4 %copy-start.2 = (f32[2,6,256,128]{3,2,1,0:T(8,128)S(1)}, f32[2,6,256,128]{3,2,1,0:T(8,128)}, u32[]{:S(2)}) copy-start(f32[2,6,256,128]{3,2,1,0:T(8,128)} %copy-done) | copy-start | bytes 4718596
  48.6 6.5 %collective-permute-start.3 = (bf16[128,768]{1,0:T(8,128)(2,1)S(1)}, bf16[128,768]{1,0:T(8,128)(2,1)S(1)}, u32[]{:S(2)}, u32[]{:S(2)}) collective-permute-start(bf16[128,768]{1,0:T(8,128)(2,1)S(1)} %bitcast.8), channel_id=1, source_target_pairs={{1,0},{0,1},{3,2},{2,3},{5,4},{4,5},{7,6},{6,7},{9,8},{8,9},{11,10... | collective-permute-start | bytes 589832 | tf_op jit(solution)/shard_map/ppermute | solution.py:365

commit v3 on v0

v3 whole, which is shorter than its diff:
```python
import functools

import jax
import jax.numpy as jnp
from jax import lax
from jax.experimental import pallas as pl
from jax.experimental.pallas import tpu as pltpu
from jax.sharding import PartitionSpec as P

KERNEL = 32
LANES = 128
WIDE = 256
HALO = 16
EDGE = 8
EXTRA = 48
F32 = jnp.float32
BF16 = jnp.bfloat16

VMEM = pl.BlockSpec(memory_space=pltpu.VMEM)
SMEM = pl.BlockSpec(memory_space=pltpu.SMEM)
HBM = pl.BlockSpec(memory_space=pltpu.HBM)


def layer_norm(rows, gain, bias):
    values = rows.astype(F32)
    center = jnp.mean(values, axis=-1, keepdims=True)
    values = values - center
    spread = jnp.mean(values * values, axis=-1, keepdims=True)
    return (values * lax.rsqrt(spread + 1e-05) * gain + bias).astype(BF16)


def swish(z):
    return z * jax.nn.sigmoid(z)


def cuts(width, most):
    return [slice(at, at + most) for at in range(0, width, most)]


def valid_rows(first, rows, length):
    index = first + lax.broadcasted_iota(jnp.int32, (rows, 1), 0)
    return index < length


def glu_of(normed, weight_ref, cut, keep):
    value = jnp.dot(normed, weight_ref[0, :, cut], preferred_element_type=F32)
    gate = jnp.dot(normed, weight_ref[1, :, cut], preferred_element_type=F32)
    glu = (value * jax.nn.sigmoid(gate)).astype(BF16)
    return jnp.where(keep, glu.astype(F32), 0.0)


def three_parts(vector):
    parts = []
    for _ in range(3):
        part = vector.astype(BF16).astype(F32)
        parts.append(part)
        vector = vector - part
    return parts


def affine(vectors_ref):
    rows = [vectors_ref[at : at + 1, :] for at in range(vectors_ref.shape[0] - 2)]
    half = len(rows) // 2
    return jnp.concatenate(rows[:half], axis=1), jnp.concatenate(rows[half:], axis=1)


def clear_ends(edge_ref):
    tiles, total, _ = edge_ref.shape
    zeros = jnp.zeros((EDGE, LANES), F32)
    for tile in range(tiles):
        edge_ref[tile, 0:EDGE, :] = zeros
        edge_ref[tile, total - EDGE : total, :] = zeros


def taps_at(taps_ref, offset, tile):
    cut = slice(tile * LANES, (tile + 1) * LANES)
    taps = {}
    for step in range(5):
        tap = 8 * step + offset - 1
        if 0 <= tap < KERNEL:
            taps[step] = jnp.broadcast_to(taps_ref[tap : tap + 1, cut], (8, LANES))
    return taps


def block_conv(block, tile, edge_ref, taps_ref):
    rows = block.shape[0]
    edge_ref[tile, EDGE : EDGE + rows, :] = block
    count = (rows + 2 * HALO) // 8
    total = [None] * count
    for offset in range(8):
        taps = taps_at(taps_ref, offset, tile)
        for at in range(count + 4):
            start = 8 * at + offset - 2 * HALO
            if start <= -8 or start >= rows:
                continue
            values = edge_ref[tile, EDGE + start : EDGE + start + 8, :]
            for step, tap in taps.items():
                if 0 <= at - step < count:
                    term = values * tap
                    seen = total[at - step]
                    total[at - step] = term if seen is None else seen + term
    return total


def first_block_kernel(
    lengths_ref, frames_ref, vectors_ref, taps_ref, weight_ref,
    pack_ref, sums_ref, held_ref,
    rows_ref, raw_ref, wide_taps_ref, edge_ref, rows_sem, weight_sems,
):
    rows = rows_ref.shape[0]
    chans = held_ref.shape[2]
    own = lax.axis_index("tensor")
    rows_copy = pltpu.make_async_copy(frames_ref.at[0], rows_ref, rows_sem)
    rows_copy.start()
    pieces = cuts(chans, WIDE)
    copies = []
    for at, cut in enumerate(pieces):
        for side in range(2):
            place = (side, pl.ds(cut.start, WIDE))
            copy = pltpu.make_async_copy(
                weight_ref.at[place], raw_ref.at[place], weight_sems.at[at, side]
            )
            copy.start()
            copies.append(copy)
    clear_ends(edge_ref)
    keep = valid_rows(own * rows, rows, lengths_ref[0])
    taps = taps_ref[...]
    wide_taps_ref[...] = taps.astype(F32)
    pack_ref[rows : rows + KERNEL, :] = taps
    last = vectors_ref.shape[0] - 2
    extra = three_parts(vectors_ref[last : last + 1, :])
    extra += three_parts(vectors_ref[last + 1 : last + 2, :])
    extra.append(jnp.zeros((EXTRA - KERNEL - len(extra), chans), F32))
    pack_ref[rows + KERNEL :, :] = jnp.concatenate(extra).astype(BF16)
    gain, bias = affine(vectors_ref)
    rows_copy.wait()
    normed = layer_norm(rows_ref[...], gain, bias)
    for at, cut in enumerate(pieces):
        for side in range(2):
            copies[2 * at + side].wait()
            held_ref[side, :, cut] = raw_ref[side, cut, :].T
        glu = glu_of(normed, held_ref, cut, keep)
        pack_ref[0:rows, cut] = glu.astype(BF16)
        for tile in range(cut.start // LANES, cut.stop // LANES):
            seen = slice(tile * LANES - cut.start, (tile + 1) * LANES - cut.start)
            total = block_conv(glu[:, seen], tile, edge_ref, wide_taps_ref)
            for step, each in enumerate(total):
                sums_ref[tile, 8 * step : 8 * step + 8, :] = each


def last_block_kernel(
    lengths_ref, rows_ref, vectors_ref, taps_ref, weight_ref, first_sums_ref,
    late_ref, near_ref, sent_ref, kept_ref, spread_ref,
    wide_taps_ref, edge_ref, sums_ref,
):
    rows, chans = late_ref.shape
    tiles = chans // LANES
    own = lax.axis_index("tensor")
    peer = 1 - own
    length = lengths_ref[0]
    count = length.astype(F32)
    keep = valid_rows(peer * rows, rows, length)
    own_valid, peer_valid = (valid_rows(at * rows, rows, length).astype(F32) for at in (own, peer))
    clear_ends(edge_ref)
    wide_taps_ref[...] = taps_ref[...].astype(F32)
    reach = rows + 2 * HALO
    own_at = pl.multiple_of(own * rows, rows)
    peer_at = pl.multiple_of(peer * rows, rows)
    for tile in range(tiles):
        sums_ref[tile, pl.ds(peer_at, reach), :] = jnp.zeros((reach, LANES), F32)
        sums_ref[tile, pl.ds(own_at, reach), :] = first_sums_ref[tile]
    normed = layer_norm(rows_ref[...], *affine(vectors_ref))
    for cut in cuts(chans, WIDE):
        glu = glu_of(normed, weight_ref, cut, keep)
        late_ref[:, cut] = glu.astype(BF16)
        for tile in range(cut.start // LANES, cut.stop // LANES):
            seen = slice(tile * LANES - cut.start, (tile + 1) * LANES - cut.start)
            lanes = slice(tile * LANES, (tile + 1) * LANES)
            for step, each in enumerate(block_conv(glu[:, seen], tile, edge_ref, wide_taps_ref)):
                at = pl.ds(peer_at + 8 * step, 8)
                sums_ref[tile, at, :] = sums_ref[tile, at, :] + each
            kept = sums_ref[tile, pl.ds(own_at + HALO, rows), :]
            sent = sums_ref[tile, pl.ds(peer_at + HALO, rows), :]
            kept_ref[tile] = kept
            sent_ref[tile] = sent
            sums = jnp.sum(kept * own_valid, axis=0, keepdims=True)
            sums += jnp.sum(sent * peer_valid, axis=0, keepdims=True)
            mean = sums / count
            off = (kept - mean) * own_valid
            squares = jnp.sum(off * off, axis=0, keepdims=True)
            off = (sent - mean) * peer_valid
            squares += jnp.sum(off * off, axis=0, keepdims=True)
            spread_ref[0, :, lanes] = sums
            spread_ref[0, :, chans + lanes.start : chans + lanes.stop] = squares
    near = pl.multiple_of(own * (rows - HALO), HALO)
    near_ref[...] = late_ref[pl.ds(near, HALO), :]
    spread_ref[0, :, 2 * chans :] = jnp.full((1, LANES), count, F32)
    stats = spread_ref[0]
    for at in range(1, spread_ref.shape[0]):
        spread_ref[at] = stats


def peer_conv_kernel(
    vectors_ref, weight_ref, pack_ref, sums_ref, taps_ref, norms_ref, held_ref,
    raw_ref, edge_ref, weight_sem,
):
    parts, chans, cols = held_ref.shape
    rows = pack_ref.shape[0] - EXTRA
    copy = pltpu.make_async_copy(weight_ref, raw_ref, weight_sem)
    copy.start()
    clear_ends(edge_ref)
    taps_ref[...] = pack_ref[rows : rows + KERNEL, :].astype(F32)
    extra = pack_ref[rows + KERNEL :, :].astype(F32)
    last = vectors_ref.shape[0] - 2
    norms_ref[0] = vectors_ref[last : last + 2, :]
    norms_ref[1, 0:1, :] = extra[0:1] + (extra[1:2] + extra[2:3])
    norms_ref[1, 1:2, :] = extra[3:4] + (extra[4:5] + extra[5:6])
    for tile in range(chans // LANES):
        lanes = slice(tile * LANES, (tile + 1) * LANES)
        block = pack_ref[0:rows, lanes].astype(F32)
        for step, each in enumerate(block_conv(block, tile, edge_ref, taps_ref)):
            sums_ref[tile, 8 * step : 8 * step + 8, :] = each
    copy.wait()
    for place in range(parts):
        for cut in cuts(chans, WIDE):
            at = place * chans
            held_ref[place, cut, :] = raw_ref[:, at + cut.start : at + cut.stop].T


def scales(stats_ref, norms_ref):
    chans = norms_ref.shape[2]
    own = lax.axis_index("tensor")
    found = []
    for shift, place in enumerate((own, 1 - own)):
        seen = stats_ref[:, pl.ds(place, 1), :, :]
        counts = seen[..., 2 * chans : 2 * chans + 1]
        sums = seen[..., :chans]
        count = jnp.sum(counts, axis=0)[0]
        mean = jnp.sum(sums, axis=0)[0] / count
        off = sums / counts - mean
        var = jnp.sum(seen[..., chans : 2 * chans] + counts * off * off, axis=0)[0] / count
        scale = lax.rsqrt(var + 1e-05) * norms_ref[shift, 0:1, :]
        found.append((mean, scale, norms_ref[shift, 1:2, :]))
    return found


def branch_rows(found, conv_of, weight_ref):
    own = lax.axis_index("tensor")
    total = None
    for shift, (mean, scale, bias) in enumerate(found):
        acts = []
        for tile in range(mean.shape[1] // LANES):
            lanes = slice(tile * LANES, (tile + 1) * LANES)
            z = (conv_of(shift, tile) - mean[:, lanes]) * scale[:, lanes] + bias[:, lanes]
            acts.append(swish(z).astype(BF16))
        place = own if shift == 0 else 1 - own
        term = jnp.dot(jnp.concatenate(acts, axis=1), weight_ref[place], preferred_element_type=F32)
        total = term if total is None else total + term
    return total


def sent_kernel(
    stats_ref, conv_ref, early_ref, near_ref, taps_ref, norms_ref, weight_ref,
    out_ref, peer_ref, edge_ref,
):
    own = lax.axis_index("tensor")
    tiles, rows, _ = conv_ref.shape
    target = pl.multiple_of(jnp.where(own == 0, 0, rows - HALO), HALO)
    source = pl.multiple_of(jnp.where(own == 0, 0, 2 * HALO), HALO)
    for tile in range(tiles):
        lanes = slice(tile * LANES, (tile + 1) * LANES)
        edge_ref[tile] = jnp.zeros((3 * HALO, LANES), F32)
        edge_ref[tile, pl.ds(source, HALO), :] = near_ref[:, lanes].astype(F32)
        peer_ref[tile] = early_ref[tile, HALO : HALO + rows, :]
        total = [peer_ref[tile, pl.ds(target + 8 * at, 8), :] for at in range(HALO // 8)]
        for tap in range(KERNEL):
            weight = jnp.broadcast_to(taps_ref[tap : tap + 1, lanes], (8, LANES))
            for at in range(HALO // 8):
                start = 8 * at + tap + 1
                total[at] += edge_ref[tile, start : start + 8, :] * weight
        for at in range(HALO // 8):
            peer_ref[tile, pl.ds(target + 8 * at, 8), :] = total[at]
    found = scales(stats_ref, norms_ref)
    branch = branch_rows(found, lambda shift, tile: (peer_ref if shift else conv_ref)[tile], weight_ref)
    out_ref[...] = branch.astype(BF16)


def columns(ref, place, cols):
    return ref.at[:, pl.ds(pl.multiple_of(place * cols, LANES), cols)]


def kept_kernel(
    stats_ref, conv_ref, early_ref, late_ref, taps_ref, norms_ref, weight_ref, frames_ref,
    out_ref, base_ref, mine_ref, edge_ref, peer_ref, sems, out_sem,
):
    own = lax.axis_index("tensor")
    rows, cols = mine_ref.shape
    tiles = conv_ref.shape[0]
    copies = [(columns(frames_ref, own, cols), mine_ref), (columns(frames_ref, 1 - own, cols), base_ref)]
    copies = [pltpu.make_async_copy(*pair, sems.at[at]) for at, pair in enumerate(copies)]
    for copy in copies:
        copy.start()
    clear_ends(edge_ref)
    source = pl.multiple_of(jnp.where(own == 0, 0, rows + HALO), HALO)
    target = pl.multiple_of(jnp.where(own == 0, rows - HALO, 0), HALO)
    for tile in range(tiles):
        lanes = slice(tile * LANES, (tile + 1) * LANES)
        total = block_conv(late_ref[:, lanes].astype(F32), tile, edge_ref, taps_ref)
        for step in range(rows // 8):
            peer_ref[tile, 8 * step : 8 * step + 8, :] = total[step + HALO // 8]
        for at in range(HALO // 8):
            place = pl.ds(target + 8 * at, 8)
            peer_ref[tile, place, :] = peer_ref[tile, place, :] + early_ref[tile, pl.ds(source + 8 * at, 8), :]
    found = scales(stats_ref, norms_ref)
    branch = branch_rows(found, lambda shift, tile: (peer_ref if shift else conv_ref)[tile], weight_ref)
    for copy in copies:
        copy.wait()
    mine_ref[...] = (mine_ref[...].astype(F32) + branch).astype(BF16)
    out_copy = pltpu.make_async_copy(mine_ref, columns(out_ref, own, cols), out_sem)
    out_copy.start()
    out_copy.wait()


def finish_kernel(filled_ref, base_ref, got_ref, out_ref, done_ref, out_sem):
    own = lax.axis_index("tensor")
    cols = base_ref.shape[1]
    done_ref[...] = (base_ref[...].astype(F32) + got_ref[...].astype(F32)).astype(BF16)
    copy = pltpu.make_async_copy(done_ref, columns(out_ref, 1 - own, cols), out_sem)
    copy.start()
    copy.wait()


def shape(dims, kind):
    return jax.ShapeDtypeStruct(dims, kind)


def call(kernel, outs, in_specs, operands, out_specs=None, scratch=(), name=None, aliases=None, room=32):
    return pl.pallas_call(
        kernel,
        out_shape=tuple(outs),
        in_specs=list(in_specs),
        out_specs=tuple(out_specs or [VMEM] * len(outs)),
        scratch_shapes=list(scratch),
        input_output_aliases=aliases or {},
        compiler_params=pltpu.CompilerParams(vmem_limit_bytes=room * 1024 * 1024),
        name=name,
    )(*operands)


def two_parts(
    devices, frames_in, lengths, ln_gain, ln_bias, glu_weight, conv_kernel, bn_gain, bn_bias, out_weight
):
    _, span, width = frames_in.shape
    chans = glu_weight.shape[1]
    cols = out_weight.shape[0]
    tiles = chans // LANES
    pieces = chans // WIDE

    def swap(value):
        return lax.ppermute(value, "tensor", [(0, 1), (1, 0)])

    frames = swap(frames_in[0])
    vectors = jnp.concatenate([ln_gain, ln_bias, bn_gain, bn_bias]).reshape(-1, chans)
    edge = pltpu.VMEM((tiles, span + 2 * EDGE, LANES), F32)
    wide_taps = pltpu.VMEM((KERNEL, chans), F32)
    dma = pltpu.SemaphoreType.DMA
    reach = shape((tiles, span + 2 * HALO, LANES), F32)
    block = shape((tiles, span, LANES), F32)
    pack, first_sums, held = call(
        first_block_kernel,
        (shape((span + EXTRA, chans), BF16), reach, shape((2, width, chans), BF16)),
        [SMEM, HBM, VMEM, VMEM, HBM],
        (lengths, frames_in, vectors, conv_kernel, glu_weight),
        scratch=(
            pltpu.VMEM((span, width), BF16),
            pltpu.VMEM((2, chans, width), BF16),
            wide_taps,
            edge,
            dma,
            dma((pieces, 2)),
        ),
        name="first_block",
        room=48,
    )
    early = swap(pack)
    late, near, sent_conv, kept_conv, spread = call(
        last_block_kernel,
        (
            shape((span, chans), BF16),
            shape((HALO, chans), BF16),
            block,
            block,
            shape((devices, 1, 2 * chans + LANES), F32),
        ),
        [SMEM] + [VMEM] * 5,
        (lengths, frames, vectors, conv_kernel, held, first_sums),
        scratch=(wide_taps, edge, pltpu.VMEM((tiles, 2 * span + 2 * HALO, LANES), F32)),
        name="last_block",
    )
    spread, early = lax.optimization_barrier((spread, early))
    stats = lax.all_to_all(spread, ("dp", "tensor"), split_axis=0, concat_axis=0, tiled=True)
    stats = stats.reshape((devices // 2, 2) + spread.shape[1:])
    near, late = swap(near), swap(late)
    early_sums, taps, norms, weight = call(
        peer_conv_kernel,
        (reach, shape((KERNEL, chans), F32), shape((2, 2, chans), F32), shape((2, chans, cols), BF16)),
        [VMEM, HBM, VMEM],
        (vectors, out_weight, early),
        scratch=(pltpu.VMEM(out_weight.shape, BF16), edge, dma),
        name="peer_conv",
    )
    (sent,) = call(
        sent_kernel,
        (shape((span, cols), BF16),),
        [VMEM] * 7,
        (stats, sent_conv, early_sums, near, taps, norms, weight),
        scratch=(pltpu.VMEM(block.shape, F32), pltpu.VMEM((tiles, 3 * HALO, LANES), F32)),
        name="branch_sent",
    )
    got = swap(sent)
    filled, base = call(
        kept_kernel,
        (shape((span, width), BF16), shape((span, cols), BF16)),
        [VMEM] * 7 + [HBM],
        (stats, kept_conv, early_sums, late, taps, norms, weight, frames_in[0]),
        out_specs=(HBM, VMEM),
        scratch=(
            pltpu.VMEM((span, cols), BF16),
            edge,
            pltpu.VMEM(block.shape, F32),
            dma((2,)),
            dma,
        ),
        name="branch_kept",
    )
    (out,) = call(
        finish_kernel,
        (shape((span, width), BF16),),
        [HBM, VMEM, VMEM],
        (filled, base, got),
        out_specs=(HBM,),
        scratch=(pltpu.VMEM((span, cols), BF16), dma),
        aliases={0: 0},
        name="residual",
    )
    return out[None]


def contract_last(left, right):
    return lax.dot_general(
        left, right, (((1,), (1,)), ((), ())), preferred_element_type=F32
    )


def many_parts(
    devices, frames_in, lengths, ln_gain, ln_bias, glu_weight, conv_kernel, bn_gain, bn_bias, out_weight
):
    rows = frames_in[0]
    chans = glu_weight.shape[1]
    normed = layer_norm(rows, ln_gain, ln_bias)
    proj = contract_last(
        lax.all_gather(normed, "tensor", axis=0, tiled=True),
        glu_weight.reshape(2 * chans, rows.shape[1]),
    )
    valid = valid_rows(0, proj.shape[0], lengths[0])
    glu = (proj[:, :chans] * jax.nn.sigmoid(proj[:, chans:])).astype(BF16)
    glu = jnp.where(valid, glu, jnp.zeros_like(glu)).astype(F32)
    padded = jnp.pad(glu, ((15, KERNEL - 16), (0, 0)))
    taps = conv_kernel.astype(F32)
    conv = jnp.zeros_like(glu)
    for tap in range(KERNEL):
        conv = conv + padded[tap : tap + glu.shape[0]] * taps[tap]
    own = lengths[0].astype(F32)
    local = jnp.sum(jnp.where(valid, conv, 0.0), axis=0) / own
    squares = jnp.sum(jnp.where(valid, conv - local, 0.0) ** 2, axis=0)
    count = lax.psum(own, "dp")
    mean = lax.psum(local * own, "dp") / count
    var = lax.psum(squares + own * (local - mean) ** 2, "dp") / count
    z = (conv - mean) * (lax.rsqrt(var + 1e-05) * bn_gain) + bn_bias
    act = lax.all_gather(swish(z).astype(BF16), "tensor", axis=1, tiled=True)
    branch = contract_last(act, out_weight)
    branch = lax.all_to_all(branch, "tensor", split_axis=0, concat_axis=1, tiled=True)
    return (rows.astype(F32) + branch).astype(BF16)[None]


def solution(mesh):
    sizes = dict(mesh.shape)
    body = two_parts if sizes["tensor"] == 2 else many_parts
    body = functools.partial(body, sizes["tensor"] * sizes["dp"])
    return jax.shard_map(
        body,
        mesh=mesh,
        in_specs=(
            P("dp", "tensor", None),
            P("dp"),
            P(),
            P(),
            P(None, "tensor", None),
            P(None, "tensor"),
            P("tensor"),
            P("tensor"),
            P("tensor", None),
        ),
        out_specs=P("dp", "tensor", None),
        check_vma=False,
    )
```

time: 120 us -> 45.1 us (0.38)
  blocking collectives: 100 us -> 0 us
  Pallas kernels: 0 us -> 14 us
  starting transfers between devices: 0 us -> 11.2 us
  other arithmetic: 11.8 us -> 0.76 us
  waiting for transfers between devices: 0 us -> 8.37 us
  local copies, waits for them, and re-layouts: 2.41 us -> 9.43 us
  matrix products: 4.56 us -> 0 us
    psum x2 -> x0, blocking collectives: 63.3 us -> none  [the longest x1 33.8 us: batch_stats(): sums, count = lax.psum((local_sums, own_count), 'dp')]
    all_gather x2 -> x0, blocking collectives: 24.3 us -> none  [the longest x1 12.8 us: per_device(): lax.all_gather(normed, 'tensor', axis=0, tiled=True)]
    pallas_call x0 -> x6, Pallas kernels: none -> 14 us  [call(): pl.pallas_call(kernel, out_shape=tuple(outs), in_specs=list(in_specs), ou...]
    all_to_all x1 -> x0, blocking collectives: 12.8 us -> none  [per_device(): lax.all_to_all(partial_cols, 'tensor', split_axis=0, concat_axis=1, tiled...]
    unnamed x8 -> x24, local copies, waits for them, and re-layouts: 0.02 us -> 9.43 us
    reduce_sum x4 -> x0, other arithmetic: 5.81 us -> none  [the longest x1 3.26 us: batch_stats(): local_sums = reduce_fn(jnp.sum(conv * weight_rows, axis=0)[None])[0]]
    ppermute x0 -> x5, starting transfers between devices: none -> 5.66 us  [swap(): return lax.ppermute(value, 'tensor', [(0, 1), (1, 0)])]
    all_to_all x0 -> x1, starting transfers between devices: none -> 5.56 us  [two_parts(): lax.all_to_all(spread, ('dp', 'tensor'), split_axis=0, concat_axis=0, til...]
  transfers between devices with their start and end apart: 0 -> 6, of which waited for: 0 -> 4; matrix products, arithmetic and copies ran while one was open for 0% -> 2% of each run, Pallas kernels for 0% -> 30%
where the time goes in v3:
time: 45.1 us; the launch traced here: 44.5 us
  Pallas kernels  14 us (31%)
  starting transfers between devices  11.2 us (25%)
  local copies, waits for them, and re-layouts  9.43 us (21%)
  waiting for transfers between devices  8.37 us (19%)
  other arithmetic  0.76 us (2%)
  between operations  0.73 us (2%)
    pallas_call x6, Pallas kernels, call(): pl.pallas_call(kernel, out_shape=tuple(outs), in_specs=list(in_specs), ou...  14 us
    unnamed x24, local copies, waits for them, and re-layouts  9.43 us
    ppermute x5, starting transfers between devices, swap(): return lax.ppermute(value, 'tensor', [(0, 1), (1, 0)])  5.66 us
    all_to_all x1, starting transfers between devices, two_parts(): lax.all_to_all(spread, ('dp', 'tensor'), split_axis=0, concat_axis=0, til...  5.56 us
    ppermute x5, waiting for transfers between devices, swap(): return lax.ppermute(value, 'tensor', [(0, 1), (1, 0)])  5.51 us
    all_to_all x1, waiting for transfers between devices, two_parts(): lax.all_to_all(spread, ('dp', 'tensor'), split_axis=0, concat_axis=0, til...  2.87 us
  transfers between devices with their start and end apart: 6, of which 4 were waited for; matrix products, arithmetic and copies ran while one was open for 2% of the time, Pallas kernels for 30%

profile of v3, /device:TPU:0, one launch (start us, length us, event | category | flops | bytes accessed | tf_op | source)
XLA Modules:
  0.0 44.5 jit_solution(7158777708612634292)
XLA Ops:
  0.0 3.0 %collective-permute-start = (bf16[128,1536]{1,0:T(8,128)(2,1)}, bf16[128,1536]{1,0:T(8,128)(2,1)S(1)}, u32[]{:S(2)}, u32[]{:S(2)}) collective-permute-start(bf16[128,1536]{1,0:T(8,128)(2,1)} %bitcast.5), channel_id=1, source_target_pairs={{0,1},{1,0},{2,3},{3,2},{4,5},{5,4},{6,7},{7,6},{8,9},{9,8},{10,11... | collective-permute-start | bytes 1179656 | tf_op jit(solution)/shard_map/ppermute | solution.py:360
  3.6 0.8 %pad_maximum_fusion = f32[4608]{0:T(1024)S(1)} fusion(f32[768]{0:T(1024)} %param.16, f32[768]{0:T(1024)} %param.15, f32[1536]{0:T(1024)} %param.12, f32[1536]{0:T(1024)} %param.11), kind=kLoop, calls=%fused_computation | loop fusion | flops 13824 | bytes 36864 | tf_op jit(solution)/shard_map/concatenate | solution.py:363
  4.4 0.0 copy-start.1
  4.4 1.0 %copy-done.1 = bf16[1,128,1536]{2,1,0:T(8,128)(2,1)S(1)} copy-done((bf16[1,128,1536]{2,1,0:T(8,128)(2,1)S(1)}, bf16[1,128,1536]{2,1,0:T(8,128)(2,1)}, u32[]{:S(2)}) %copy-start.1) | copy-done | bytes 393240
  5.4 0.8 %copy-done.11 = bf16[32,768]{1,0:T(8,128)(2,1)S(1)} copy-done((bf16[32,768]{1,0:T(8,128)(2,1)S(1)}, bf16[32,768]{1,0:T(8,128)(2,1)}, u32[]{:S(2)}) %copy-start.11) | copy-done | bytes 49176
  6.2 4.4 %first_block.1 = (bf16[176,768]{1,0:T(8,128)(2,1)S(1)}, f32[6,160,128]{2,1,0:T(8,128)S(1)}, bf16[2,1536,768]{2,1,0:T(8,128)(2,1)S(1)}) custom-call(s32[1]{0:T(128)S(6)} %copy.12.lengths_ref, bf16[1,128,1536]{2,1,0:T(8,128)(2,1)S(1)} %copy-done.1, f32[6,768]{1,0:T(8,128)S(1)} %reshape.6.vectors_ref, bf16[32,768]{1,0:T(8,128)(2,1)S(1)} %copy-done.11, ...), custom_call_target="tpu_custom_call" | custom-call | tf_op jit(solution)/shard_map/first_block/pallas_call | solution.py:338
  10.6 0.1 collective-permute-start.1
  10.7 1.9 %collective-permute-done.rows_ref = bf16[128,1536]{1,0:T(8,128)(2,1)S(1)} collective-permute-done((bf16[128,1536]{1,0:T(8,128)(2,1)}, bf16[128,1536]{1,0:T(8,128)(2,1)S(1)}, u32[]{:S(2)}, u32[]{:S(2)}) %collective-permute-start) | collective-permute-done | bytes 393248 | tf_op jit(solution)/shard_map/ppermute | solution.py:360
  12.5 3.0 %last_block.1 = (bf16[128,768]{1,0:T(8,128)(2,1)}, bf16[16,768]{1,0:T(8,128)(2,1)S(1)}, f32[6,128,128]{2,1,0:T(8,128)S(1)}, f32[6,128,128]{2,1,0:T(8,128)S(1)}, f32[32,1,1664]{2,1,0:T(1,128)}) custom-call(s32[1]{0:T(128)S(6)} %copy.12.lengths_ref, bf16[128,1536]{1,0:T(8,128)(2,1)S(1)} %collective-permute-done.rows_ref, f32[6,768]{1,0:T(8,128)S(1)} %reshape.6.vectors_ref, ...), custom_call_target="tpu_custom_call" | custom-call | tf_op jit(solution)/shard_map/last_block/pallas_call | solution.py:338
  15.5 0.7 %copy-done.3 = f32[6,128,128]{2,1,0:T(8,128)} copy-done((f32[6,128,128]{2,1,0:T(8,128)}, f32[6,128,128]{2,1,0:T(8,128)S(1)}, u32[]{:S(2)}) %copy-start.3) | copy-done | bytes 393240
  16.2 0.8 %copy-done.5 = f32[6,128,128]{2,1,0:T(8,128)} copy-done((f32[6,128,128]{2,1,0:T(8,128)}, f32[6,128,128]{2,1,0:T(8,128)S(1)}, u32[]{:S(2)}) %copy-start.5) | copy-done | bytes 393240
  17.0 1.6 %collective-permute-done.1.pack_ref = bf16[176,768]{1,0:T(8,128)(2,1)S(1)} collective-permute-done((bf16[176,768]{1,0:T(8,128)(2,1)S(1)}, bf16[176,768]{1,0:T(8,128)(2,1)S(1)}, u32[]{:S(2)}, u32[]{:S(2)}) %collective-permute-start.1) | collective-permute-done | bytes 270368 | tf_op jit(solution)/shard_map/ppermute | solution.py:360
  18.6 5.6 %all-to-all-start = ((f32[32,1,1664]{2,1,0:T(1,128)}), f32[32,1,1664]{2,1,0:T(1,128)S(1)}, u32[]{:S(2)}, u32[]{:S(2)}) async-start(f32[32,1,1664]{2,1,0:T(1,128)} %get-tuple-element.25), calls=%async_computation | async-start | bytes 425984 | tf_op jit(solution)/shard_map/all_to_all | solution.py:401
  24.2 1.8 %collective-permute-start.3 = (bf16[16,768]{1,0:T(8,128)(2,1)S(1)}, bf16[16,768]{1,0:T(8,128)(2,1)S(1)}, u32[]{:S(2)}, u32[]{:S(2)}) collective-permute-start(bf16[16,768]{1,0:T(8,128)(2,1)S(1)} %get-tuple-element.36), channel_id=1, source_target_pairs={{0,1},{1,0},{2,3},{3,2},{4,5},{5,4},{6,7},{7,6},{8,9},{9,8},{10,11... | collective-permute-start | bytes 73736 | tf_op jit(solution)/shard_map/ppermute | solution.py:360
  26.0 0.0 copy-done.9
  26.0 0.3 collective-permute-start.2
  26.3 1.7 %copy-done = bf16[768,1536]{1,0:T(8,128)(2,1)S(1)} copy-done((bf16[768,1536]{1,0:T(8,128)(2,1)S(1)}, bf16[768,1536]{1,0:T(8,128)(2,1)}, u32[]{:S(2)}) %copy-start) | copy-done | bytes 2359320
  27.9 1.0 %copy-done.10 = bf16[176,768]{1,0:T(8,128)(2,1)S(1)} copy-done((bf16[176,768]{1,0:T(8,128)(2,1)S(1)}, bf16[176,768]{1,0:T(8,128)(2,1)}, u32[]{:S(2)}) %copy-start.10) | copy-done | bytes 270360
  28.9 1.7 %peer_conv.1 = (f32[6,160,128]{2,1,0:T(8,128)S(1)}, f32[32,768]{1,0:T(8,128)S(1)}, f32[2,2,768]{2,1,0:T(2,128)S(1)}, bf16[2,768,768]{2,1,0:T(8,128)(2,1)S(1)}) custom-call(f32[6,768]{1,0:T(8,128)S(1)} %reshape.6.vectors_ref, bf16[768,1536]{1,0:T(8,128)(2,1)S(1)} %copy-done, bf16[176,768]{1,0:T(8,128)(2,1)S(1)} %copy-done.10), custom_call_target="tpu_custom_call" | custom-call | tf_op jit(solution)/shard_map/peer_conv/pallas_call | solution.py:338
  30.6 0.0 copy-start.7
  30.6 0.6 %copy-done.7 = f32[32,768]{1,0:T(8,128)} copy-done((f32[32,768]{1,0:T(8,128)}, f32[32,768]{1,0:T(8,128)S(1)}, u32[]{:S(2)}) %copy-start.7) | copy-done | bytes 98328
  31.2 0.0 collective-permute-done.3.near_ref
  31.2 2.9 %all-to-all-done = f32[32,1,1664]{2,1,0:T(1,128)S(1)} async-done(((f32[32,1,1664]{2,1,0:T(1,128)}), f32[32,1,1664]{2,1,0:T(1,128)S(1)}, u32[]{:S(2)}, u32[]{:S(2)}) %all-to-all-start) | async-done | bytes 213024 | tf_op jit(solution)/shard_map/all_to_all | solution.py:401
  34.1 1.0 %copy-done.6 = f32[6,128,128]{2,1,0:T(8,128)S(1)} copy-done((f32[6,128,128]{2,1,0:T(8,128)S(1)}, f32[6,128,128]{2,1,0:T(8,128)}, u32[]{:S(2)}) %copy-start.6) | copy-done | bytes 393240
  35.1 0.9 %copy-done.8 = f32[32,768]{1,0:T(8,128)S(1)} copy-done((f32[32,768]{1,0:T(8,128)S(1)}, f32[32,768]{1,0:T(8,128)}, u32[]{:S(2)}) %copy-start.8) | copy-done | bytes 98328
  36.0 0.9 %branch_sent.1 = bf16[128,768]{1,0:T(8,128)(2,1)S(1)} custom-call(f32[16,2,1,1664]{3,2,1,0:T(1,128)S(1)} %bitcast.3, f32[6,128,128]{2,1,0:T(8,128)S(1)} %copy-done.6, f32[6,160,128]{2,1,0:T(8,128)S(1)} %get-tuple-element.28.early_ref, bf16[16,768]{1,0:T(8,128)(2,1)S(1)} %collective-permute-done.3.near_ref, f32[32,768]{1,0:T(8,128)S(1)} %copy-done.8, ...), custom_call_target="tpu_custom_call" | custom-call | tf_op jit(solution)/shard_map/branch_sent/pallas_call | solution.py:338
  36.9 0.5 %collective-permute-start.4 = (bf16[128,768]{1,0:T(8,128)(2,1)S(1)}, bf16[128,768]{1,0:T(8,128)(2,1)S(1)}, u32[]{:S(2)}, u32[]{:S(2)}) collective-permute-start(bf16[128,768]{1,0:T(8,128)(2,1)S(1)} %branch_sent.1), channel_id=1, source_target_pairs={{0,1},{1,0},{2,3},{3,2},{4,5},{5,4},{6,7},{7,6},{8,9},{9,8},{10,11... | collective-permute-start | bytes 589832 | tf_op jit(solution)/shard_map/ppermute | solution.py:360
  37.5 0.0 collective-permute-done.2.late_ref
  37.5 1.0 %copy-done.4 = f32[6,128,128]{2,1,0:T(8,128)S(1)} copy-done((f32[6,128,128]{2,1,0:T(8,128)S(1)}, f32[6,128,128]{2,1,0:T(8,128)}, u32[]{:S(2)}) %copy-start.4) | copy-done | bytes 393240
  38.5 3.3 %branch_kept.1 = (bf16[128,1536]{1,0:T(8,128)(2,1)}, bf16[128,768]{1,0:T(8,128)(2,1)S(1)}) custom-call(f32[16,2,1,1664]{3,2,1,0:T(1,128)S(1)} %bitcast.4, f32[6,128,128]{2,1,0:T(8,128)S(1)} %copy-done.4, f32[6,160,128]{2,1,0:T(8,128)S(1)} %get-tuple-element.28.early_ref, bf16[128,768]{1,0:T(8,128)(2,1)} %collective-permute-done.2.late_ref, ...), custom_call_target="tpu_custom_call" | custom-call | tf_op jit(solution)/shard_map/branch_kept/pallas_call | solution.py:338
  41.8 2.0 %collective-permute-done.4.got_ref = bf16[128,768]{1,0:T(8,128)(2,1)S(1)} collective-permute-done((bf16[128,768]{1,0:T(8,128)(2,1)S(1)}, bf16[128,768]{1,0:T(8,128)(2,1)S(1)}, u32[]{:S(2)}, u32[]{:S(2)}) %collective-permute-start.4) | collective-permute-done | bytes 196640 | tf_op jit(solution)/shard_map/ppermute | solution.py:360
  43.8 0.7 %residual.1 = bf16[128,1536]{1,0:T(8,128)(2,1)} custom-call(bf16[128,1536]{1,0:T(8,128)(2,1)} %get-tuple-element.33.filled_ref, bf16[128,768]{1,0:T(8,128)(2,1)S(1)} %get-tuple-element.34.base_ref, bf16[128,768]{1,0:T(8,128)(2,1)S(1)} %collective-permute-done.4.got_ref), custom_call_target="tpu_custom_call", output_to_operand_aliasing={{}: (0, {})} | custom-call | tf_op jit(solution)/shard_map/residual/pallas_call | solution.py:338
  (12 shorter events, 0.0 us)
Async XLA Ops:
  0.0 12.5 %collective-permute-start = (bf16[128,1536]{1,0:T(8,128)(2,1)}, bf16[128,1536]{1,0:T(8,128)(2,1)S(1)}, u32[]{:S(2)}, u32[]{:S(2)}) collective-permute-start(bf16[128,1536]{1,0:T(8,128)(2,1)} %bitcast.5), channel_id=1, source_target_pairs={{0,1},{1,0},{2,3},{3,2},{4,5},{5,4},{6,7},{7,6},{8,9},{9,8},{10,11... | collective-permute-start | bytes 1179656 | tf_op jit(solution)/shard_map/ppermute | solution.py:360
  4.4 1.0 %copy-start.1 = (bf16[1,128,1536]{2,1,0:T(8,128)(2,1)S(1)}, bf16[1,128,1536]{2,1,0:T(8,128)(2,1)}, u32[]{:S(2)}) copy-start(bf16[1,128,1536]{2,1,0:T(8,128)(2,1)} %frames_ref.1) | copy-start | bytes 1179652
  5.4 0.8 %copy-start.11 = (bf16[32,768]{1,0:T(8,128)(2,1)S(1)}, bf16[32,768]{1,0:T(8,128)(2,1)}, u32[]{:S(2)}) copy-start(bf16[32,768]{1,0:T(8,128)(2,1)} %taps_ref.3) | copy-start | bytes 147460
  10.6 8.0 %collective-permute-start.1 = (bf16[176,768]{1,0:T(8,128)(2,1)S(1)}, bf16[176,768]{1,0:T(8,128)(2,1)S(1)}, u32[]{:S(2)}, u32[]{:S(2)}) collective-permute-start(bf16[176,768]{1,0:T(8,128)(2,1)S(1)} %get-tuple-element.24), channel_id=1, source_target_pairs={{0,1},{1,0},{2,3},{3,2},{4,5},{5,4},{6,7},{7,6},{8,9},{9,8},{10,11... | collective-permute-start | bytes 811016 | tf_op jit(solution)/shard_map/ppermute | solution.py:360
  15.5 0.7 %copy-start.3 = (f32[6,128,128]{2,1,0:T(8,128)}, f32[6,128,128]{2,1,0:T(8,128)S(1)}, u32[]{:S(2)}) copy-start(f32[6,128,128]{2,1,0:T(8,128)S(1)} %get-tuple-element.26.conv_ref) | copy-start | bytes 1179652
  16.2 0.8 %copy-start.5 = (f32[6,128,128]{2,1,0:T(8,128)}, f32[6,128,128]{2,1,0:T(8,128)S(1)}, u32[]{:S(2)}) copy-start(f32[6,128,128]{2,1,0:T(8,128)S(1)} %get-tuple-element.35.conv_ref) | copy-start | bytes 1179652
  17.0 20.5 %copy-start.2 = (bf16[1,128,1536]{2,1,0:T(8,128)(2,1)S(1)}, bf16[1,128,1536]{2,1,0:T(8,128)(2,1)}, u32[]{:S(2)}) copy-start(bf16[1,128,1536]{2,1,0:T(8,128)(2,1)} %frames_ref.1) | copy-start | bytes 1179652
  18.6 7.4 %copy-start.9 = (bf16[176,768]{1,0:T(8,128)(2,1)}, bf16[176,768]{1,0:T(8,128)(2,1)S(1)}, u32[]{:S(2)}) copy-start(bf16[176,768]{1,0:T(8,128)(2,1)S(1)} %collective-permute-done.1.pack_ref) | copy-start | bytes 811012
  18.6 15.5 %all-to-all-start = ((f32[32,1,1664]{2,1,0:T(1,128)}), f32[32,1,1664]{2,1,0:T(1,128)S(1)}, u32[]{:S(2)}, u32[]{:S(2)}) async-start(f32[32,1,1664]{2,1,0:T(1,128)} %get-tuple-element.25), calls=%async_computation | async-start | bytes 425984 | tf_op jit(solution)/shard_map/all_to_all | solution.py:401
  24.2 7.1 %collective-permute-start.3 = (bf16[16,768]{1,0:T(8,128)(2,1)S(1)}, bf16[16,768]{1,0:T(8,128)(2,1)S(1)}, u32[]{:S(2)}, u32[]{:S(2)}) collective-permute-start(bf16[16,768]{1,0:T(8,128)(2,1)S(1)} %get-tuple-element.36), channel_id=1, source_target_pairs={{0,1},{1,0},{2,3},{3,2},{4,5},{5,4},{6,7},{7,6},{8,9},{9,8},{10,11... | collective-permute-start | bytes 73736 | tf_op jit(solution)/shard_map/ppermute | solution.py:360
  26.0 11.5 %collective-permute-start.2 = (bf16[128,768]{1,0:T(8,128)(2,1)}, bf16[128,768]{1,0:T(8,128)(2,1)}, u32[]{:S(2)}, u32[]{:S(2)}) collective-permute-start(bf16[128,768]{1,0:T(8,128)(2,1)} %get-tuple-element.29), channel_id=1, source_target_pairs={{0,1},{1,0},{2,3},{3,2},{4,5},{5,4},{6,7},{7,6},{8,9},{9,8},{10,11... | collective-permute-start | bytes 589832 | tf_op jit(solution)/shard_map/ppermute | solution.py:360
  26.3 1.7 %copy-start = (bf16[768,1536]{1,0:T(8,128)(2,1)S(1)}, bf16[768,1536]{1,0:T(8,128)(2,1)}, u32[]{:S(2)}) copy-start(bf16[768,1536]{1,0:T(8,128)(2,1)} %weight_ref.3) | copy-start | bytes 7077892
  27.9 1.0 %copy-start.10 = (bf16[176,768]{1,0:T(8,128)(2,1)S(1)}, bf16[176,768]{1,0:T(8,128)(2,1)}, u32[]{:S(2)}) copy-start(bf16[176,768]{1,0:T(8,128)(2,1)} %copy-done.9) | copy-start | bytes 811012
  30.6 0.6 %copy-start.7 = (f32[32,768]{1,0:T(8,128)}, f32[32,768]{1,0:T(8,128)S(1)}, u32[]{:S(2)}) copy-start(f32[32,768]{1,0:T(8,128)S(1)} %get-tuple-element.30.taps_ref) | copy-start | bytes 294916
  34.1 1.0 %copy-start.6 = (f32[6,128,128]{2,1,0:T(8,128)S(1)}, f32[6,128,128]{2,1,0:T(8,128)}, u32[]{:S(2)}) copy-start(f32[6,128,128]{2,1,0:T(8,128)} %copy-done.5) | copy-start | bytes 1179652
  35.1 0.9 %copy-start.8 = (f32[32,768]{1,0:T(8,128)S(1)}, f32[32,768]{1,0:T(8,128)}, u32[]{:S(2)}) copy-start(f32[32,768]{1,0:T(8,128)} %copy-done.7) | copy-start | bytes 294916
  36.9 6.9 %collective-permute-start.4 = (bf16[128,768]{1,0:T(8,128)(2,1)S(1)}, bf16[128,768]{1,0:T(8,128)(2,1)S(1)}, u32[]{:S(2)}, u32[]{:S(2)}) collective-permute-start(bf16[128,768]{1,0:T(8,128)(2,1)S(1)} %branch_sent.1), channel_id=1, source_target_pairs={{0,1},{1,0},{2,3},{3,2},{4,5},{5,4},{6,7},{7,6},{8,9},{9,8},{10,11... | collective-permute-start | bytes 589832 | tf_op jit(solution)/shard_map/ppermute | solution.py:360
  37.5 1.0 %copy-start.4 = (f32[6,128,128]{2,1,0:T(8,128)S(1)}, f32[6,128,128]{2,1,0:T(8,128)}, u32[]{:S(2)}) copy-start(f32[6,128,128]{2,1,0:T(8,128)} %copy-done.3) | copy-start | bytes 1179652

commit v4 on v3

v4 whole, which is shorter than its diff:
```python
import functools

import jax
import jax.numpy as jnp
from jax import lax
from jax.experimental import pallas as pl
from jax.experimental.pallas import tpu as pltpu
from jax.sharding import PartitionSpec as P

KERNEL = 32
LANES = 128
WIDE = 256
HALO = 16
EDGE = 8
KEPT, SENT, HALF, OTHER, REST, BLOCKS = 0, 1, 2, 3, 4, 72
EXTRA = 48
F32 = jnp.float32
BF16 = jnp.bfloat16

VMEM = pl.BlockSpec(memory_space=pltpu.VMEM)
SMEM = pl.BlockSpec(memory_space=pltpu.SMEM)
HBM = pl.BlockSpec(memory_space=pltpu.HBM)


def layer_norm(rows, gain, bias):
    values = rows.astype(F32)
    center = jnp.mean(values, axis=-1, keepdims=True)
    values = values - center
    spread = jnp.mean(values * values, axis=-1, keepdims=True)
    return (values * lax.rsqrt(spread + 1e-05) * gain + bias).astype(BF16)


def swish(z):
    return z * jax.nn.sigmoid(z)


def cuts(width, most):
    return [slice(at, at + most) for at in range(0, width, most)]


def valid_rows(first, rows, length):
    index = first + lax.broadcasted_iota(jnp.int32, (rows, 1), 0)
    return index < length


def glu_of(normed, weight_ref, cut, keep):
    value = jnp.dot(normed, weight_ref[0, :, cut], preferred_element_type=F32)
    gate = jnp.dot(normed, weight_ref[1, :, cut], preferred_element_type=F32)
    glu = (value * jax.nn.sigmoid(gate)).astype(BF16)
    return jnp.where(keep, glu.astype(F32), 0.0)


def three_parts(vector):
    parts = []
    for _ in range(3):
        part = vector.astype(BF16).astype(F32)
        parts.append(part)
        vector = vector - part
    return parts


def affine(vectors_ref):
    rows = [vectors_ref[at : at + 1, :] for at in range(vectors_ref.shape[0] - 2)]
    half = len(rows) // 2
    return jnp.concatenate(rows[:half], axis=1), jnp.concatenate(rows[half:], axis=1)


def clear_ends(edge_ref):
    tiles, total, _ = edge_ref.shape
    zeros = jnp.zeros((EDGE, LANES), F32)
    for tile in range(tiles):
        edge_ref[tile, 0:EDGE, :] = zeros
        edge_ref[tile, total - EDGE : total, :] = zeros


def taps_at(taps_ref, offset, tile):
    cut = slice(tile * LANES, (tile + 1) * LANES)
    taps = {}
    for step in range(5):
        tap = 8 * step + offset - 1
        if 0 <= tap < KERNEL:
            taps[step] = jnp.broadcast_to(taps_ref[tap : tap + 1, cut], (8, LANES))
    return taps


def block_conv(block, tile, edge_ref, taps_ref):
    rows = block.shape[0]
    edge_ref[tile, EDGE : EDGE + rows, :] = block
    count = (rows + 2 * HALO) // 8
    total = [None] * count
    for offset in range(8):
        taps = taps_at(taps_ref, offset, tile)
        for at in range(count + 4):
            start = 8 * at + offset - 2 * HALO
            if start <= -8 or start >= rows:
                continue
            values = edge_ref[tile, EDGE + start : EDGE + start + 8, :]
            for step, tap in taps.items():
                if 0 <= at - step < count:
                    term = values * tap
                    seen = total[at - step]
                    total[at - step] = term if seen is None else seen + term
    return total


def first_block_kernel(
    lengths_ref, frames_ref, vectors_ref, taps_ref, weight_ref,
    glu_ref, sums_ref, held_ref, store_ref,
    rows_ref, raw_ref, wide_taps_ref, edge_ref, base_ref, rows_sem, weight_sems, base_sem,
):
    rows = rows_ref.shape[0]
    chans = held_ref.shape[2]
    own = lax.axis_index("tensor")
    rows_copy = pltpu.make_async_copy(frames_ref.at[0], rows_ref, rows_sem)
    rows_copy.start()
    pieces = cuts(chans, WIDE)
    copies = []
    for at, cut in enumerate(pieces):
        for side in range(2):
            place = (side, pl.ds(cut.start, WIDE))
            copy = pltpu.make_async_copy(
                weight_ref.at[place], raw_ref.at[place], weight_sems.at[at, side]
            )
            copy.start()
            copies.append(copy)
    clear_ends(edge_ref)
    keep = valid_rows(own * rows, rows, lengths_ref[0])
    wide_taps_ref[...] = taps_ref[...].astype(F32)
    gain, bias = affine(vectors_ref)
    rows_copy.wait()
    normed = layer_norm(rows_ref[...], gain, bias)
    tiles = chans // LANES
    for shift, half in enumerate((own, 1 - own)):
        for tile in range(tiles):
            lanes = pl.ds(pl.multiple_of((half * tiles + tile) * LANES, LANES), LANES)
            base_ref[shift, tile] = rows_ref[:, lanes].astype(F32)
    base_copy = pltpu.make_async_copy(base_ref, store_ref.at[pl.ds(HALF, 2)], base_sem)
    base_copy.start()
    for at, cut in enumerate(pieces):
        for side in range(2):
            copies[2 * at + side].wait()
            held_ref[side, :, cut] = raw_ref[side, cut, :].T
        glu = glu_of(normed, held_ref, cut, keep)
        glu_ref[:, cut] = glu.astype(BF16)
        for tile in range(cut.start // LANES, cut.stop // LANES):
            seen = slice(tile * LANES - cut.start, (tile + 1) * LANES - cut.start)
            total = block_conv(glu[:, seen], tile, edge_ref, wide_taps_ref)
            for step, each in enumerate(total):
                sums_ref[tile, 8 * step : 8 * step + 8, :] = each
    base_copy.wait()


def last_block_kernel(
    lengths_ref, rows_ref, vectors_ref, taps_ref, weight_ref, first_sums_ref, _,
    late_ref, near_ref, spread_ref, store_ref,
    wide_taps_ref, edge_ref, sums_ref, glu_ref, stats_ref, glu_sems, conv_sems, stats_sem,
):
    rows, chans = glu_ref.shape
    tiles = chans // LANES
    own = lax.axis_index("tensor")
    peer = 1 - own
    length = lengths_ref[0]
    count = length.astype(F32)
    keep = valid_rows(peer * rows, rows, length)
    own_valid, peer_valid = (valid_rows(at * rows, rows, length).astype(F32) for at in (own, peer))
    clear_ends(edge_ref)
    taps = taps_ref[...]
    wide_taps_ref[...] = taps.astype(F32)
    near_ref[HALO : HALO + KERNEL, :] = taps
    last = vectors_ref.shape[0] - 2
    extra = three_parts(vectors_ref[last : last + 1, :])
    extra += three_parts(vectors_ref[last + 1 : last + 2, :])
    extra.append(jnp.zeros((EXTRA - KERNEL - len(extra), chans), F32))
    near_ref[HALO + KERNEL :, :] = jnp.concatenate(extra).astype(BF16)
    reach = rows + 2 * HALO
    own_at = pl.multiple_of(own * rows, rows)
    peer_at = pl.multiple_of(peer * rows, rows)
    for tile in range(tiles):
        sums_ref[tile, pl.ds(peer_at, reach), :] = jnp.zeros((reach, LANES), F32)
        sums_ref[tile, pl.ds(own_at, reach), :] = first_sums_ref[tile]
    normed = layer_norm(rows_ref[...], *affine(vectors_ref))
    copies = []
    for piece, cut in enumerate(cuts(chans, WIDE)):
        glu = glu_of(normed, weight_ref, cut, keep)
        glu_ref[:, cut] = glu.astype(BF16)
        lanes = pl.ds(cut.start, WIDE)
        copies.append(
            pltpu.make_async_copy(glu_ref.at[:, lanes], late_ref.at[:, lanes], glu_sems.at[piece])
        )
        copies[-1].start()
        for tile in range(cut.start // LANES, cut.stop // LANES):
            seen = slice(tile * LANES - cut.start, (tile + 1) * LANES - cut.start)
            for step, each in enumerate(block_conv(glu[:, seen], tile, edge_ref, wide_taps_ref)):
                at = pl.ds(peer_at + 8 * step, 8)
                sums_ref[tile, at, :] = sums_ref[tile, at, :] + each
            own_rows, peer_rows = (pl.ds(at + HALO, rows) for at in (own_at, peer_at))
            for block, place in ((KEPT, own_rows), (SENT, peer_rows)):
                copies.append(
                    pltpu.make_async_copy(
                        sums_ref.at[tile, place], store_ref.at[block, tile], conv_sems.at[tile, block]
                    )
                )
                copies[-1].start()
            kept = sums_ref[tile, own_rows, :]
            sent = sums_ref[tile, peer_rows, :]
            mean = jnp.sum(kept * own_valid, axis=0, keepdims=True)
            mean += jnp.sum(sent * peer_valid, axis=0, keepdims=True)
            mean = mean / count
            high = mean.astype(BF16)
            low = (mean - high.astype(F32)).astype(BF16)
            mean = high.astype(F32) + low.astype(F32)
            off = (kept - mean) * own_valid
            squares = jnp.sum(off * off, axis=0, keepdims=True)
            off = (sent - mean) * peer_valid
            squares += jnp.sum(off * off, axis=0, keepdims=True)
            put_sums(stats_ref, tile, chans, high, low, squares.astype(BF16))
    near = pl.multiple_of(own * (rows - HALO), HALO)
    near_ref[0:HALO, :] = glu_ref[pl.ds(near, HALO), :]
    high = jnp.full((1, LANES), count, F32).astype(BF16)
    low = (jnp.full((1, LANES), count, F32) - high.astype(F32)).astype(BF16)
    stats_ref[0, :, chans + chans // 2 :] = jnp.concatenate([high, low])
    stats = stats_ref[0]
    for at in range(1, stats_ref.shape[0]):
        stats_ref[at] = stats
    copies.append(pltpu.make_async_copy(stats_ref, spread_ref, stats_sem))
    copies[-1].start()
    for copy in copies:
        copy.wait()


def put_sums(spread_ref, tile, chans, high, low, squares):
    lanes = slice(tile * LANES, (tile + 1) * LANES)
    spread_ref[0, :, lanes] = jnp.concatenate([high, low])
    half = chans // 2
    row, at = divmod(tile * LANES, half)
    spread_ref[0, row : row + 1, chans + at : chans + at + LANES] = squares


def turn_kernel(weight_ref, held_ref):
    parts, chans, _ = held_ref.shape
    for place in range(parts):
        for cut in cuts(chans, WIDE):
            at = place * chans
            held_ref[place, cut, :] = weight_ref[:, at + cut.start : at + cut.stop].T


def peer_conv_kernel(
    vectors_ref, near_ref, early_ref, given_ref,
    sent_ref, norms_ref, store_ref,
    edge_ref, wide_taps_ref, rest_ref, part_ref, rest_sem, conv_sem,
):
    rows, chans = early_ref.shape
    own = lax.axis_index("tensor")
    conv_copy = pltpu.make_async_copy(given_ref.at[SENT], sent_ref.at[0], conv_sem)
    conv_copy.start()
    clear_ends(edge_ref)
    taps = near_ref[HALO : HALO + KERNEL, :].astype(F32)
    wide_taps_ref[...] = taps
    extra = near_ref[HALO + KERNEL :, :].astype(F32)
    last = vectors_ref.shape[0] - 2
    norms_ref[0:2, :] = vectors_ref[last:, :]
    norms_ref[2:3, :] = extra[0:1] + (extra[1:2] + extra[2:3])
    norms_ref[3:4, :] = extra[3:4] + (extra[4:5] + extra[5:6])
    norms = norms_ref[...]
    target = pl.multiple_of(jnp.where(own == 0, 0, rows - HALO), HALO)
    source = pl.multiple_of(jnp.where(own == 0, 0, 2 * HALO), HALO)
    eighths = HALO // 8
    for tile in range(chans // LANES):
        lanes = slice(tile * LANES, (tile + 1) * LANES)
        rest_ref[tile, 0:KERNEL, :] = taps[:, lanes]
        rest_ref[tile, KERNEL : KERNEL + 4, :] = norms[:, lanes]
        part_ref[tile] = jnp.zeros((3 * HALO, LANES), F32)
        part_ref[tile, pl.ds(source, HALO), :] = near_ref[0:HALO, lanes].astype(F32)
        total = block_conv(early_ref[:, lanes].astype(F32), tile, edge_ref, wide_taps_ref)
        for at in range(eighths):
            start = KERNEL + 8 + 8 * at
            rest_ref[tile, start : start + 8, :] = jnp.where(own == 0, total[at], total[at - eighths])
        for step in range(rows // 8):
            sent_ref[1, tile, 8 * step : 8 * step + 8, :] = total[step + eighths]
        total = [sent_ref[1, tile, pl.ds(target + 8 * at, 8), :] for at in range(eighths)]
        for tap in range(KERNEL):
            weight = jnp.broadcast_to(wide_taps_ref[tap : tap + 1, lanes], (8, LANES))
            for at in range(eighths):
                start = 8 * at + tap + 1
                total[at] += part_ref[tile, start : start + 8, :] * weight
        for at in range(eighths):
            sent_ref[1, tile, pl.ds(target + 8 * at, 8), :] = total[at]
    rest_copy = pltpu.make_async_copy(rest_ref, store_ref.at[REST], rest_sem)
    rest_copy.start()
    conv_copy.wait()
    rest_copy.wait()


def scales(stats_ref, norms):
    chans = norms.shape[1]
    half = chans // 2
    own = lax.axis_index("tensor")
    found = []
    for shift, place in enumerate((own, 1 - own)):
        seen = stats_ref[:, pl.ds(place, 1), :, :].astype(F32)
        both = seen[:, :, 0:1, :] + seen[:, :, 1:2, :]
        means, counts = both[..., :chans], both[..., chans + half : chans + half + 1]
        squares = jnp.concatenate([seen[:, :, at : at + 1, chans : chans + half] for at in range(2)], axis=-1)
        count = jnp.sum(counts, axis=0)[0]
        mean = jnp.sum(means * counts, axis=0)[0] / count
        off = means - mean
        var = jnp.sum(squares + counts * off * off, axis=0)[0] / count
        scale = lax.rsqrt(var + 1e-05) * norms[2 * shift : 2 * shift + 1]
        found.append((mean, scale, norms[2 * shift + 1 : 2 * shift + 2]))
    return found


def branch_rows(found, conv_of, weight_ref):
    own = lax.axis_index("tensor")
    total = None
    for shift, (mean, scale, bias) in reversed(list(enumerate(found))):
        acts = []
        for tile in range(mean.shape[1] // LANES):
            lanes = slice(tile * LANES, (tile + 1) * LANES)
            z = (conv_of(shift, tile) - mean[:, lanes]) * scale[:, lanes] + bias[:, lanes]
            acts.append(swish(z).astype(BF16))
        place = own if shift == 0 else 1 - own
        term = jnp.dot(jnp.concatenate(acts, axis=1), weight_ref[place], preferred_element_type=F32)
        total = term if total is None else total + term
    return total


def sent_kernel(stats_ref, conv_ref, norms_ref, weight_ref, out_ref):
    found = scales(stats_ref, norms_ref[...])
    branch = branch_rows(found, lambda shift, tile: conv_ref[shift, tile], weight_ref)
    out_ref[...] = branch.astype(BF16)


def columns(ref, place, cols):
    return ref.at[:, pl.ds(pl.multiple_of(place * cols, LANES), cols)]


def kept_kernel(
    stats_ref, late_ref, weight_ref, store_ref,
    mine_ref, base_ref, rest_ref, edge_ref, wide_taps_ref, conv_ref, sums_ref, glu_ref, half_ref, sems,
):
    own = lax.axis_index("tensor")
    rows, _ = mine_ref.shape
    tiles = conv_ref.shape[0]
    copies = [
        (store_ref.at[REST], rest_ref),
        (late_ref, glu_ref),
        (store_ref.at[KEPT], conv_ref),
        (store_ref.at[HALF], half_ref),
        (store_ref.at[OTHER], base_ref),
    ]
    copies = [pltpu.make_async_copy(*pair, sems.at[at]) for at, pair in enumerate(copies)]
    for copy in copies:
        copy.start()
    clear_ends(edge_ref)
    target = pl.multiple_of(jnp.where(own == 0, rows - HALO, 0), HALO)
    copies[0].wait()
    copies[1].wait()
    for tile in range(tiles):
        lanes = slice(tile * LANES, (tile + 1) * LANES)
        wide_taps_ref[:, lanes] = rest_ref[tile, 0:KERNEL, :]
        total = block_conv(glu_ref[:, lanes].astype(F32), tile, edge_ref, wide_taps_ref)
        for step in range(rows // 8):
            sums_ref[tile, 8 * step : 8 * step + 8, :] = total[step + HALO // 8]
        for at in range(HALO // 8):
            place, start = pl.ds(target + 8 * at, 8), KERNEL + 8 + 8 * at
            sums_ref[tile, place, :] = sums_ref[tile, place, :] + rest_ref[tile, start : start + 8, :]
    norms = [rest_ref[tile, KERNEL : KERNEL + 4, :] for tile in range(tiles)]
    found = scales(stats_ref, jnp.concatenate(norms, axis=1))
    copies[2].wait()
    branch = branch_rows(found, lambda shift, tile: (sums_ref if shift else conv_ref)[tile], weight_ref)
    copies[3].wait()
    for tile in range(tiles):
        lanes = slice(tile * LANES, (tile + 1) * LANES)
        mine_ref[:, lanes] = (half_ref[tile] + branch[:, lanes]).astype(BF16)
    copies[4].wait()


def finish_kernel(mine_ref, base_ref, got_ref, out_ref, done_ref, sems):
    own = lax.axis_index("tensor")
    rows, cols = mine_ref.shape
    copies = [pltpu.make_async_copy(mine_ref, columns(out_ref, own, cols), sems.at[0])]
    copies[0].start()
    for tile in range(cols // LANES):
        lanes = slice(tile * LANES, (tile + 1) * LANES)
        done_ref[:, lanes] = (base_ref[tile] + got_ref[:, lanes].astype(F32)).astype(BF16)
    copies.append(pltpu.make_async_copy(done_ref, columns(out_ref, 1 - own, cols), sems.at[1]))
    copies[1].start()
    for copy in copies:
        copy.wait()


def shape(dims, kind):
    return jax.ShapeDtypeStruct(dims, kind)


def call(kernel, outs, in_specs, operands, out_specs=None, scratch=(), name=None, aliases=None, room=32):
    return pl.pallas_call(
        kernel,
        out_shape=tuple(outs),
        in_specs=list(in_specs),
        out_specs=tuple(out_specs or [VMEM] * len(outs)),
        scratch_shapes=list(scratch),
        input_output_aliases=aliases or {},
        compiler_params=pltpu.CompilerParams(vmem_limit_bytes=room * 1024 * 1024),
        name=name,
    )(*operands)


def two_parts(
    devices, frames_in, lengths, ln_gain, ln_bias, glu_weight, conv_kernel, bn_gain, bn_bias, out_weight
):
    _, span, width = frames_in.shape
    chans = glu_weight.shape[1]
    cols = out_weight.shape[0]
    tiles = chans // LANES
    pieces = chans // WIDE

    def swap(value):
        return lax.ppermute(value, "tensor", [(0, 1), (1, 0)])

    frames = swap(frames_in[0])
    vectors = jnp.concatenate([ln_gain, ln_bias, bn_gain, bn_bias]).reshape(-1, chans)
    edge = pltpu.VMEM((tiles, span + 2 * EDGE, LANES), F32)
    wide_taps = pltpu.VMEM((KERNEL, chans), F32)
    dma = pltpu.SemaphoreType.DMA
    reach = shape((tiles, span + 2 * HALO, LANES), F32)
    block = shape((tiles, span, LANES), F32)
    rest = pltpu.VMEM(block.shape, F32)
    store = shape((BLOCKS,) + block.shape, F32)
    early, first_sums, held, store_first = call(
        first_block_kernel,
        (shape((span, chans), BF16), reach, shape((2, width, chans), BF16), store),
        [SMEM, HBM, VMEM, VMEM, HBM],
        (lengths, frames_in, vectors, conv_kernel, glu_weight),
        out_specs=(VMEM, VMEM, VMEM, HBM),
        scratch=(
            pltpu.VMEM((span, width), BF16),
            pltpu.VMEM((2, chans, width), BF16),
            wide_taps,
            edge,
            pltpu.VMEM((2,) + block.shape, F32),
            dma,
            dma((pieces, 2)),
            dma,
        ),
        name="first_block",
        room=48,
    )
    early = swap(early)
    late, near, spread, store_second = call(
        last_block_kernel,
        (
            shape((span, chans), BF16),
            shape((HALO + EXTRA, chans), BF16),
            shape((devices, 2, chans + chans // 2 + LANES), BF16),
            store,
        ),
        [SMEM] + [VMEM] * 5 + [HBM],
        (lengths, frames, vectors, conv_kernel, held, first_sums, store_first),
        out_specs=(HBM, VMEM, HBM, HBM),
        scratch=(
            wide_taps,
            edge,
            pltpu.VMEM((tiles, 2 * span + 2 * HALO, LANES), F32),
            pltpu.VMEM((span, chans), BF16),
            pltpu.VMEM((devices, 2, chans + chans // 2 + LANES), BF16),
            dma((pieces,)),
            dma((tiles, 2)),
            dma,
        ),
        aliases={6: 3},
        name="last_block",
        room=40,
    )
    spread, early, out_weight = lax.optimization_barrier((spread, early, out_weight))
    stats = lax.all_to_all(spread, ("dp", "tensor"), split_axis=0, concat_axis=0, tiled=True)
    stats = stats.reshape((devices // 2, 2) + spread.shape[1:])
    near, late = swap(near), swap(late)
    (weight,) = call(turn_kernel, (shape((2, chans, cols), BF16),), [VMEM], (out_weight,), name="turn")
    sent_conv, norms, store_third = call(
        peer_conv_kernel,
        (shape((2,) + block.shape, F32), shape((4, chans), F32), store),
        [VMEM, VMEM, VMEM, HBM],
        (vectors, near, early, store_second),
        out_specs=(VMEM, VMEM, HBM),
        scratch=(edge, wide_taps, rest, pltpu.VMEM((tiles, 3 * HALO, LANES), F32), dma, dma),
        aliases={3: 2},
        name="peer_conv",
        room=40,
    )
    (sent,) = call(
        sent_kernel,
        (shape((span, cols), BF16),),
        [VMEM] * 4,
        (stats, sent_conv, norms, weight),
        name="branch_sent",
    )
    got = swap(sent)
    mine, base = call(
        kept_kernel,
        (shape((span, cols), BF16), block),
        [VMEM, HBM, VMEM, HBM],
        (stats, late, weight, store_third),
        scratch=(
            rest,
            edge,
            wide_taps,
            pltpu.VMEM(block.shape, F32),
            pltpu.VMEM(block.shape, F32),
            pltpu.VMEM((span, chans), BF16),
            pltpu.VMEM(block.shape, F32),
            dma((5,)),
        ),
        name="branch_kept",
    )
    (out,) = call(
        finish_kernel,
        (shape((span, width), BF16),),
        [VMEM] * 3,
        (mine, base, got),
        out_specs=(HBM,),
        scratch=(pltpu.VMEM((span, cols), BF16), dma((2,))),
        name="residual",
    )
    return out[None]


def contract_last(left, right):
    return lax.dot_general(
        left, right, (((1,), (1,)), ((), ())), preferred_element_type=F32
    )


def many_parts(
    devices, frames_in, lengths, ln_gain, ln_bias, glu_weight, conv_kernel, bn_gain, bn_bias, out_weight
):
    rows = frames_in[0]
    chans = glu_weight.shape[1]
    normed = layer_norm(rows, ln_gain, ln_bias)
    proj = contract_last(
        lax.all_gather(normed, "tensor", axis=0, tiled=True),
        glu_weight.reshape(2 * chans, rows.shape[1]),
    )
    valid = valid_rows(0, proj.shape[0], lengths[0])
    glu = (proj[:, :chans] * jax.nn.sigmoid(proj[:, chans:])).astype(BF16)
    glu = jnp.where(valid, glu, jnp.zeros_like(glu)).astype(F32)
    padded = jnp.pad(glu, ((15, KERNEL - 16), (0, 0)))
    taps = conv_kernel.astype(F32)
    conv = jnp.zeros_like(glu)
    for tap in range(KERNEL):
        conv = conv + padded[tap : tap + glu.shape[0]] * taps[tap]
    own = lengths[0].astype(F32)
    local = jnp.sum(jnp.where(valid, conv, 0.0), axis=0) / own
    squares = jnp.sum(jnp.where(valid, conv - local, 0.0) ** 2, axis=0)
    count = lax.psum(own, "dp")
    mean = lax.psum(local * own, "dp") / count
    var = lax.psum(squares + own * (local - mean) ** 2, "dp") / count
    z = (conv - mean) * (lax.rsqrt(var + 1e-05) * bn_gain) + bn_bias
    act = lax.all_gather(swish(z).astype(BF16), "tensor", axis=1, tiled=True)
    branch = contract_last(act, out_weight)
    branch = lax.all_to_all(branch, "tensor", split_axis=0, concat_axis=1, tiled=True)
    return (rows.astype(F32) + branch).astype(BF16)[None]


def solution(mesh):
    sizes = dict(mesh.shape)
    body = two_parts if sizes["tensor"] == 2 else many_parts
    body = functools.partial(body, sizes["tensor"] * sizes["dp"])
    return jax.shard_map(
        body,
        mesh=mesh,
        in_specs=(
            P("dp", "tensor", None),
            P("dp"),
            P(),
            P(),
            P(None, "tensor", None),
            P(None, "tensor"),
            P("tensor"),
            P("tensor"),
            P("tensor", None),
        ),
        out_specs=P("dp", "tensor", None),
        check_vma=False,
    )
```

time: 45.1 us -> 40.1 us (0.89)
  local copies, waits for them, and re-layouts: 9.43 us -> 3.46 us
  Pallas kernels: 14 us -> 14.6 us
    unnamed x24 -> x6, local copies, waits for them, and re-layouts: 9.43 us -> 3.45 us
    ppermute x5, waiting for transfers between devices: 5.51 us -> 8.16 us  [swap(): return lax.ppermute(value, 'tensor', [(0, 1), (1, 0)])]
    all_to_all x1, waiting for transfers between devices: 2.87 us -> 0.65 us  [two_parts(): lax.all_to_all(spread, ('dp', 'tensor'), split_axis=0, concat_axis=0, til...]
    pallas_call x6 -> x7, Pallas kernels: 14 us -> 14.6 us  [call(): pl.pallas_call(kernel, out_shape=tuple(outs), in_specs=list(in_specs), ou...]
  transfers between devices with their start and end apart: 6 -> 6, of which waited for: 4 -> 6; matrix products, arithmetic and copies ran while one was open for 2% -> 2% of each run, Pallas kernels for 30% -> 35%
where the time goes in v4:
time: 40.1 us; the launch traced here: 39.8 us
  Pallas kernels  14.6 us (36%)
  starting transfers between devices  11.4 us (28%)
  waiting for transfers between devices  8.82 us (22%)
  local copies, waits for them, and re-layouts  3.46 us (9%)
  other arithmetic  0.76 us (2%)
  between operations  0.73 us (2%)
    pallas_call x7, Pallas kernels, call(): pl.pallas_call(kernel, out_shape=tuple(outs), in_specs=list(in_specs), ou...  14.6 us
    ppermute x5, waiting for transfers between devices, swap(): return lax.ppermute(value, 'tensor', [(0, 1), (1, 0)])  8.16 us
    ppermute x5, starting transfers between devices, swap(): return lax.ppermute(value, 'tensor', [(0, 1), (1, 0)])  6.04 us
    all_to_all x1, starting transfers between devices, two_parts(): lax.all_to_all(spread, ('dp', 'tensor'), split_axis=0, concat_axis=0, til...  5.33 us
    unnamed x6, local copies, waits for them, and re-layouts  3.45 us
  transfers between devices with their start and end apart: 6, of which 6 were waited for; matrix products, arithmetic and copies ran while one was open for 2% of the time, Pallas kernels for 35%

profile of v4, /device:TPU:0, one launch (start us, length us, event | category | flops | bytes accessed | tf_op | source)
XLA Modules:
  0.0 39.8 jit_solution(12322100044925976722)
XLA Ops:
  0.0 3.0 %collective-permute-start = (bf16[128,1536]{1,0:T(8,128)(2,1)}, bf16[128,1536]{1,0:T(8,128)(2,1)S(1)}, u32[]{:S(2)}, u32[]{:S(2)}) collective-permute-start(bf16[128,1536]{1,0:T(8,128)(2,1)} %bitcast.5), channel_id=1, source_target_pairs={{0,1},{1,0},{2,3},{3,2},{4,5},{5,4},{6,7},{7,6},{8,9},{9,8},{10,11... | collective-permute-start | bytes 1179656 | tf_op jit(solution)/shard_map/ppermute | solution.py:420
  3.6 0.8 %pad_maximum_fusion = f32[4608]{0:T(1024)S(1)} fusion(f32[768]{0:T(1024)} %param.16, f32[768]{0:T(1024)} %param.15, f32[1536]{0:T(1024)} %param.12, f32[1536]{0:T(1024)} %param.11), kind=kLoop, calls=%fused_computation | loop fusion | flops 13824 | bytes 36864 | tf_op jit(solution)/shard_map/concatenate | solution.py:423
  4.4 0.0 copy-start.1
  4.4 1.0 %copy-done.1 = bf16[1,128,1536]{2,1,0:T(8,128)(2,1)S(1)} copy-done((bf16[1,128,1536]{2,1,0:T(8,128)(2,1)S(1)}, bf16[1,128,1536]{2,1,0:T(8,128)(2,1)}, u32[]{:S(2)}) %copy-start.1) | copy-done | bytes 393240
  5.4 0.0 copy-start.2
  5.4 0.8 %copy-done.2 = bf16[32,768]{1,0:T(8,128)(2,1)S(1)} copy-done((bf16[32,768]{1,0:T(8,128)(2,1)S(1)}, bf16[32,768]{1,0:T(8,128)(2,1)}, u32[]{:S(2)}) %copy-start.2) | copy-done | bytes 49176
  6.2 4.6 %first_block.1 = (bf16[128,768]{1,0:T(8,128)(2,1)S(1)}, f32[6,160,128]{2,1,0:T(8,128)S(1)}, bf16[2,1536,768]{2,1,0:T(8,128)(2,1)S(1)}, f32[72,6,128,128]{3,2,1,0:T(8,128)}) custom-call(s32[1]{0:T(128)S(6)} %copy.14.lengths_ref, bf16[1,128,1536]{2,1,0:T(8,128)(2,1)S(1)} %copy-done.1, f32[6,768]{1,0:T(8,128)S(1)} %reshape.6.vectors_ref, ...), custom_call_target="tpu_custom_call" | custom-call | tf_op jit(solution)/shard_map/first_block/pallas_call | solution.py:398
  10.8 0.1 collective-permute-start.1
  10.9 1.4 %collective-permute-done.rows_ref = bf16[128,1536]{1,0:T(8,128)(2,1)S(1)} collective-permute-done((bf16[128,1536]{1,0:T(8,128)(2,1)}, bf16[128,1536]{1,0:T(8,128)(2,1)S(1)}, u32[]{:S(2)}, u32[]{:S(2)}) %collective-permute-start) | collective-permute-done | bytes 393248 | tf_op jit(solution)/shard_map/ppermute | solution.py:420
  12.3 3.3 %last_block.1 = (bf16[128,768]{1,0:T(8,128)(2,1)}, bf16[64,768]{1,0:T(8,128)(2,1)S(1)}, bf16[32,2,1280]{2,1,0:T(2,128)(2,1)}, f32[72,6,128,128]{3,2,1,0:T(8,128)}) custom-call(s32[1]{0:T(128)S(6)} %copy.14.lengths_ref, bf16[128,1536]{1,0:T(8,128)(2,1)S(1)} %collective-permute-done.rows_ref, ...), custom_call_target="tpu_custom_call", output_to_operand_aliasing={{3}: (6, {})} | custom-call | tf_op jit(solution)/shard_map/last_block/pallas_call | solution.py:398
  15.6 1.7 %collective-permute-done.1.early_ref = bf16[128,768]{1,0:T(8,128)(2,1)S(1)} collective-permute-done((bf16[128,768]{1,0:T(8,128)(2,1)S(1)}, bf16[128,768]{1,0:T(8,128)(2,1)S(1)}, u32[]{:S(2)}, u32[]{:S(2)}) %collective-permute-start.1) | collective-permute-done | bytes 196640 | tf_op jit(solution)/shard_map/ppermute | solution.py:420
  17.2 5.3 %all-to-all-start = ((bf16[32,2,1280]{2,1,0:T(2,128)(2,1)}), bf16[32,2,1280]{2,1,0:T(2,128)(2,1)S(1)}, u32[]{:S(2)}, u32[]{:S(2)}) async-start(bf16[32,2,1280]{2,1,0:T(2,128)(2,1)} %get-tuple-element.26), calls=%async_computation | async-start | bytes 327680 | tf_op jit(solution)/shard_map/all_to_all | solution.py:477
  22.6 1.8 %collective-permute-start.3 = (bf16[64,768]{1,0:T(8,128)(2,1)S(1)}, bf16[64,768]{1,0:T(8,128)(2,1)S(1)}, u32[]{:S(2)}, u32[]{:S(2)}) collective-permute-start(bf16[64,768]{1,0:T(8,128)(2,1)S(1)} %get-tuple-element.29), channel_id=1, source_target_pairs={{0,1},{1,0},{2,3},{3,2},{4,5},{5,4},{6,7},{7,6},{8,9},{9,8},{10,11... | collective-permute-start | bytes 294920 | tf_op jit(solution)/shard_map/ppermute | solution.py:420
  24.4 0.3 collective-permute-start.2
  24.7 0.0 copy-start
  24.7 1.7 %copy-done = bf16[768,1536]{1,0:T(8,128)(2,1)S(1)} copy-done((bf16[768,1536]{1,0:T(8,128)(2,1)S(1)}, bf16[768,1536]{1,0:T(8,128)(2,1)}, u32[]{:S(2)}) %copy-start) | copy-done | bytes 2359320
  26.3 0.7 %turn.1.weight_ref = bf16[2,768,768]{2,1,0:T(8,128)(2,1)S(1)} custom-call(bf16[768,1536]{1,0:T(8,128)(2,1)S(1)} %copy-done), custom_call_target="tpu_custom_call" | custom-call | tf_op jit(solution)/shard_map/turn/pallas_call | solution.py:398
  27.0 2.3 %collective-permute-done.3.near_ref = bf16[64,768]{1,0:T(8,128)(2,1)S(1)} collective-permute-done((bf16[64,768]{1,0:T(8,128)(2,1)S(1)}, bf16[64,768]{1,0:T(8,128)(2,1)S(1)}, u32[]{:S(2)}, u32[]{:S(2)}) %collective-permute-start.3) | collective-permute-done | bytes 98336 | tf_op jit(solution)/shard_map/ppermute | solution.py:420
  29.3 1.8 %peer_conv.1 = (f32[2,6,128,128]{3,2,1,0:T(8,128)S(1)}, f32[4,768]{1,0:T(4,128)S(1)}, f32[72,6,128,128]{3,2,1,0:T(8,128)}) custom-call(f32[6,768]{1,0:T(8,128)S(1)} %reshape.6.vectors_ref, bf16[64,768]{1,0:T(8,128)(2,1)S(1)} %collective-permute-done.3.near_ref, ...), custom_call_target="tpu_custom_call", output_to_operand_aliasing={{2}: (3, {})} | custom-call | tf_op jit(solution)/shard_map/peer_conv/pallas_call | solution.py:398
  31.1 0.7 %all-to-all-done = bf16[32,2,1280]{2,1,0:T(2,128)(2,1)S(1)} async-done(((bf16[32,2,1280]{2,1,0:T(2,128)(2,1)}), bf16[32,2,1280]{2,1,0:T(2,128)(2,1)S(1)}, u32[]{:S(2)}, u32[]{:S(2)}) %all-to-all-start) | async-done | bytes 163872 | tf_op jit(solution)/shard_map/all_to_all | solution.py:477
  31.7 0.8 %branch_sent.1 = bf16[128,768]{1,0:T(8,128)(2,1)S(1)} custom-call(bf16[16,2,2,1280]{3,2,1,0:T(2,128)(2,1)S(1)} %bitcast.3, f32[2,6,128,128]{3,2,1,0:T(8,128)S(1)} %get-tuple-element.35.conv_ref, f32[4,768]{1,0:T(4,128)S(1)} %get-tuple-element.36.norms_ref, bf16[2,768,768]{2,1,0:T(8,128)(2,1)S(1)} %turn.1.weight_ref), custom_call_target="tpu_custom_call" | custom-call | tf_op jit(solution)/shard_map/branch_sent/pallas_call | solution.py:398
  32.5 0.9 %collective-permute-start.4 = (bf16[128,768]{1,0:T(8,128)(2,1)S(1)}, bf16[128,768]{1,0:T(8,128)(2,1)S(1)}, u32[]{:S(2)}, u32[]{:S(2)}) collective-permute-start(bf16[128,768]{1,0:T(8,128)(2,1)S(1)} %branch_sent.1), channel_id=1, source_target_pairs={{0,1},{1,0},{2,3},{3,2},{4,5},{5,4},{6,7},{7,6},{8,9},{9,8},{10,11... | collective-permute-start | bytes 589832 | tf_op jit(solution)/shard_map/ppermute | solution.py:420
  33.4 0.2 collective-permute-done.2.late_ref
  33.6 2.8 %branch_kept.1 = (bf16[128,768]{1,0:T(8,128)(2,1)S(1)}, f32[6,128,128]{2,1,0:T(8,128)S(1)}) custom-call(bf16[16,2,2,1280]{3,2,1,0:T(2,128)(2,1)S(1)} %bitcast.4, bf16[128,768]{1,0:T(8,128)(2,1)} %collective-permute-done.2.late_ref, bf16[2,768,768]{2,1,0:T(8,128)(2,1)S(1)} %turn.1.weight_ref, f32[72,6,128,128]{3,2,1,0:T(8,128)} %get-tuple-element.32.store_ref), custom_call_target="tpu_custom_call" | custom-call | tf_op jit(solution)/shard_map/branch_kept/pallas_call | solution.py:398
  36.4 2.6 %collective-permute-done.4.got_ref = bf16[128,768]{1,0:T(8,128)(2,1)S(1)} collective-permute-done((bf16[128,768]{1,0:T(8,128)(2,1)S(1)}, bf16[128,768]{1,0:T(8,128)(2,1)S(1)}, u32[]{:S(2)}, u32[]{:S(2)}) %collective-permute-start.4) | collective-permute-done | bytes 196640 | tf_op jit(solution)/shard_map/ppermute | solution.py:420
  39.0 0.8 %residual.1 = bf16[128,1536]{1,0:T(8,128)(2,1)} custom-call(bf16[128,768]{1,0:T(8,128)(2,1)S(1)} %get-tuple-element.33.mine_ref, f32[6,128,128]{2,1,0:T(8,128)S(1)} %get-tuple-element.34.base_ref, bf16[128,768]{1,0:T(8,128)(2,1)S(1)} %collective-permute-done.4.got_ref), custom_call_target="tpu_custom_call" | custom-call | tf_op jit(solution)/shard_map/residual/pallas_call | solution.py:398
  (1 shorter events, 0.0 us)
Async XLA Ops:
  0.0 12.3 %collective-permute-start = (bf16[128,1536]{1,0:T(8,128)(2,1)}, bf16[128,1536]{1,0:T(8,128)(2,1)S(1)}, u32[]{:S(2)}, u32[]{:S(2)}) collective-permute-start(bf16[128,1536]{1,0:T(8,128)(2,1)} %bitcast.5), channel_id=1, source_target_pairs={{0,1},{1,0},{2,3},{3,2},{4,5},{5,4},{6,7},{7,6},{8,9},{9,8},{10,11... | collective-permute-start | bytes 1179656 | tf_op jit(solution)/shard_map/ppermute | solution.py:420
  4.4 1.0 %copy-start.1 = (bf16[1,128,1536]{2,1,0:T(8,128)(2,1)S(1)}, bf16[1,128,1536]{2,1,0:T(8,128)(2,1)}, u32[]{:S(2)}) copy-start(bf16[1,128,1536]{2,1,0:T(8,128)(2,1)} %frames_ref.1) | copy-start | bytes 1179652
  5.4 0.8 %copy-start.2 = (bf16[32,768]{1,0:T(8,128)(2,1)S(1)}, bf16[32,768]{1,0:T(8,128)(2,1)}, u32[]{:S(2)}) copy-start(bf16[32,768]{1,0:T(8,128)(2,1)} %taps_ref.3) | copy-start | bytes 147460
  10.8 6.4 %collective-permute-start.1 = (bf16[128,768]{1,0:T(8,128)(2,1)S(1)}, bf16[128,768]{1,0:T(8,128)(2,1)S(1)}, u32[]{:S(2)}, u32[]{:S(2)}) collective-permute-start(bf16[128,768]{1,0:T(8,128)(2,1)S(1)} %get-tuple-element.25), channel_id=1, source_target_pairs={{0,1},{1,0},{2,3},{3,2},{4,5},{5,4},{6,7},{7,6},{8,9},{9,8},{10,11... | collective-permute-start | bytes 589832 | tf_op jit(solution)/shard_map/ppermute | solution.py:420
  17.2 14.5 %all-to-all-start = ((bf16[32,2,1280]{2,1,0:T(2,128)(2,1)}), bf16[32,2,1280]{2,1,0:T(2,128)(2,1)S(1)}, u32[]{:S(2)}, u32[]{:S(2)}) async-start(bf16[32,2,1280]{2,1,0:T(2,128)(2,1)} %get-tuple-element.26), calls=%async_computation | async-start | bytes 327680 | tf_op jit(solution)/shard_map/all_to_all | solution.py:477
  22.6 6.7 %collective-permute-start.3 = (bf16[64,768]{1,0:T(8,128)(2,1)S(1)}, bf16[64,768]{1,0:T(8,128)(2,1)S(1)}, u32[]{:S(2)}, u32[]{:S(2)}) collective-permute-start(bf16[64,768]{1,0:T(8,128)(2,1)S(1)} %get-tuple-element.29), channel_id=1, source_target_pairs={{0,1},{1,0},{2,3},{3,2},{4,5},{5,4},{6,7},{7,6},{8,9},{9,8},{10,11... | collective-permute-start | bytes 294920 | tf_op jit(solution)/shard_map/ppermute | solution.py:420
  24.4 9.2 %collective-permute-start.2 = (bf16[128,768]{1,0:T(8,128)(2,1)}, bf16[128,768]{1,0:T(8,128)(2,1)}, u32[]{:S(2)}, u32[]{:S(2)}) collective-permute-start(bf16[128,768]{1,0:T(8,128)(2,1)} %get-tuple-element.27), channel_id=1, source_target_pairs={{0,1},{1,0},{2,3},{3,2},{4,5},{5,4},{6,7},{7,6},{8,9},{9,8},{10,11... | collective-permute-start | bytes 589832 | tf_op jit(solution)/shard_map/ppermute | solution.py:420
  24.7 1.7 %copy-start = (bf16[768,1536]{1,0:T(8,128)(2,1)S(1)}, bf16[768,1536]{1,0:T(8,128)(2,1)}, u32[]{:S(2)}) copy-start(bf16[768,1536]{1,0:T(8,128)(2,1)} %weight_ref.2) | copy-start | bytes 7077892
  32.5 6.5 %collective-permute-start.4 = (bf16[128,768]{1,0:T(8,128)(2,1)S(1)}, bf16[128,768]{1,0:T(8,128)(2,1)S(1)}, u32[]{:S(2)}, u32[]{:S(2)}) collective-permute-start(bf16[128,768]{1,0:T(8,128)(2,1)S(1)} %branch_sent.1), channel_id=1, source_target_pairs={{0,1},{1,0},{2,3},{3,2},{4,5},{5,4},{6,7},{7,6},{8,9},{9,8},{10,11... | collective-permute-start | bytes 589832 | tf_op jit(solution)/shard_map/ppermute | solution.py:420

commit v5 on v4

--- a/solution.py
+++ b/solution.py
@@ -12,8 +12,8 @@
 WIDE = 256
 HALO = 16
 EDGE = 8
-KEPT, SENT, HALF, OTHER, REST, BLOCKS = 0, 1, 2, 3, 4, 72
-EXTRA = 48
+KEPT, SENT, HALF, OTHER, BLOCKS = 0, 1, 2, 3, 72
+EXTRA = 8
 F32 = jnp.float32
 BF16 = jnp.bfloat16
 
@@ -103,9 +103,14 @@
     return total
 
 
+def half_lanes(tile, tiles):
+    half, place = divmod(tile, tiles // 2)
+    return half, slice(place * LANES, (place + 1) * LANES)
+
+
 def first_block_kernel(
     lengths_ref, frames_ref, vectors_ref, taps_ref, weight_ref,
-    glu_ref, sums_ref, held_ref, store_ref,
+    soon_ref, later_ref, sums_ref, held_ref, pivot_ref, store_ref,
     rows_ref, raw_ref, wide_taps_ref, edge_ref, base_ref, rows_sem, weight_sems, base_sem,
 ):
     rows = rows_ref.shape[0]
@@ -141,81 +146,95 @@
             copies[2 * at + side].wait()
             held_ref[side, :, cut] = raw_ref[side, cut, :].T
         glu = glu_of(normed, held_ref, cut, keep)
-        glu_ref[:, cut] = glu.astype(BF16)
         for tile in range(cut.start // LANES, cut.stop // LANES):
             seen = slice(tile * LANES - cut.start, (tile + 1) * LANES - cut.start)
             total = block_conv(glu[:, seen], tile, edge_ref, wide_taps_ref)
             for step, each in enumerate(total):
                 sums_ref[tile, 8 * step : 8 * step + 8, :] = each
+            lanes = slice(tile * LANES, (tile + 1) * LANES)
+            conv = sums_ref[tile, HALO : HALO + rows, :]
+            pivot = jnp.sum(conv, axis=0, keepdims=True) * (1.0 / rows)
+            pivot = pivot.astype(BF16).astype(F32)
+            pivot_ref[:, lanes] = pivot
+            half, there = half_lanes(tile, tiles)
+            (soon_ref, later_ref)[half][:, there] = (conv - pivot).astype(BF16)
     base_copy.wait()
 
 
 def last_block_kernel(
-    lengths_ref, rows_ref, vectors_ref, taps_ref, weight_ref, first_sums_ref, _,
-    late_ref, near_ref, spread_ref, store_ref,
-    wide_taps_ref, edge_ref, sums_ref, glu_ref, stats_ref, glu_sems, conv_sems, stats_sem,
+    lengths_ref, rows_ref, vectors_ref, taps_ref, weight_ref, first_sums_ref, pivot_ref, later_ref, _,
+    late_ref, tail_ref, spread_ref, store_ref,
+    wide_taps_ref, edge_ref, conv_ref, mask_ref, peer_rows_ref, stats_ref, late_sems, conv_sems, stats_sem,
 ):
-    rows, chans = glu_ref.shape
+    rows, chans = peer_rows_ref.shape
     tiles = chans // LANES
     own = lax.axis_index("tensor")
     peer = 1 - own
     length = lengths_ref[0]
     count = length.astype(F32)
     keep = valid_rows(peer * rows, rows, length)
-    own_valid, peer_valid = (valid_rows(at * rows, rows, length).astype(F32) for at in (own, peer))
+    for at, place in enumerate((own, peer)):
+        valid = valid_rows(place * rows, rows, length).astype(F32)
+        mask_ref[at] = jnp.broadcast_to(valid, (rows, LANES))
+    first_one = (own == 0).astype(F32)
+    last_one = 1.0 - first_one
     clear_ends(edge_ref)
-    taps = taps_ref[...]
-    wide_taps_ref[...] = taps.astype(F32)
-    near_ref[HALO : HALO + KERNEL, :] = taps
+    wide_taps_ref[...] = taps_ref[...].astype(F32)
     last = vectors_ref.shape[0] - 2
     extra = three_parts(vectors_ref[last : last + 1, :])
     extra += three_parts(vectors_ref[last + 1 : last + 2, :])
-    extra.append(jnp.zeros((EXTRA - KERNEL - len(extra), chans), F32))
-    near_ref[HALO + KERNEL :, :] = jnp.concatenate(extra).astype(BF16)
-    reach = rows + 2 * HALO
-    own_at = pl.multiple_of(own * rows, rows)
-    peer_at = pl.multiple_of(peer * rows, rows)
-    for tile in range(tiles):
-        sums_ref[tile, pl.ds(peer_at, reach), :] = jnp.zeros((reach, LANES), F32)
-        sums_ref[tile, pl.ds(own_at, reach), :] = first_sums_ref[tile]
+    extra.append(pivot_ref[...])
+    extra.append(jnp.zeros((EXTRA - len(extra), chans), F32))
+    extra = jnp.concatenate(extra)
+    wide = chans // 2
+    tail_ref[0:rows, :] = later_ref[...]
+    tail_ref[rows + 2 * HALO :, :] = jnp.concatenate([extra[:, :wide], extra[:, wide:]]).astype(BF16)
     normed = layer_norm(rows_ref[...], *affine(vectors_ref))
     copies = []
-    for piece, cut in enumerate(cuts(chans, WIDE)):
+    for cut in cuts(chans, WIDE):
         glu = glu_of(normed, weight_ref, cut, keep)
-        glu_ref[:, cut] = glu.astype(BF16)
-        lanes = pl.ds(cut.start, WIDE)
-        copies.append(
-            pltpu.make_async_copy(glu_ref.at[:, lanes], late_ref.at[:, lanes], glu_sems.at[piece])
-        )
-        copies[-1].start()
         for tile in range(cut.start // LANES, cut.stop // LANES):
             seen = slice(tile * LANES - cut.start, (tile + 1) * LANES - cut.start)
-            for step, each in enumerate(block_conv(glu[:, seen], tile, edge_ref, wide_taps_ref)):
-                at = pl.ds(peer_at + 8 * step, 8)
-                sums_ref[tile, at, :] = sums_ref[tile, at, :] + each
-            own_rows, peer_rows = (pl.ds(at + HALO, rows) for at in (own_at, peer_at))
-            for block, place in ((KEPT, own_rows), (SENT, peer_rows)):
+            lanes = slice(tile * LANES, (tile + 1) * LANES)
+            total = block_conv(glu[:, seen], tile, edge_ref, wide_taps_ref)
+            first = [first_sums_ref[tile, 8 * at : 8 * at + 8, :] for at in range(len(total))]
+            kept, sent = first[2:-2], total[2:-2]
+            for at in range(2):
+                kept[at] += total[at - 2] * last_one
+                kept[at - 2] += total[at] * first_one
+                sent[at] += first[at - 2] * first_one
+                sent[at - 2] += first[at] * last_one
+            near = jnp.concatenate(kept[:2]) * last_one + jnp.concatenate(kept[-2:]) * first_one
+            kept, sent = jnp.concatenate(kept), jnp.concatenate(sent)
+            for block, conv in ((KEPT, kept), (SENT, sent)):
+                conv_ref[block, tile] = conv
                 copies.append(
                     pltpu.make_async_copy(
-                        sums_ref.at[tile, place], store_ref.at[block, tile], conv_sems.at[tile, block]
+                        conv_ref.at[block, tile], store_ref.at[block, tile], conv_sems.at[tile, block]
                     )
                 )
                 copies[-1].start()
-            kept = sums_ref[tile, own_rows, :]
-            sent = sums_ref[tile, peer_rows, :]
-            mean = jnp.sum(kept * own_valid, axis=0, keepdims=True)
-            mean += jnp.sum(sent * peer_valid, axis=0, keepdims=True)
+            pivot = pivot_ref[:, lanes]
+            near = (near - pivot).astype(BF16)
+            half, there = half_lanes(tile, tiles)
+            tail_ref[rows + half * HALO : rows + (half + 1) * HALO, there] = near
+            peer_rows_ref[:, lanes] = (sent - pivot).astype(BF16)
+            copies.append(
+                pltpu.make_async_copy(
+                    peer_rows_ref.at[:, pl.ds(lanes.start, LANES)],
+                    late_ref.at[:, pl.ds(lanes.start, LANES)],
+                    late_sems.at[tile],
+                )
+            )
+            copies[-1].start()
+            mean = jnp.sum(kept * mask_ref[0] + sent * mask_ref[1], axis=0, keepdims=True)
             mean = mean / count
             high = mean.astype(BF16)
             low = (mean - high.astype(F32)).astype(BF16)
             mean = high.astype(F32) + low.astype(F32)
-            off = (kept - mean) * own_valid
-            squares = jnp.sum(off * off, axis=0, keepdims=True)
-            off = (sent - mean) * peer_valid
-            squares += jnp.sum(off * off, axis=0, keepdims=True)
+            kept, sent = (kept - mean) * mask_ref[0], (sent - mean) * mask_ref[1]
+            squares = jnp.sum(kept * kept + sent * sent, axis=0, keepdims=True)
             put_sums(stats_ref, tile, chans, high, low, squares.astype(BF16))
-    near = pl.multiple_of(own * (rows - HALO), HALO)
-    near_ref[0:HALO, :] = glu_ref[pl.ds(near, HALO), :]
     high = jnp.full((1, LANES), count, F32).astype(BF16)
     low = (jnp.full((1, LANES), count, F32) - high.astype(F32)).astype(BF16)
     stats_ref[0, :, chans + chans // 2 :] = jnp.concatenate([high, low])
@@ -236,63 +255,30 @@
     spread_ref[0, row : row + 1, chans + at : chans + at + LANES] = squares
 
 
-def turn_kernel(weight_ref, held_ref):
+def turn_kernel(weight_ref, vectors_ref, store_ref, held_ref, conv_ref, norms_ref, sem):
     parts, chans, _ = held_ref.shape
+    copy = pltpu.make_async_copy(store_ref.at[SENT], conv_ref, sem)
+    copy.start()
+    norms_ref[...] = vectors_ref[vectors_ref.shape[0] - 2 :, :]
     for place in range(parts):
         for cut in cuts(chans, WIDE):
             at = place * chans
             held_ref[place, cut, :] = weight_ref[:, at + cut.start : at + cut.stop].T
-
-
-def peer_conv_kernel(
-    vectors_ref, near_ref, early_ref, given_ref,
-    sent_ref, norms_ref, store_ref,
-    edge_ref, wide_taps_ref, rest_ref, part_ref, rest_sem, conv_sem,
-):
-    rows, chans = early_ref.shape
-    own = lax.axis_index("tensor")
-    conv_copy = pltpu.make_async_copy(given_ref.at[SENT], sent_ref.at[0], conv_sem)
-    conv_copy.start()
-    clear_ends(edge_ref)
-    taps = near_ref[HALO : HALO + KERNEL, :].astype(F32)
-    wide_taps_ref[...] = taps
-    extra = near_ref[HALO + KERNEL :, :].astype(F32)
-    last = vectors_ref.shape[0] - 2
-    norms_ref[0:2, :] = vectors_ref[last:, :]
-    norms_ref[2:3, :] = extra[0:1] + (extra[1:2] + extra[2:3])
-    norms_ref[3:4, :] = extra[3:4] + (extra[4:5] + extra[5:6])
-    norms = norms_ref[...]
-    target = pl.multiple_of(jnp.where(own == 0, 0, rows - HALO), HALO)
-    source = pl.multiple_of(jnp.where(own == 0, 0, 2 * HALO), HALO)
-    eighths = HALO // 8
-    for tile in range(chans // LANES):
-        lanes = slice(tile * LANES, (tile + 1) * LANES)
-        rest_ref[tile, 0:KERNEL, :] = taps[:, lanes]
-        rest_ref[tile, KERNEL : KERNEL + 4, :] = norms[:, lanes]
-        part_ref[tile] = jnp.zeros((3 * HALO, LANES), F32)
-        part_ref[tile, pl.ds(source, HALO), :] = near_ref[0:HALO, lanes].astype(F32)
-        total = block_conv(early_ref[:, lanes].astype(F32), tile, edge_ref, wide_taps_ref)
-        for at in range(eighths):
-            start = KERNEL + 8 + 8 * at
-            rest_ref[tile, start : start + 8, :] = jnp.where(own == 0, total[at], total[at - eighths])
-        for step in range(rows // 8):
-            sent_ref[1, tile, 8 * step : 8 * step + 8, :] = total[step + eighths]
-        total = [sent_ref[1, tile, pl.ds(target + 8 * at, 8), :] for at in range(eighths)]
-        for tap in range(KERNEL):
-            weight = jnp.broadcast_to(wide_taps_ref[tap : tap + 1, lanes], (8, LANES))
-            for at in range(eighths):
-                start = 8 * at + tap + 1
-                total[at] += part_ref[tile, start : start + 8, :] * weight
-        for at in range(eighths):
-            sent_ref[1, tile, pl.ds(target + 8 * at, 8), :] = total[at]
-    rest_copy = pltpu.make_async_copy(rest_ref, store_ref.at[REST], rest_sem)
-    rest_copy.start()
-    conv_copy.wait()
-    rest_copy.wait()
-
-
-def scales(stats_ref, norms):
-    chans = norms.shape[1]
+    copy.wait()
+
+
+def peer_vectors(tail_ref):
+    first = tail_ref.shape[0] - 2 * EXTRA
+    parts = tail_ref[first:, :].astype(F32)
+    parts = jnp.concatenate([parts[:EXTRA], parts[EXTRA:]], axis=1)
+    gain, bias = (parts[at : at + 1] + (parts[at + 1 : at + 2] + parts[at + 2 : at + 3]) for at in (0, 3))
+    return gain, bias, parts[6:7]
+
+
+def scales(stats_ref, norms_ref, tail_ref):
+    chans = norms_ref.shape[1]
+    gain, bias, pivot = peer_vectors(tail_ref)
+    norms = [(norms_ref[0:1, :], norms_ref[1:2, :], 0.0), (gain, bias, pivot)]
     half = chans // 2
     own = lax.axis_index("tensor")
     found = []
@@ -305,29 +291,37 @@
         mean = jnp.sum(means * counts, axis=0)[0] / count
         off = means - mean
         var = jnp.sum(squares + counts * off * off, axis=0)[0] / count
-        scale = lax.rsqrt(var + 1e-05) * norms[2 * shift : 2 * shift + 1]
-        found.append((mean, scale, norms[2 * shift + 1 : 2 * shift + 2]))
+        gain, bias, pivot = norms[shift]
+        found.append((mean - pivot, lax.rsqrt(var + 1e-05) * gain, bias))
     return found
 
 
-def branch_rows(found, conv_of, weight_ref):
+def branch_rows(found, conv_ref, peer_ref, weight_ref):
     own = lax.axis_index("tensor")
     total = None
-    for shift, (mean, scale, bias) in reversed(list(enumerate(found))):
+    for shift in (1, 0):
+        mean, scale, bias = found[shift]
         acts = []
-        for tile in range(mean.shape[1] // LANES):
+        for tile in range(conv_ref.shape[0]):
             lanes = slice(tile * LANES, (tile + 1) * LANES)
-            z = (conv_of(shift, tile) - mean[:, lanes]) * scale[:, lanes] + bias[:, lanes]
+            conv = peer_ref[:, lanes].astype(F32) if shift else conv_ref[tile]
+            z = (conv - mean[:, lanes]) * scale[:, lanes] + bias[:, lanes]
             acts.append(swish(z).astype(BF16))
-        place = own if shift == 0 else 1 - own
+        place = 1 - own if shift else own
         term = jnp.dot(jnp.concatenate(acts, axis=1), weight_ref[place], preferred_element_type=F32)
         total = term if total is None else total + term
     return total
 
 
-def sent_kernel(stats_ref, conv_ref, norms_ref, weight_ref, out_ref):
-    found = scales(stats_ref, norms_ref[...])
-    branch = branch_rows(found, lambda shift, tile: conv_ref[shift, tile], weight_ref)
+def sent_kernel(stats_ref, conv_ref, soon_ref, tail_ref, norms_ref, weight_ref, out_ref, peer_ref):
+    rows, wide = soon_ref.shape
+    target = pl.multiple_of(jnp.where(lax.axis_index("tensor") == 0, 0, rows - HALO), HALO)
+    peer_ref[:, :wide] = soon_ref[...]
+    peer_ref[:, wide:] = tail_ref[0:rows, :]
+    peer_ref[pl.ds(target, HALO), :wide] = tail_ref[rows : rows + HALO, :]
+    peer_ref[pl.ds(target, HALO), wide:] = tail_ref[rows + HALO : rows + 2 * HALO, :]
+    found = scales(stats_ref, norms_ref, tail_ref)
+    branch = branch_rows(found, conv_ref, peer_ref, weight_ref)
     out_ref[...] = branch.astype(BF16)
 
 
@@ -336,15 +330,10 @@
 
 
 def kept_kernel(
-    stats_ref, late_ref, weight_ref, store_ref,
-    mine_ref, base_ref, rest_ref, edge_ref, wide_taps_ref, conv_ref, sums_ref, glu_ref, half_ref, sems,
+    stats_ref, late_ref, tail_ref, norms_ref, weight_ref, store_ref,
+    mine_ref, base_ref, conv_ref, half_ref, sems,
 ):
-    own = lax.axis_index("tensor")
-    rows, _ = mine_ref.shape
-    tiles = conv_ref.shape[0]
     copies = [
-        (store_ref.at[REST], rest_ref),
-        (late_ref, glu_ref),
         (store_ref.at[KEPT], conv_ref),
         (store_ref.at[HALF], half_ref),
         (store_ref.at[OTHER], base_ref),
@@ -352,28 +341,14 @@
     copies = [pltpu.make_async_copy(*pair, sems.at[at]) for at, pair in enumerate(copies)]
     for copy in copies:
         copy.start()
-    clear_ends(edge_ref)
-    target = pl.multiple_of(jnp.where(own == 0, rows - HALO, 0), HALO)
+    found = scales(stats_ref, norms_ref, tail_ref)
     copies[0].wait()
+    branch = branch_rows(found, conv_ref, late_ref, weight_ref)
     copies[1].wait()
-    for tile in range(tiles):
-        lanes = slice(tile * LANES, (tile + 1) * LANES)
-        wide_taps_ref[:, lanes] = rest_ref[tile, 0:KERNEL, :]
-        total = block_conv(glu_ref[:, lanes].astype(F32), tile, edge_ref, wide_taps_ref)
-        for step in range(rows // 8):
-            sums_ref[tile, 8 * step : 8 * step + 8, :] = total[step + HALO // 8]
-        for at in range(HALO // 8):
-            place, start = pl.ds(target + 8 * at, 8), KERNEL + 8 + 8 * at
-            sums_ref[tile, place, :] = sums_ref[tile, place, :] + rest_ref[tile, start : start + 8, :]
-    norms = [rest_ref[tile, KERNEL : KERNEL + 4, :] for tile in range(tiles)]
-    found = scales(stats_ref, jnp.concatenate(norms, axis=1))
-    copies[2].wait()
-    branch = branch_rows(found, lambda shift, tile: (sums_ref if shift else conv_ref)[tile], weight_ref)
-    copies[3].wait()
-    for tile in range(tiles):
+    for tile in range(conv_ref.shape[0]):
         lanes = slice(tile * LANES, (tile + 1) * LANES)
         mine_ref[:, lanes] = (half_ref[tile] + branch[:, lanes]).astype(BF16)
-    copies[4].wait()
+    copies[2].wait()
 
 
 def finish_kernel(mine_ref, base_ref, got_ref, out_ref, done_ref, sems):
@@ -426,14 +401,20 @@
     dma = pltpu.SemaphoreType.DMA
     reach = shape((tiles, span + 2 * HALO, LANES), F32)
     block = shape((tiles, span, LANES), F32)
-    rest = pltpu.VMEM(block.shape, F32)
     store = shape((BLOCKS,) + block.shape, F32)
-    early, first_sums, held, store_first = call(
+    soon, later, first_sums, held, pivot, store_first = call(
         first_block_kernel,
-        (shape((span, chans), BF16), reach, shape((2, width, chans), BF16), store),
+        (
+            shape((span, chans // 2), BF16),
+            shape((span, chans // 2), BF16),
+            reach,
+            shape((2, width, chans), BF16),
+            shape((1, chans), F32),
+            store,
+        ),
         [SMEM, HBM, VMEM, VMEM, HBM],
         (lengths, frames_in, vectors, conv_kernel, glu_weight),
-        out_specs=(VMEM, VMEM, VMEM, HBM),
+        out_specs=(VMEM,) * 5 + (HBM,),
         scratch=(
             pltpu.VMEM((span, width), BF16),
             pltpu.VMEM((2, chans, width), BF16),
@@ -447,71 +428,60 @@
         name="first_block",
         room=48,
     )
-    early = swap(early)
-    late, near, spread, store_second = call(
+    soon = swap(soon)
+    late, tail, spread, store_second = call(
         last_block_kernel,
         (
             shape((span, chans), BF16),
-            shape((HALO + EXTRA, chans), BF16),
+            shape((span + 2 * HALO + 2 * EXTRA, chans // 2), BF16),
             shape((devices, 2, chans + chans // 2 + LANES), BF16),
             store,
         ),
-        [SMEM] + [VMEM] * 5 + [HBM],
-        (lengths, frames, vectors, conv_kernel, held, first_sums, store_first),
+        [SMEM] + [VMEM] * 7 + [HBM],
+        (lengths, frames, vectors, conv_kernel, held, first_sums, pivot, later, store_first),
         out_specs=(HBM, VMEM, HBM, HBM),
         scratch=(
             wide_taps,
             edge,
-            pltpu.VMEM((tiles, 2 * span + 2 * HALO, LANES), F32),
+            pltpu.VMEM((2, tiles, span, LANES), F32),
+            pltpu.VMEM((2, span, LANES), F32),
             pltpu.VMEM((span, chans), BF16),
             pltpu.VMEM((devices, 2, chans + chans // 2 + LANES), BF16),
-            dma((pieces,)),
+            dma((tiles,)),
             dma((tiles, 2)),
             dma,
         ),
-        aliases={6: 3},
+        aliases={8: 3},
         name="last_block",
         room=40,
     )
-    spread, early, out_weight = lax.optimization_barrier((spread, early, out_weight))
+    spread, soon, out_weight = lax.optimization_barrier((spread, soon, out_weight))
     stats = lax.all_to_all(spread, ("dp", "tensor"), split_axis=0, concat_axis=0, tiled=True)
     stats = stats.reshape((devices // 2, 2) + spread.shape[1:])
-    near, late = swap(near), swap(late)
-    (weight,) = call(turn_kernel, (shape((2, chans, cols), BF16),), [VMEM], (out_weight,), name="turn")
-    sent_conv, norms, store_third = call(
-        peer_conv_kernel,
-        (shape((2,) + block.shape, F32), shape((4, chans), F32), store),
-        [VMEM, VMEM, VMEM, HBM],
-        (vectors, near, early, store_second),
-        out_specs=(VMEM, VMEM, HBM),
-        scratch=(edge, wide_taps, rest, pltpu.VMEM((tiles, 3 * HALO, LANES), F32), dma, dma),
-        aliases={3: 2},
-        name="peer_conv",
-        room=40,
+    tail, late = swap(tail), swap(late)
+    weight, sent_conv, norms = call(
+        turn_kernel,
+        (shape((2, chans, cols), BF16), block, shape((2, chans), F32)),
+        [VMEM, VMEM, HBM],
+        (out_weight, vectors, store_second),
+        scratch=(dma,),
+        name="turn",
     )
     (sent,) = call(
         sent_kernel,
         (shape((span, cols), BF16),),
-        [VMEM] * 4,
-        (stats, sent_conv, norms, weight),
+        [VMEM] * 6,
+        (stats, sent_conv, soon, tail, norms, weight),
+        scratch=(pltpu.VMEM((span, chans), BF16),),
         name="branch_sent",
     )
     got = swap(sent)
     mine, base = call(
         kept_kernel,
         (shape((span, cols), BF16), block),
-        [VMEM, HBM, VMEM, HBM],
-        (stats, late, weight, store_third),
-        scratch=(
-            rest,
-            edge,
-            wide_taps,
-            pltpu.VMEM(block.shape, F32),
-            pltpu.VMEM(block.shape, F32),
-            pltpu.VMEM((span, chans), BF16),
-            pltpu.VMEM(block.shape, F32),
-            dma((5,)),
-        ),
+        [VMEM] * 5 + [HBM],
+        (stats, late, tail, norms, weight, store_second),
+        scratch=(pltpu.VMEM(block.shape, F32), pltpu.VMEM(block.shape, F32), dma((3,))),
         name="branch_kept",
     )
     (out,) = call(

time: 40.1 us -> 39.7 us (0.990)
  Pallas kernels: 14.6 us -> 12.4 us
  waiting for transfers between devices: 8.82 us -> 10.1 us
  starting transfers between devices: 11.4 us -> 11.9 us
    pallas_call x7 -> x6, Pallas kernels: 14.6 us -> 12.4 us  [call(): pl.pallas_call(kernel, out_shape=tuple(outs), in_specs=list(in_specs), ou...]
    all_to_all x1, starting transfers between devices: 5.33 us -> 6.39 us  [two_parts(): lax.all_to_all(spread, ('dp', 'tensor'), split_axis=0, concat_axis=0, til...]
    all_to_all x1, waiting for transfers between devices: 0.65 us -> 1.35 us  [two_parts(): lax.all_to_all(spread, ('dp', 'tensor'), split_axis=0, concat_axis=0, til...]
    ppermute x5, waiting for transfers between devices: 8.16 us -> 8.75 us  [swap(): return lax.ppermute(value, 'tensor', [(0, 1), (1, 0)])]
    ppermute x5, starting transfers between devices: 6.04 us -> 5.48 us  [swap(): return lax.ppermute(value, 'tensor', [(0, 1), (1, 0)])]
  transfers between devices with their start and end apart: 6 -> 6, of which waited for: 6 -> 5; matrix products, arithmetic and copies ran while one was open for 2% -> 2% of each run, Pallas kernels for 35% -> 29%
where the time goes in v5:
time: 39.7 us; the launch traced here: 39.3 us
  Pallas kernels  12.4 us (31%)
  starting transfers between devices  11.9 us (30%)
  waiting for transfers between devices  10.1 us (25%)
  local copies, waits for them, and re-layouts  3.46 us (9%)
  other arithmetic  0.76 us (2%)
  between operations  0.72 us (2%)
    pallas_call x6, Pallas kernels, call(): pl.pallas_call(kernel, out_shape=tuple(outs), in_specs=list(in_specs), ou...  12.4 us
    ppermute x5, waiting for transfers between devices, swap(): return lax.ppermute(value, 'tensor', [(0, 1), (1, 0)])  8.75 us
    all_to_all x1, starting transfers between devices, two_parts(): lax.all_to_all(spread, ('dp', 'tensor'), split_axis=0, concat_axis=0, til...  6.39 us
    ppermute x5, starting transfers between devices, swap(): return lax.ppermute(value, 'tensor', [(0, 1), (1, 0)])  5.48 us
    unnamed x6, local copies, waits for them, and re-layouts  3.45 us
    all_to_all x1, waiting for transfers between devices, two_parts(): lax.all_to_all(spread, ('dp', 'tensor'), split_axis=0, concat_axis=0, til...  1.35 us
  transfers between devices with their start and end apart: 6, of which 5 were waited for; matrix products, arithmetic and copies ran while one was open for 2% of the time, Pallas kernels for 29%

profile of v5, /device:TPU:0, one launch (start us, length us, event | category | flops | bytes accessed | tf_op | source)
XLA Modules:
  0.0 39.3 jit_solution(17633615652811562985)
XLA Ops:
  0.0 3.0 %collective-permute-start = (bf16[128,1536]{1,0:T(8,128)(2,1)}, bf16[128,1536]{1,0:T(8,128)(2,1)S(1)}, u32[]{:S(2)}, u32[]{:S(2)}) collective-permute-start(bf16[128,1536]{1,0:T(8,128)(2,1)} %bitcast.5), channel_id=1, source_target_pairs={{0,1},{1,0},{2,3},{3,2},{4,5},{5,4},{6,7},{7,6},{8,9},{9,8},{10,11... | collective-permute-start | bytes 1179656 | tf_op jit(solution)/shard_map/ppermute | solution.py:395
  3.6 0.8 %pad_maximum_fusion = f32[4608]{0:T(1024)S(1)} fusion(f32[768]{0:T(1024)} %param.16, f32[768]{0:T(1024)} %param.15, f32[1536]{0:T(1024)} %param.12, f32[1536]{0:T(1024)} %param.11), kind=kLoop, calls=%fused_computation | loop fusion | flops 13824 | bytes 36864 | tf_op jit(solution)/shard_map/concatenate | solution.py:398
  4.4 0.0 copy-start.1
  4.4 1.0 %copy-done.1 = bf16[1,128,1536]{2,1,0:T(8,128)(2,1)S(1)} copy-done((bf16[1,128,1536]{2,1,0:T(8,128)(2,1)S(1)}, bf16[1,128,1536]{2,1,0:T(8,128)(2,1)}, u32[]{:S(2)}) %copy-start.1) | copy-done | bytes 393240
  5.4 0.0 copy-start.2
  5.4 0.8 %copy-done.2 = bf16[32,768]{1,0:T(8,128)(2,1)S(1)} copy-done((bf16[32,768]{1,0:T(8,128)(2,1)S(1)}, bf16[32,768]{1,0:T(8,128)(2,1)}, u32[]{:S(2)}) %copy-start.2) | copy-done | bytes 49176
  6.2 4.7 %first_block.1 = (bf16[128,384]{1,0:T(8,128)(2,1)S(1)}, bf16[128,384]{1,0:T(8,128)(2,1)S(1)}, f32[6,160,128]{2,1,0:T(8,128)S(1)}, bf16[2,1536,768]{2,1,0:T(8,128...) custom-call(s32[1]{0:T(128)S(6)} %copy.12.lengths_ref, bf16[1,128,1536]{2,1,0:T(8,128)(2,1)S(1)} %copy-done.1, ...), custom_call_target="tpu_custom_call" | custom-call | tf_op jit(solution)/shard_map/first_block/pallas_call | solution.py:373
  10.9 0.1 collective-permute-start.1
  11.0 1.3 %collective-permute-done.rows_ref = bf16[128,1536]{1,0:T(8,128)(2,1)S(1)} collective-permute-done((bf16[128,1536]{1,0:T(8,128)(2,1)}, bf16[128,1536]{1,0:T(8,128)(2,1)S(1)}, u32[]{:S(2)}, u32[]{:S(2)}) %collective-permute-start) | collective-permute-done | bytes 393248 | tf_op jit(solution)/shard_map/ppermute | solution.py:395
  12.3 3.3 %last_block.1 = (bf16[128,768]{1,0:T(8,128)(2,1)}, bf16[176,384]{1,0:T(8,128)(2,1)S(1)}, bf16[32,2,1280]{2,1,0:T(2,128)(2,1)}, f32[72,6,128,128]{3,2,1,0:T(8,128)}) custom-call(s32[1]{0:T(128)S(6)} %copy.12.lengths_ref, bf16[128,1536]{1,0:T(8,128)(2,1)S(1)} %collective-permute-done.rows_ref, ...), custom_call_target="tpu_custom_call", output_to_operand_aliasing={{3}: (8, {})} | custom-call | tf_op jit(solution)/shard_map/last_block/pallas_call | solution.py:373
  15.6 0.0 collective-permute-done.1.soon_ref
  15.6 6.4 %all-to-all-start = ((bf16[32,2,1280]{2,1,0:T(2,128)(2,1)}), bf16[32,2,1280]{2,1,0:T(2,128)(2,1)S(1)}, u32[]{:S(2)}, u32[]{:S(2)}) async-start(bf16[32,2,1280]{2,1,0:T(2,128)(2,1)} %get-tuple-element.30), calls=%async_computation | async-start | bytes 327680 | tf_op jit(solution)/shard_map/all_to_all | solution.py:459
  22.0 1.8 %collective-permute-start.3 = (bf16[176,384]{1,0:T(8,128)(2,1)S(1)}, bf16[176,384]{1,0:T(8,128)(2,1)S(1)}, u32[]{:S(2)}, u32[]{:S(2)}) collective-permute-start(bf16[176,384]{1,0:T(8,128)(2,1)S(1)} %get-tuple-element.32), channel_id=1, source_target_pairs={{0,1},{1,0},{2,3},{3,2},{4,5},{5,4},{6,7},{7,6},{8,9},{9,8},{10,11... | collective-permute-start | bytes 405512 | tf_op jit(solution)/shard_map/ppermute | solution.py:395
  23.8 0.3 collective-permute-start.2
  24.1 0.0 copy-start
  24.1 1.7 %copy-done = bf16[768,1536]{1,0:T(8,128)(2,1)S(1)} copy-done((bf16[768,1536]{1,0:T(8,128)(2,1)S(1)}, bf16[768,1536]{1,0:T(8,128)(2,1)}, u32[]{:S(2)}) %copy-start) | copy-done | bytes 2359320
  25.7 1.0 %turn.1 = (bf16[2,768,768]{2,1,0:T(8,128)(2,1)S(1)}, f32[6,128,128]{2,1,0:T(8,128)S(1)}, f32[2,768]{1,0:T(2,128)S(1)}) custom-call(bf16[768,1536]{1,0:T(8,128)(2,1)S(1)} %copy-done, f32[6,768]{1,0:T(8,128)S(1)} %reshape.6.vectors_ref, f32[72,6,128,128]{3,2,1,0:T(8,128)} %get-tuple-element.34.store_ref), custom_call_target="tpu_custom_call" | custom-call | tf_op jit(solution)/shard_map/turn/pallas_call | solution.py:373
  26.8 3.0 %collective-permute-done.3.tail_ref = bf16[176,384]{1,0:T(8,128)(2,1)S(1)} collective-permute-done((bf16[176,384]{1,0:T(8,128)(2,1)S(1)}, bf16[176,384]{1,0:T(8,128)(2,1)S(1)}, u32[]{:S(2)}, u32[]{:S(2)}) %collective-permute-start.3) | collective-permute-done | bytes 135200 | tf_op jit(solution)/shard_map/ppermute | solution.py:395
  29.8 1.3 %all-to-all-done = bf16[32,2,1280]{2,1,0:T(2,128)(2,1)S(1)} async-done(((bf16[32,2,1280]{2,1,0:T(2,128)(2,1)}), bf16[32,2,1280]{2,1,0:T(2,128)(2,1)S(1)}, u32[]{:S(2)}, u32[]{:S(2)}) %all-to-all-start) | async-done | bytes 163872 | tf_op jit(solution)/shard_map/all_to_all | solution.py:459
  31.1 0.9 %branch_sent.1 = bf16[128,768]{1,0:T(8,128)(2,1)S(1)} custom-call(bf16[16,2,2,1280]{3,2,1,0:T(2,128)(2,1)S(1)} %bitcast.3, f32[6,128,128]{2,1,0:T(8,128)S(1)} %get-tuple-element.39.conv_ref, bf16[128,384]{1,0:T(8,128)(2,1)S(1)} %collective-permute-done.1.soon_ref, bf16[176,384]{1,0:T(8,128)(2,1)S(1)} %collective-permute-done.3.tail_ref, ...), custom_call_target="tpu_custom_call" | custom-call | tf_op jit(solution)/shard_map/branch_sent/pallas_call | solution.py:373
  32.0 0.3 collective-permute-start.4
  32.4 1.4 %collective-permute-done.2.late_ref = bf16[128,768]{1,0:T(8,128)(2,1)S(1)} collective-permute-done((bf16[128,768]{1,0:T(8,128)(2,1)}, bf16[128,768]{1,0:T(8,128)(2,1)S(1)}, u32[]{:S(2)}, u32[]{:S(2)}) %collective-permute-start.2) | collective-permute-done | bytes 196640 | tf_op jit(solution)/shard_map/ppermute | solution.py:395
  33.7 1.7 %branch_kept.1 = (bf16[128,768]{1,0:T(8,128)(2,1)S(1)}, f32[6,128,128]{2,1,0:T(8,128)S(1)}) custom-call(bf16[16,2,2,1280]{3,2,1,0:T(2,128)(2,1)S(1)} %bitcast.4, bf16[128,768]{1,0:T(8,128)(2,1)S(1)} %collective-permute-done.2.late_ref, bf16[176,384]{1,0:T(8,128)(2,1)S(1)} %collective-permute-done.3.tail_ref, f32[2,768]{1,0:T(2,128)S(1)} %get-tuple-element.35.norms_ref, ...), custom_call_target="tpu_custom_call" | custom-call | tf_op jit(solution)/shard_map/branch_kept/pallas_call | solution.py:373
  35.4 3.0 %collective-permute-done.4.got_ref = bf16[128,768]{1,0:T(8,128)(2,1)S(1)} collective-permute-done((bf16[128,768]{1,0:T(8,128)(2,1)S(1)}, bf16[128,768]{1,0:T(8,128)(2,1)S(1)}, u32[]{:S(2)}, u32[]{:S(2)}) %collective-permute-start.4) | collective-permute-done | bytes 196640 | tf_op jit(solution)/shard_map/ppermute | solution.py:395
  38.5 0.8 %residual.1 = bf16[128,1536]{1,0:T(8,128)(2,1)} custom-call(bf16[128,768]{1,0:T(8,128)(2,1)S(1)} %get-tuple-element.37.mine_ref, f32[6,128,128]{2,1,0:T(8,128)S(1)} %get-tuple-element.38.base_ref, bf16[128,768]{1,0:T(8,128)(2,1)S(1)} %collective-permute-done.4.got_ref), custom_call_target="tpu_custom_call" | custom-call | tf_op jit(solution)/shard_map/residual/pallas_call | solution.py:373
  (1 shorter events, 0.0 us)
Async XLA Ops:
  0.0 12.3 %collective-permute-start = (bf16[128,1536]{1,0:T(8,128)(2,1)}, bf16[128,1536]{1,0:T(8,128)(2,1)S(1)}, u32[]{:S(2)}, u32[]{:S(2)}) collective-permute-start(bf16[128,1536]{1,0:T(8,128)(2,1)} %bitcast.5), channel_id=1, source_target_pairs={{0,1},{1,0},{2,3},{3,2},{4,5},{5,4},{6,7},{7,6},{8,9},{9,8},{10,11... | collective-permute-start | bytes 1179656 | tf_op jit(solution)/shard_map/ppermute | solution.py:395
  4.4 1.0 %copy-start.1 = (bf16[1,128,1536]{2,1,0:T(8,128)(2,1)S(1)}, bf16[1,128,1536]{2,1,0:T(8,128)(2,1)}, u32[]{:S(2)}) copy-start(bf16[1,128,1536]{2,1,0:T(8,128)(2,1)} %frames_ref.1) | copy-start | bytes 1179652
  5.4 0.8 %copy-start.2 = (bf16[32,768]{1,0:T(8,128)(2,1)S(1)}, bf16[32,768]{1,0:T(8,128)(2,1)}, u32[]{:S(2)}) copy-start(bf16[32,768]{1,0:T(8,128)(2,1)} %taps_ref.3) | copy-start | bytes 147460
  10.9 4.7 %collective-permute-start.1 = (bf16[128,384]{1,0:T(8,128)(2,1)S(1)}, bf16[128,384]{1,0:T(8,128)(2,1)S(1)}, u32[]{:S(2)}, u32[]{:S(2)}) collective-permute-start(bf16[128,384]{1,0:T(8,128)(2,1)S(1)} %get-tuple-element.29), channel_id=1, source_target_pairs={{0,1},{1,0},{2,3},{3,2},{4,5},{5,4},{6,7},{7,6},{8,9},{9,8},{10,11... | collective-permute-start | bytes 294920 | tf_op jit(solution)/shard_map/ppermute | solution.py:395
  15.6 15.5 %all-to-all-start = ((bf16[32,2,1280]{2,1,0:T(2,128)(2,1)}), bf16[32,2,1280]{2,1,0:T(2,128)(2,1)S(1)}, u32[]{:S(2)}, u32[]{:S(2)}) async-start(bf16[32,2,1280]{2,1,0:T(2,128)(2,1)} %get-tuple-element.30), calls=%async_computation | async-start | bytes 327680 | tf_op jit(solution)/shard_map/all_to_all | solution.py:459
  22.0 7.8 %collective-permute-start.3 = (bf16[176,384]{1,0:T(8,128)(2,1)S(1)}, bf16[176,384]{1,0:T(8,128)(2,1)S(1)}, u32[]{:S(2)}, u32[]{:S(2)}) collective-permute-start(bf16[176,384]{1,0:T(8,128)(2,1)S(1)} %get-tuple-element.32), channel_id=1, source_target_pairs={{0,1},{1,0},{2,3},{3,2},{4,5},{5,4},{6,7},{7,6},{8,9},{9,8},{10,11... | collective-permute-start | bytes 405512 | tf_op jit(solution)/shard_map/ppermute | solution.py:395
  23.8 9.9 %collective-permute-start.2 = (bf16[128,768]{1,0:T(8,128)(2,1)}, bf16[128,768]{1,0:T(8,128)(2,1)S(1)}, u32[]{:S(2)}, u32[]{:S(2)}) collective-permute-start(bf16[128,768]{1,0:T(8,128)(2,1)} %get-tuple-element.31), channel_id=1, source_target_pairs={{0,1},{1,0},{2,3},{3,2},{4,5},{5,4},{6,7},{7,6},{8,9},{9,8},{10,11... | collective-permute-start | bytes 589832 | tf_op jit(solution)/shard_map/ppermute | solution.py:395
  24.1 1.7 %copy-start = (bf16[768,1536]{1,0:T(8,128)(2,1)S(1)}, bf16[768,1536]{1,0:T(8,128)(2,1)}, u32[]{:S(2)}) copy-start(bf16[768,1536]{1,0:T(8,128)(2,1)} %weight_ref.2) | copy-start | bytes 7077892
  32.0 6.5 %collective-permute-start.4 = (bf16[128,768]{1,0:T(8,128)(2,1)S(1)}, bf16[128,768]{1,0:T(8,128)(2,1)S(1)}, u32[]{:S(2)}, u32[]{:S(2)}) collective-permute-start(bf16[128,768]{1,0:T(8,128)(2,1)S(1)} %branch_sent.1), channel_id=1, source_target_pairs={{0,1},{1,0},{2,3},{3,2},{4,5},{5,4},{6,7},{7,6},{8,9},{9,8},{10,11... | collective-permute-start | bytes 589832 | tf_op jit(solution)/shard_map/ppermute | solution.py:395

commit v6 on v5

--- a/solution.py
+++ b/solution.py
@@ -282,7 +282,7 @@
     half = chans // 2
     own = lax.axis_index("tensor")
     found = []
-    for shift, place in enumerate((own, 1 - own)):
+    for shift, place in enumerate((1 - own, own)):
         seen = stats_ref[:, pl.ds(place, 1), :, :].astype(F32)
         both = seen[:, :, 0:1, :] + seen[:, :, 1:2, :]
         means, counts = both[..., :chans], both[..., chans + half : chans + half + 1]
@@ -456,7 +456,10 @@
         room=40,
     )
     spread, soon, out_weight = lax.optimization_barrier((spread, soon, out_weight))
-    stats = lax.all_to_all(spread, ("dp", "tensor"), split_axis=0, concat_axis=0, tiled=True)
+    stats = lax.all_to_all(
+        spread, ("dp", "tensor"), split_axis=0, concat_axis=0, tiled=True,
+        axis_index_groups=[list(reversed(range(devices)))],
+    )
     stats = stats.reshape((devices // 2, 2) + spread.shape[1:])
     tail, late = swap(tail), swap(late)
     weight, sent_conv, norms = call(

time: 39.7 us -> 39.1 us (0.985)
  waiting for transfers between devices: 10.1 us -> 9.46 us
    all_to_all x1, waiting for transfers between devices: 1.35 us -> 0.94 us  [two_parts(): lax.all_to_all(spread, ('dp', 'tensor'), split_axis=0, concat_axis=0, til...]
  transfers between devices with their start and end apart: 6 -> 6, of which waited for: 5 -> 5; matrix products, arithmetic and copies ran while one was open for 2% -> 2% of each run, Pallas kernels for 29% -> 30%
where the time goes in v6:
time: 39.1 us; the launch traced here: 38.7 us
  starting transfers between devices  12.2 us (31%)
  Pallas kernels  12.2 us (31%)
  waiting for transfers between devices  9.46 us (24%)
  local copies, waits for them, and re-layouts  3.46 us (9%)
  other arithmetic  0.76 us (2%)
  between operations  0.72 us (2%)
    pallas_call x6, Pallas kernels, call(): pl.pallas_call(kernel, out_shape=tuple(outs), in_specs=list(in_specs), ou...  12.2 us
    ppermute x5, waiting for transfers between devices, swap(): return lax.ppermute(value, 'tensor', [(0, 1), (1, 0)])  8.52 us
    all_to_all x1, starting transfers between devices, two_parts(): lax.all_to_all(spread, ('dp', 'tensor'), split_axis=0, concat_axis=0, til...  6.39 us
    ppermute x5, starting transfers between devices, swap(): return lax.ppermute(value, 'tensor', [(0, 1), (1, 0)])  5.76 us
    unnamed x6, local copies, waits for them, and re-layouts  3.45 us
    all_to_all x1, waiting for transfers between devices, two_parts(): lax.all_to_all(spread, ('dp', 'tensor'), split_axis=0, concat_axis=0, til...  0.94 us
  transfers between devices with their start and end apart: 6, of which 5 were waited for; matrix products, arithmetic and copies ran while one was open for 2% of the time, Pallas kernels for 30%

profile of v6, /device:TPU:0, one launch (start us, length us, event | category | flops | bytes accessed | tf_op | source)
XLA Modules:
  0.0 38.7 jit_solution(13179626487116777041)
XLA Ops:
  0.0 3.0 %collective-permute-start = (bf16[128,1536]{1,0:T(8,128)(2,1)}, bf16[128,1536]{1,0:T(8,128)(2,1)S(1)}, u32[]{:S(2)}, u32[]{:S(2)}) collective-permute-start(bf16[128,1536]{1,0:T(8,128)(2,1)} %bitcast.5), channel_id=1, source_target_pairs={{0,1},{1,0},{2,3},{3,2},{4,5},{5,4},{6,7},{7,6},{8,9},{9,8},{10,11... | collective-permute-start | bytes 1179656 | tf_op jit(solution)/shard_map/ppermute | solution.py:395
  3.6 0.8 %pad_maximum_fusion = f32[4608]{0:T(1024)S(1)} fusion(f32[768]{0:T(1024)} %param.16, f32[768]{0:T(1024)} %param.15, f32[1536]{0:T(1024)} %param.12, f32[1536]{0:T(1024)} %param.11), kind=kLoop, calls=%fused_computation | loop fusion | flops 13824 | bytes 36864 | tf_op jit(solution)/shard_map/concatenate | solution.py:398
  4.4 0.0 copy-start.1
  4.4 1.0 %copy-done.1 = bf16[1,128,1536]{2,1,0:T(8,128)(2,1)S(1)} copy-done((bf16[1,128,1536]{2,1,0:T(8,128)(2,1)S(1)}, bf16[1,128,1536]{2,1,0:T(8,128)(2,1)}, u32[]{:S(2)}) %copy-start.1) | copy-done | bytes 393240
  5.4 0.0 copy-start.2
  5.4 0.8 %copy-done.2 = bf16[32,768]{1,0:T(8,128)(2,1)S(1)} copy-done((bf16[32,768]{1,0:T(8,128)(2,1)S(1)}, bf16[32,768]{1,0:T(8,128)(2,1)}, u32[]{:S(2)}) %copy-start.2) | copy-done | bytes 49176
  6.2 4.7 %first_block.1 = (bf16[128,384]{1,0:T(8,128)(2,1)S(1)}, bf16[128,384]{1,0:T(8,128)(2,1)S(1)}, f32[6,160,128]{2,1,0:T(8,128)S(1)}, bf16[2,1536,768]{2,1,0:T(8,128...) custom-call(s32[1]{0:T(128)S(6)} %copy.12.lengths_ref, bf16[1,128,1536]{2,1,0:T(8,128)(2,1)S(1)} %copy-done.1, ...), custom_call_target="tpu_custom_call" | custom-call | tf_op jit(solution)/shard_map/first_block/pallas_call | solution.py:373
  10.9 0.1 collective-permute-start.1
  11.0 1.3 %collective-permute-done.rows_ref = bf16[128,1536]{1,0:T(8,128)(2,1)S(1)} collective-permute-done((bf16[128,1536]{1,0:T(8,128)(2,1)}, bf16[128,1536]{1,0:T(8,128)(2,1)S(1)}, u32[]{:S(2)}, u32[]{:S(2)}) %collective-permute-start) | collective-permute-done | bytes 393248 | tf_op jit(solution)/shard_map/ppermute | solution.py:395
  12.3 3.3 %last_block.1 = (bf16[128,768]{1,0:T(8,128)(2,1)}, bf16[176,384]{1,0:T(8,128)(2,1)S(1)}, bf16[32,2,1280]{2,1,0:T(2,128)(2,1)}, f32[72,6,128,128]{3,2,1,0:T(8,128)}) custom-call(s32[1]{0:T(128)S(6)} %copy.12.lengths_ref, bf16[128,1536]{1,0:T(8,128)(2,1)S(1)} %collective-permute-done.rows_ref, ...), custom_call_target="tpu_custom_call", output_to_operand_aliasing={{3}: (8, {})} | custom-call | tf_op jit(solution)/shard_map/last_block/pallas_call | solution.py:373
  15.6 0.0 collective-permute-done.1.soon_ref
  15.6 6.4 %all-to-all-start = ((bf16[32,2,1280]{2,1,0:T(2,128)(2,1)}), bf16[32,2,1280]{2,1,0:T(2,128)(2,1)S(1)}, u32[]{:S(2)}, u32[]{:S(2)}) async-start(bf16[32,2,1280]{2,1,0:T(2,128)(2,1)} %get-tuple-element.30), calls=%async_computation | async-start | bytes 327680 | tf_op jit(solution)/shard_map/all_to_all | solution.py:459
  22.0 1.8 %collective-permute-start.3 = (bf16[176,384]{1,0:T(8,128)(2,1)S(1)}, bf16[176,384]{1,0:T(8,128)(2,1)S(1)}, u32[]{:S(2)}, u32[]{:S(2)}) collective-permute-start(bf16[176,384]{1,0:T(8,128)(2,1)S(1)} %get-tuple-element.32), channel_id=1, source_target_pairs={{0,1},{1,0},{2,3},{3,2},{4,5},{5,4},{6,7},{7,6},{8,9},{9,8},{10,11... | collective-permute-start | bytes 405512 | tf_op jit(solution)/shard_map/ppermute | solution.py:395
  23.8 0.3 collective-permute-start.2
  24.1 0.0 copy-start
  24.1 1.7 %copy-done = bf16[768,1536]{1,0:T(8,128)(2,1)S(1)} copy-done((bf16[768,1536]{1,0:T(8,128)(2,1)S(1)}, bf16[768,1536]{1,0:T(8,128)(2,1)}, u32[]{:S(2)}) %copy-start) | copy-done | bytes 2359320
  25.7 1.0 %turn.1 = (bf16[2,768,768]{2,1,0:T(8,128)(2,1)S(1)}, f32[6,128,128]{2,1,0:T(8,128)S(1)}, f32[2,768]{1,0:T(2,128)S(1)}) custom-call(bf16[768,1536]{1,0:T(8,128)(2,1)S(1)} %copy-done, f32[6,768]{1,0:T(8,128)S(1)} %reshape.6.vectors_ref, f32[72,6,128,128]{3,2,1,0:T(8,128)} %get-tuple-element.34.store_ref), custom_call_target="tpu_custom_call" | custom-call | tf_op jit(solution)/shard_map/turn/pallas_call | solution.py:373
  26.8 3.1 %collective-permute-done.3.tail_ref = bf16[176,384]{1,0:T(8,128)(2,1)S(1)} collective-permute-done((bf16[176,384]{1,0:T(8,128)(2,1)S(1)}, bf16[176,384]{1,0:T(8,128)(2,1)S(1)}, u32[]{:S(2)}, u32[]{:S(2)}) %collective-permute-start.3) | collective-permute-done | bytes 135200 | tf_op jit(solution)/shard_map/ppermute | solution.py:395
  29.8 0.9 %all-to-all-done = bf16[32,2,1280]{2,1,0:T(2,128)(2,1)S(1)} async-done(((bf16[32,2,1280]{2,1,0:T(2,128)(2,1)}), bf16[32,2,1280]{2,1,0:T(2,128)(2,1)S(1)}, u32[]{:S(2)}, u32[]{:S(2)}) %all-to-all-start) | async-done | bytes 163872 | tf_op jit(solution)/shard_map/all_to_all | solution.py:459
  30.8 0.9 %branch_sent.1 = bf16[128,768]{1,0:T(8,128)(2,1)S(1)} custom-call(bf16[16,2,2,1280]{3,2,1,0:T(2,128)(2,1)S(1)} %bitcast.3, f32[6,128,128]{2,1,0:T(8,128)S(1)} %get-tuple-element.39.conv_ref, bf16[128,384]{1,0:T(8,128)(2,1)S(1)} %collective-permute-done.1.soon_ref, bf16[176,384]{1,0:T(8,128)(2,1)S(1)} %collective-permute-done.3.tail_ref, ...), custom_call_target="tpu_custom_call" | custom-call | tf_op jit(solution)/shard_map/branch_sent/pallas_call | solution.py:373
  31.7 0.6 %collective-permute-start.4 = (bf16[128,768]{1,0:T(8,128)(2,1)S(1)}, bf16[128,768]{1,0:T(8,128)(2,1)S(1)}, u32[]{:S(2)}, u32[]{:S(2)}) collective-permute-start(bf16[128,768]{1,0:T(8,128)(2,1)S(1)} %branch_sent.1), channel_id=1, source_target_pairs={{0,1},{1,0},{2,3},{3,2},{4,5},{5,4},{6,7},{7,6},{8,9},{9,8},{10,11... | collective-permute-start | bytes 589832 | tf_op jit(solution)/shard_map/ppermute | solution.py:395
  32.3 1.5 %collective-permute-done.2.late_ref = bf16[128,768]{1,0:T(8,128)(2,1)S(1)} collective-permute-done((bf16[128,768]{1,0:T(8,128)(2,1)}, bf16[128,768]{1,0:T(8,128)(2,1)S(1)}, u32[]{:S(2)}, u32[]{:S(2)}) %collective-permute-start.2) | collective-permute-done | bytes 196640 | tf_op jit(solution)/shard_map/ppermute | solution.py:395
  33.8 1.6 %branch_kept.1 = (bf16[128,768]{1,0:T(8,128)(2,1)S(1)}, f32[6,128,128]{2,1,0:T(8,128)S(1)}) custom-call(bf16[16,2,2,1280]{3,2,1,0:T(2,128)(2,1)S(1)} %bitcast.4, bf16[128,768]{1,0:T(8,128)(2,1)S(1)} %collective-permute-done.2.late_ref, bf16[176,384]{1,0:T(8,128)(2,1)S(1)} %collective-permute-done.3.tail_ref, f32[2,768]{1,0:T(2,128)S(1)} %get-tuple-element.35.norms_ref, ...), custom_call_target="tpu_custom_call" | custom-call | tf_op jit(solution)/shard_map/branch_kept/pallas_call | solution.py:373
  35.3 2.6 %collective-permute-done.4.got_ref = bf16[128,768]{1,0:T(8,128)(2,1)S(1)} collective-permute-done((bf16[128,768]{1,0:T(8,128)(2,1)S(1)}, bf16[128,768]{1,0:T(8,128)(2,1)S(1)}, u32[]{:S(2)}, u32[]{:S(2)}) %collective-permute-start.4) | collective-permute-done | bytes 196640 | tf_op jit(solution)/shard_map/ppermute | solution.py:395
  38.0 0.8 %residual.1 = bf16[128,1536]{1,0:T(8,128)(2,1)} custom-call(bf16[128,768]{1,0:T(8,128)(2,1)S(1)} %get-tuple-element.37.mine_ref, f32[6,128,128]{2,1,0:T(8,128)S(1)} %get-tuple-element.38.base_ref, bf16[128,768]{1,0:T(8,128)(2,1)S(1)} %collective-permute-done.4.got_ref), custom_call_target="tpu_custom_call" | custom-call | tf_op jit(solution)/shard_map/residual/pallas_call | solution.py:373
  (1 shorter events, 0.0 us)
Async XLA Ops:
  0.0 12.3 %collective-permute-start = (bf16[128,1536]{1,0:T(8,128)(2,1)}, bf16[128,1536]{1,0:T(8,128)(2,1)S(1)}, u32[]{:S(2)}, u32[]{:S(2)}) collective-permute-start(bf16[128,1536]{1,0:T(8,128)(2,1)} %bitcast.5), channel_id=1, source_target_pairs={{0,1},{1,0},{2,3},{3,2},{4,5},{5,4},{6,7},{7,6},{8,9},{9,8},{10,11... | collective-permute-start | bytes 1179656 | tf_op jit(solution)/shard_map/ppermute | solution.py:395
  4.4 1.0 %copy-start.1 = (bf16[1,128,1536]{2,1,0:T(8,128)(2,1)S(1)}, bf16[1,128,1536]{2,1,0:T(8,128)(2,1)}, u32[]{:S(2)}) copy-start(bf16[1,128,1536]{2,1,0:T(8,128)(2,1)} %frames_ref.1) | copy-start | bytes 1179652
  5.4 0.8 %copy-start.2 = (bf16[32,768]{1,0:T(8,128)(2,1)S(1)}, bf16[32,768]{1,0:T(8,128)(2,1)}, u32[]{:S(2)}) copy-start(bf16[32,768]{1,0:T(8,128)(2,1)} %taps_ref.3) | copy-start | bytes 147460
  10.9 4.7 %collective-permute-start.1 = (bf16[128,384]{1,0:T(8,128)(2,1)S(1)}, bf16[128,384]{1,0:T(8,128)(2,1)S(1)}, u32[]{:S(2)}, u32[]{:S(2)}) collective-permute-start(bf16[128,384]{1,0:T(8,128)(2,1)S(1)} %get-tuple-element.29), channel_id=1, source_target_pairs={{0,1},{1,0},{2,3},{3,2},{4,5},{5,4},{6,7},{7,6},{8,9},{9,8},{10,11... | collective-permute-start | bytes 294920 | tf_op jit(solution)/shard_map/ppermute | solution.py:395
  15.6 15.2 %all-to-all-start = ((bf16[32,2,1280]{2,1,0:T(2,128)(2,1)}), bf16[32,2,1280]{2,1,0:T(2,128)(2,1)S(1)}, u32[]{:S(2)}, u32[]{:S(2)}) async-start(bf16[32,2,1280]{2,1,0:T(2,128)(2,1)} %get-tuple-element.30), calls=%async_computation | async-start | bytes 327680 | tf_op jit(solution)/shard_map/all_to_all | solution.py:459
  22.0 7.8 %collective-permute-start.3 = (bf16[176,384]{1,0:T(8,128)(2,1)S(1)}, bf16[176,384]{1,0:T(8,128)(2,1)S(1)}, u32[]{:S(2)}, u32[]{:S(2)}) collective-permute-start(bf16[176,384]{1,0:T(8,128)(2,1)S(1)} %get-tuple-element.32), channel_id=1, source_target_pairs={{0,1},{1,0},{2,3},{3,2},{4,5},{5,4},{6,7},{7,6},{8,9},{9,8},{10,11... | collective-permute-start | bytes 405512 | tf_op jit(solution)/shard_map/ppermute | solution.py:395
  23.8 9.9 %collective-permute-start.2 = (bf16[128,768]{1,0:T(8,128)(2,1)}, bf16[128,768]{1,0:T(8,128)(2,1)S(1)}, u32[]{:S(2)}, u32[]{:S(2)}) collective-permute-start(bf16[128,768]{1,0:T(8,128)(2,1)} %get-tuple-element.31), channel_id=1, source_target_pairs={{0,1},{1,0},{2,3},{3,2},{4,5},{5,4},{6,7},{7,6},{8,9},{9,8},{10,11... | collective-permute-start | bytes 589832 | tf_op jit(solution)/shard_map/ppermute | solution.py:395
  24.1 1.7 %copy-start = (bf16[768,1536]{1,0:T(8,128)(2,1)S(1)}, bf16[768,1536]{1,0:T(8,128)(2,1)}, u32[]{:S(2)}) copy-start(bf16[768,1536]{1,0:T(8,128)(2,1)} %weight_ref.2) | copy-start | bytes 7077892
  31.7 6.3 %collective-permute-start.4 = (bf16[128,768]{1,0:T(8,128)(2,1)S(1)}, bf16[128,768]{1,0:T(8,128)(2,1)S(1)}, u32[]{:S(2)}, u32[]{:S(2)}) collective-permute-start(bf16[128,768]{1,0:T(8,128)(2,1)S(1)} %branch_sent.1), channel_id=1, source_target_pairs={{0,1},{1,0},{2,3},{3,2},{4,5},{5,4},{6,7},{7,6},{8,9},{9,8},{10,11... | collective-permute-start | bytes 589832 | tf_op jit(solution)/shard_map/ppermute | solution.py:395

commit v7 on v6

--- a/solution.py
+++ b/solution.py
@@ -131,6 +131,9 @@
     clear_ends(edge_ref)
     keep = valid_rows(own * rows, rows, lengths_ref[0])
     wide_taps_ref[...] = taps_ref[...].astype(F32)
+    valid = keep.astype(F32)
+    valid_count = jnp.maximum(lengths_ref[0] - own * rows, 1)
+    valid_count = jnp.minimum(valid_count, rows).astype(F32)
     gain, bias = affine(vectors_ref)
     rows_copy.wait()
     normed = layer_norm(rows_ref[...], gain, bias)
@@ -153,7 +156,7 @@
                 sums_ref[tile, 8 * step : 8 * step + 8, :] = each
             lanes = slice(tile * LANES, (tile + 1) * LANES)
             conv = sums_ref[tile, HALO : HALO + rows, :]
-            pivot = jnp.sum(conv, axis=0, keepdims=True) * (1.0 / rows)
+            pivot = jnp.sum(conv * valid, axis=0, keepdims=True) / valid_count
             pivot = pivot.astype(BF16).astype(F32)
             pivot_ref[:, lanes] = pivot
             half, there = half_lanes(tile, tiles)
@@ -184,11 +187,9 @@
     extra = three_parts(vectors_ref[last : last + 1, :])
     extra += three_parts(vectors_ref[last + 1 : last + 2, :])
     extra.append(pivot_ref[...])
-    extra.append(jnp.zeros((EXTRA - len(extra), chans), F32))
-    extra = jnp.concatenate(extra)
     wide = chans // 2
     tail_ref[0:rows, :] = later_ref[...]
-    tail_ref[rows + 2 * HALO :, :] = jnp.concatenate([extra[:, :wide], extra[:, wide:]]).astype(BF16)
+    means = []
     normed = layer_norm(rows_ref[...], *affine(vectors_ref))
     copies = []
     for cut in cuts(chans, WIDE):
@@ -218,7 +219,12 @@
             near = (near - pivot).astype(BF16)
             half, there = half_lanes(tile, tiles)
             tail_ref[rows + half * HALO : rows + (half + 1) * HALO, there] = near
-            peer_rows_ref[:, lanes] = (sent - pivot).astype(BF16)
+            mean = jnp.sum(kept * mask_ref[0] + sent * mask_ref[1], axis=0, keepdims=True)
+            mean = mean / count
+            high = mean.astype(BF16)
+            low = (mean - high.astype(F32)).astype(BF16)
+            means.append(high.astype(F32))
+            peer_rows_ref[:, lanes] = (sent - means[-1]).astype(BF16)
             copies.append(
                 pltpu.make_async_copy(
                     peer_rows_ref.at[:, pl.ds(lanes.start, LANES)],
@@ -227,11 +233,7 @@
                 )
             )
             copies[-1].start()
-            mean = jnp.sum(kept * mask_ref[0] + sent * mask_ref[1], axis=0, keepdims=True)
-            mean = mean / count
-            high = mean.astype(BF16)
-            low = (mean - high.astype(F32)).astype(BF16)
-            mean = high.astype(F32) + low.astype(F32)
+            mean = means[-1] + low.astype(F32)
             kept, sent = (kept - mean) * mask_ref[0], (sent - mean) * mask_ref[1]
             squares = jnp.sum(kept * kept + sent * sent, axis=0, keepdims=True)
             put_sums(stats_ref, tile, chans, high, low, squares.astype(BF16))
@@ -243,6 +245,8 @@
         stats_ref[at] = stats
     copies.append(pltpu.make_async_copy(stats_ref, spread_ref, stats_sem))
     copies[-1].start()
+    extra = jnp.concatenate(extra + [jnp.concatenate(means, axis=1)])
+    tail_ref[rows + 2 * HALO :, :] = jnp.concatenate([extra[:, :wide], extra[:, wide:]]).astype(BF16)
     for copy in copies:
         copy.wait()
 
@@ -272,13 +276,13 @@
     parts = tail_ref[first:, :].astype(F32)
     parts = jnp.concatenate([parts[:EXTRA], parts[EXTRA:]], axis=1)
     gain, bias = (parts[at : at + 1] + (parts[at + 1 : at + 2] + parts[at + 2 : at + 3]) for at in (0, 3))
-    return gain, bias, parts[6:7]
-
-
-def scales(stats_ref, norms_ref, tail_ref):
+    return gain, bias, parts[6:7], parts[7:8]
+
+
+def scales(stats_ref, norms_ref, tail_ref, kept):
     chans = norms_ref.shape[1]
-    gain, bias, pivot = peer_vectors(tail_ref)
-    norms = [(norms_ref[0:1, :], norms_ref[1:2, :], 0.0), (gain, bias, pivot)]
+    gain, bias, *pivots = peer_vectors(tail_ref)
+    norms = [(norms_ref[0:1, :], norms_ref[1:2, :], 0.0), (gain, bias, pivots[kept])]
     half = chans // 2
     own = lax.axis_index("tensor")
     found = []
@@ -320,7 +324,7 @@
     peer_ref[:, wide:] = tail_ref[0:rows, :]
     peer_ref[pl.ds(target, HALO), :wide] = tail_ref[rows : rows + HALO, :]
     peer_ref[pl.ds(target, HALO), wide:] = tail_ref[rows + HALO : rows + 2 * HALO, :]
-    found = scales(stats_ref, norms_ref, tail_ref)
+    found = scales(stats_ref, norms_ref, tail_ref, 0)
     branch = branch_rows(found, conv_ref, peer_ref, weight_ref)
     out_ref[...] = branch.astype(BF16)
 
@@ -341,7 +345,7 @@
     copies = [pltpu.make_async_copy(*pair, sems.at[at]) for at, pair in enumerate(copies)]
     for copy in copies:
         copy.start()
-    found = scales(stats_ref, norms_ref, tail_ref)
+    found = scales(stats_ref, norms_ref, tail_ref, 1)
     copies[0].wait()
     branch = branch_rows(found, conv_ref, late_ref, weight_ref)
     copies[1].wait()

time: 39.1 us -> 39.2 us (level)
  transfers between devices with their start and end apart: 6 -> 6, of which waited for: 5 -> 5; matrix products, arithmetic and copies ran while one was open for 2% -> 2% of each run, Pallas kernels for 30% -> 29%
where the time goes in v7:
time: 39.2 us; the launch traced here: 38.8 us
  starting transfers between devices  12.2 us (31%)
  Pallas kernels  12.2 us (31%)
  waiting for transfers between devices  9.46 us (24%)
  local copies, waits for them, and re-layouts  3.46 us (9%)
  other arithmetic  0.76 us (2%)
  between operations  0.73 us (2%)
    pallas_call x6, Pallas kernels, call(): pl.pallas_call(kernel, out_shape=tuple(outs), in_specs=list(in_specs), ou...  12.2 us
    ppermute x5, waiting for transfers between devices, swap(): return lax.ppermute(value, 'tensor', [(0, 1), (1, 0)])  8.53 us
    all_to_all x1, starting transfers between devices, two_parts(): lax.all_to_all(spread, ('dp', 'tensor'), split_axis=0, concat_axis=0, til...  6.43 us
    ppermute x5, starting transfers between devices, swap(): return lax.ppermute(value, 'tensor', [(0, 1), (1, 0)])  5.74 us
    unnamed x6, local copies, waits for them, and re-layouts  3.45 us
    all_to_all x1, waiting for transfers between devices, two_parts(): lax.all_to_all(spread, ('dp', 'tensor'), split_axis=0, concat_axis=0, til...  0.94 us
  transfers between devices with their start and end apart: 6, of which 5 were waited for; matrix products, arithmetic and copies ran while one was open for 2% of the time, Pallas kernels for 29%

profile of v7, /device:TPU:0, one launch (start us, length us, event | category | flops | bytes accessed | tf_op | source)
XLA Modules:
  0.0 38.8 jit_solution(4776145405189404958)
XLA Ops:
  0.0 3.0 %collective-permute-start = (bf16[128,1536]{1,0:T(8,128)(2,1)}, bf16[128,1536]{1,0:T(8,128)(2,1)S(1)}, u32[]{:S(2)}, u32[]{:S(2)}) collective-permute-start(bf16[128,1536]{1,0:T(8,128)(2,1)} %bitcast.5), channel_id=1, source_target_pairs={{0,1},{1,0},{2,3},{3,2},{4,5},{5,4},{6,7},{7,6},{8,9},{9,8},{10,11... | collective-permute-start | bytes 1179656 | tf_op jit(solution)/shard_map/ppermute | solution.py:399
  3.6 0.8 %pad_maximum_fusion = f32[4608]{0:T(1024)S(1)} fusion(f32[768]{0:T(1024)} %param.16, f32[768]{0:T(1024)} %param.15, f32[1536]{0:T(1024)} %param.12, f32[1536]{0:T(1024)} %param.11), kind=kLoop, calls=%fused_computation | loop fusion | flops 13824 | bytes 36864 | tf_op jit(solution)/shard_map/concatenate | solution.py:402
  4.4 0.0 copy-start.1
  4.4 1.0 %copy-done.1 = bf16[1,128,1536]{2,1,0:T(8,128)(2,1)S(1)} copy-done((bf16[1,128,1536]{2,1,0:T(8,128)(2,1)S(1)}, bf16[1,128,1536]{2,1,0:T(8,128)(2,1)}, u32[]{:S(2)}) %copy-start.1) | copy-done | bytes 393240
  5.4 0.0 copy-start.2
  5.4 0.8 %copy-done.2 = bf16[32,768]{1,0:T(8,128)(2,1)S(1)} copy-done((bf16[32,768]{1,0:T(8,128)(2,1)S(1)}, bf16[32,768]{1,0:T(8,128)(2,1)}, u32[]{:S(2)}) %copy-start.2) | copy-done | bytes 49176
  6.2 4.7 %first_block.1 = (bf16[128,384]{1,0:T(8,128)(2,1)S(1)}, bf16[128,384]{1,0:T(8,128)(2,1)S(1)}, f32[6,160,128]{2,1,0:T(8,128)S(1)}, bf16[2,1536,768]{2,1,0:T(8,128...) custom-call(s32[1]{0:T(128)S(6)} %copy.12.lengths_ref, bf16[1,128,1536]{2,1,0:T(8,128)(2,1)S(1)} %copy-done.1, ...), custom_call_target="tpu_custom_call" | custom-call | tf_op jit(solution)/shard_map/first_block/pallas_call | solution.py:377
  10.9 0.1 collective-permute-start.1
  11.0 1.3 %collective-permute-done.rows_ref = bf16[128,1536]{1,0:T(8,128)(2,1)S(1)} collective-permute-done((bf16[128,1536]{1,0:T(8,128)(2,1)}, bf16[128,1536]{1,0:T(8,128)(2,1)S(1)}, u32[]{:S(2)}, u32[]{:S(2)}) %collective-permute-start) | collective-permute-done | bytes 393248 | tf_op jit(solution)/shard_map/ppermute | solution.py:399
  12.3 3.3 %last_block.1 = (bf16[128,768]{1,0:T(8,128)(2,1)}, bf16[176,384]{1,0:T(8,128)(2,1)S(1)}, bf16[32,2,1280]{2,1,0:T(2,128)(2,1)}, f32[72,6,128,128]{3,2,1,0:T(8,128)}) custom-call(s32[1]{0:T(128)S(6)} %copy.12.lengths_ref, bf16[128,1536]{1,0:T(8,128)(2,1)S(1)} %collective-permute-done.rows_ref, ...), custom_call_target="tpu_custom_call", output_to_operand_aliasing={{3}: (8, {})} | custom-call | tf_op jit(solution)/shard_map/last_block/pallas_call | solution.py:377
  15.6 0.0 collective-permute-done.1.soon_ref
  15.6 6.4 %all-to-all-start = ((bf16[32,2,1280]{2,1,0:T(2,128)(2,1)}), bf16[32,2,1280]{2,1,0:T(2,128)(2,1)S(1)}, u32[]{:S(2)}, u32[]{:S(2)}) async-start(bf16[32,2,1280]{2,1,0:T(2,128)(2,1)} %get-tuple-element.30), calls=%async_computation | async-start | bytes 327680 | tf_op jit(solution)/shard_map/all_to_all | solution.py:463
  22.0 1.8 %collective-permute-start.3 = (bf16[176,384]{1,0:T(8,128)(2,1)S(1)}, bf16[176,384]{1,0:T(8,128)(2,1)S(1)}, u32[]{:S(2)}, u32[]{:S(2)}) collective-permute-start(bf16[176,384]{1,0:T(8,128)(2,1)S(1)} %get-tuple-element.32), channel_id=1, source_target_pairs={{0,1},{1,0},{2,3},{3,2},{4,5},{5,4},{6,7},{7,6},{8,9},{9,8},{10,11... | collective-permute-start | bytes 405512 | tf_op jit(solution)/shard_map/ppermute | solution.py:399
  23.9 0.3 collective-permute-start.2
  24.1 0.0 copy-start
  24.1 1.7 %copy-done = bf16[768,1536]{1,0:T(8,128)(2,1)S(1)} copy-done((bf16[768,1536]{1,0:T(8,128)(2,1)S(1)}, bf16[768,1536]{1,0:T(8,128)(2,1)}, u32[]{:S(2)}) %copy-start) | copy-done | bytes 2359320
  25.8 1.0 %turn.1 = (bf16[2,768,768]{2,1,0:T(8,128)(2,1)S(1)}, f32[6,128,128]{2,1,0:T(8,128)S(1)}, f32[2,768]{1,0:T(2,128)S(1)}) custom-call(bf16[768,1536]{1,0:T(8,128)(2,1)S(1)} %copy-done, f32[6,768]{1,0:T(8,128)S(1)} %reshape.6.vectors_ref, f32[72,6,128,128]{3,2,1,0:T(8,128)} %get-tuple-element.34.store_ref), custom_call_target="tpu_custom_call" | custom-call | tf_op jit(solution)/shard_map/turn/pallas_call | solution.py:377
  26.8 3.1 %collective-permute-done.3.tail_ref = bf16[176,384]{1,0:T(8,128)(2,1)S(1)} collective-permute-done((bf16[176,384]{1,0:T(8,128)(2,1)S(1)}, bf16[176,384]{1,0:T(8,128)(2,1)S(1)}, u32[]{:S(2)}, u32[]{:S(2)}) %collective-permute-start.3) | collective-permute-done | bytes 135200 | tf_op jit(solution)/shard_map/ppermute | solution.py:399
  29.9 0.9 %all-to-all-done = bf16[32,2,1280]{2,1,0:T(2,128)(2,1)S(1)} async-done(((bf16[32,2,1280]{2,1,0:T(2,128)(2,1)}), bf16[32,2,1280]{2,1,0:T(2,128)(2,1)S(1)}, u32[]{:S(2)}, u32[]{:S(2)}) %all-to-all-start) | async-done | bytes 163872 | tf_op jit(solution)/shard_map/all_to_all | solution.py:463
  30.8 0.9 %branch_sent.1 = bf16[128,768]{1,0:T(8,128)(2,1)S(1)} custom-call(bf16[16,2,2,1280]{3,2,1,0:T(2,128)(2,1)S(1)} %bitcast.3, f32[6,128,128]{2,1,0:T(8,128)S(1)} %get-tuple-element.39.conv_ref, bf16[128,384]{1,0:T(8,128)(2,1)S(1)} %collective-permute-done.1.soon_ref, bf16[176,384]{1,0:T(8,128)(2,1)S(1)} %collective-permute-done.3.tail_ref, ...), custom_call_target="tpu_custom_call" | custom-call | tf_op jit(solution)/shard_map/branch_sent/pallas_call | solution.py:377
  31.7 0.6 %collective-permute-start.4 = (bf16[128,768]{1,0:T(8,128)(2,1)S(1)}, bf16[128,768]{1,0:T(8,128)(2,1)S(1)}, u32[]{:S(2)}, u32[]{:S(2)}) collective-permute-start(bf16[128,768]{1,0:T(8,128)(2,1)S(1)} %branch_sent.1), channel_id=1, source_target_pairs={{0,1},{1,0},{2,3},{3,2},{4,5},{5,4},{6,7},{7,6},{8,9},{9,8},{10,11... | collective-permute-start | bytes 589832 | tf_op jit(solution)/shard_map/ppermute | solution.py:399
  32.3 1.5 %collective-permute-done.2.late_ref = bf16[128,768]{1,0:T(8,128)(2,1)S(1)} collective-permute-done((bf16[128,768]{1,0:T(8,128)(2,1)}, bf16[128,768]{1,0:T(8,128)(2,1)S(1)}, u32[]{:S(2)}, u32[]{:S(2)}) %collective-permute-start.2) | collective-permute-done | bytes 196640 | tf_op jit(solution)/shard_map/ppermute | solution.py:399
  33.8 1.6 %branch_kept.1 = (bf16[128,768]{1,0:T(8,128)(2,1)S(1)}, f32[6,128,128]{2,1,0:T(8,128)S(1)}) custom-call(bf16[16,2,2,1280]{3,2,1,0:T(2,128)(2,1)S(1)} %bitcast.4, bf16[128,768]{1,0:T(8,128)(2,1)S(1)} %collective-permute-done.2.late_ref, bf16[176,384]{1,0:T(8,128)(2,1)S(1)} %collective-permute-done.3.tail_ref, f32[2,768]{1,0:T(2,128)S(1)} %get-tuple-element.35.norms_ref, ...), custom_call_target="tpu_custom_call" | custom-call | tf_op jit(solution)/shard_map/branch_kept/pallas_call | solution.py:377
  35.4 2.6 %collective-permute-done.4.got_ref = bf16[128,768]{1,0:T(8,128)(2,1)S(1)} collective-permute-done((bf16[128,768]{1,0:T(8,128)(2,1)S(1)}, bf16[128,768]{1,0:T(8,128)(2,1)S(1)}, u32[]{:S(2)}, u32[]{:S(2)}) %collective-permute-start.4) | collective-permute-done | bytes 196640 | tf_op jit(solution)/shard_map/ppermute | solution.py:399
  38.0 0.8 %residual.1 = bf16[128,1536]{1,0:T(8,128)(2,1)} custom-call(bf16[128,768]{1,0:T(8,128)(2,1)S(1)} %get-tuple-element.37.mine_ref, f32[6,128,128]{2,1,0:T(8,128)S(1)} %get-tuple-element.38.base_ref, bf16[128,768]{1,0:T(8,128)(2,1)S(1)} %collective-permute-done.4.got_ref), custom_call_target="tpu_custom_call" | custom-call | tf_op jit(solution)/shard_map/residual/pallas_call | solution.py:377
  (1 shorter events, 0.0 us)
Async XLA Ops:
  0.0 12.3 %collective-permute-start = (bf16[128,1536]{1,0:T(8,128)(2,1)}, bf16[128,1536]{1,0:T(8,128)(2,1)S(1)}, u32[]{:S(2)}, u32[]{:S(2)}) collective-permute-start(bf16[128,1536]{1,0:T(8,128)(2,1)} %bitcast.5), channel_id=1, source_target_pairs={{0,1},{1,0},{2,3},{3,2},{4,5},{5,4},{6,7},{7,6},{8,9},{9,8},{10,11... | collective-permute-start | bytes 1179656 | tf_op jit(solution)/shard_map/ppermute | solution.py:399
  4.4 1.0 %copy-start.1 = (bf16[1,128,1536]{2,1,0:T(8,128)(2,1)S(1)}, bf16[1,128,1536]{2,1,0:T(8,128)(2,1)}, u32[]{:S(2)}) copy-start(bf16[1,128,1536]{2,1,0:T(8,128)(2,1)} %frames_ref.1) | copy-start | bytes 1179652
  5.4 0.8 %copy-start.2 = (bf16[32,768]{1,0:T(8,128)(2,1)S(1)}, bf16[32,768]{1,0:T(8,128)(2,1)}, u32[]{:S(2)}) copy-start(bf16[32,768]{1,0:T(8,128)(2,1)} %taps_ref.3) | copy-start | bytes 147460
  10.9 4.7 %collective-permute-start.1 = (bf16[128,384]{1,0:T(8,128)(2,1)S(1)}, bf16[128,384]{1,0:T(8,128)(2,1)S(1)}, u32[]{:S(2)}, u32[]{:S(2)}) collective-permute-start(bf16[128,384]{1,0:T(8,128)(2,1)S(1)} %get-tuple-element.29), channel_id=1, source_target_pairs={{0,1},{1,0},{2,3},{3,2},{4,5},{5,4},{6,7},{7,6},{8,9},{9,8},{10,11... | collective-permute-start | bytes 294920 | tf_op jit(solution)/shard_map/ppermute | solution.py:399
  15.6 15.2 %all-to-all-start = ((bf16[32,2,1280]{2,1,0:T(2,128)(2,1)}), bf16[32,2,1280]{2,1,0:T(2,128)(2,1)S(1)}, u32[]{:S(2)}, u32[]{:S(2)}) async-start(bf16[32,2,1280]{2,1,0:T(2,128)(2,1)} %get-tuple-element.30), calls=%async_computation | async-start | bytes 327680 | tf_op jit(solution)/shard_map/all_to_all | solution.py:463
  22.0 7.8 %collective-permute-start.3 = (bf16[176,384]{1,0:T(8,128)(2,1)S(1)}, bf16[176,384]{1,0:T(8,128)(2,1)S(1)}, u32[]{:S(2)}, u32[]{:S(2)}) collective-permute-start(bf16[176,384]{1,0:T(8,128)(2,1)S(1)} %get-tuple-element.32), channel_id=1, source_target_pairs={{0,1},{1,0},{2,3},{3,2},{4,5},{5,4},{6,7},{7,6},{8,9},{9,8},{10,11... | collective-permute-start | bytes 405512 | tf_op jit(solution)/shard_map/ppermute | solution.py:399
  23.9 9.9 %collective-permute-start.2 = (bf16[128,768]{1,0:T(8,128)(2,1)}, bf16[128,768]{1,0:T(8,128)(2,1)S(1)}, u32[]{:S(2)}, u32[]{:S(2)}) collective-permute-start(bf16[128,768]{1,0:T(8,128)(2,1)} %get-tuple-element.31), channel_id=1, source_target_pairs={{0,1},{1,0},{2,3},{3,2},{4,5},{5,4},{6,7},{7,6},{8,9},{9,8},{10,11... | collective-permute-start | bytes 589832 | tf_op jit(solution)/shard_map/ppermute | solution.py:399
  24.1 1.7 %copy-start = (bf16[768,1536]{1,0:T(8,128)(2,1)S(1)}, bf16[768,1536]{1,0:T(8,128)(2,1)}, u32[]{:S(2)}) copy-start(bf16[768,1536]{1,0:T(8,128)(2,1)} %weight_ref.2) | copy-start | bytes 7077892
  31.7 6.3 %collective-permute-start.4 = (bf16[128,768]{1,0:T(8,128)(2,1)S(1)}, bf16[128,768]{1,0:T(8,128)(2,1)S(1)}, u32[]{:S(2)}, u32[]{:S(2)}) collective-permute-start(bf16[128,768]{1,0:T(8,128)(2,1)S(1)} %branch_sent.1), channel_id=1, source_target_pairs={{0,1},{1,0},{2,3},{3,2},{4,5},{5,4},{6,7},{7,6},{8,9},{9,8},{10,11... | collective-permute-start | bytes 589832 | tf_op jit(solution)/shard_map/ppermute | solution.py:399

commit v8 on v7

--- a/solution.py
+++ b/solution.py
@@ -13,6 +13,7 @@
 HALO = 16
 EDGE = 8
 KEPT, SENT, HALF, OTHER, BLOCKS = 0, 1, 2, 3, 72
+FOLDS = 3
 EXTRA = 8
 F32 = jnp.float32
 BF16 = jnp.bfloat16
@@ -103,9 +104,15 @@
     return total
 
 
-def half_lanes(tile, tiles):
-    half, place = divmod(tile, tiles // 2)
-    return half, slice(place * LANES, (place + 1) * LANES)
+def part_lanes(tile, tiles):
+    soon = tiles - tiles // FOLDS
+    place = tile if tile < soon else tile - soon
+    return int(tile >= soon), slice(place * LANES, (place + 1) * LANES)
+
+
+def folded(rows):
+    wide = rows.shape[1] // FOLDS
+    return jnp.concatenate([rows[:, at * wide : (at + 1) * wide] for at in range(FOLDS)])
 
 
 def first_block_kernel(
@@ -159,8 +166,8 @@
             pivot = jnp.sum(conv * valid, axis=0, keepdims=True) / valid_count
             pivot = pivot.astype(BF16).astype(F32)
             pivot_ref[:, lanes] = pivot
-            half, there = half_lanes(tile, tiles)
-            (soon_ref, later_ref)[half][:, there] = (conv - pivot).astype(BF16)
+            part, there = part_lanes(tile, tiles)
+            (soon_ref, later_ref)[part][:, there] = (conv - pivot).astype(BF16)
     base_copy.wait()
 
 
@@ -187,7 +194,6 @@
     extra = three_parts(vectors_ref[last : last + 1, :])
     extra += three_parts(vectors_ref[last + 1 : last + 2, :])
     extra.append(pivot_ref[...])
-    wide = chans // 2
     tail_ref[0:rows, :] = later_ref[...]
     means = []
     normed = layer_norm(rows_ref[...], *affine(vectors_ref))
@@ -217,8 +223,9 @@
                 copies[-1].start()
             pivot = pivot_ref[:, lanes]
             near = (near - pivot).astype(BF16)
-            half, there = half_lanes(tile, tiles)
-            tail_ref[rows + half * HALO : rows + (half + 1) * HALO, there] = near
+            fold, there = divmod(tile, tiles // FOLDS)
+            there = slice(there * LANES, (there + 1) * LANES)
+            tail_ref[rows + fold * HALO : rows + (fold + 1) * HALO, there] = near
             mean = jnp.sum(kept * mask_ref[0] + sent * mask_ref[1], axis=0, keepdims=True)
             mean = mean / count
             high = mean.astype(BF16)
@@ -246,7 +253,7 @@
     copies.append(pltpu.make_async_copy(stats_ref, spread_ref, stats_sem))
     copies[-1].start()
     extra = jnp.concatenate(extra + [jnp.concatenate(means, axis=1)])
-    tail_ref[rows + 2 * HALO :, :] = jnp.concatenate([extra[:, :wide], extra[:, wide:]]).astype(BF16)
+    tail_ref[rows + FOLDS * HALO :, :] = folded(extra).astype(BF16)
     for copy in copies:
         copy.wait()
 
@@ -272,30 +279,42 @@
 
 
 def peer_vectors(tail_ref):
-    first = tail_ref.shape[0] - 2 * EXTRA
+    first = tail_ref.shape[0] - FOLDS * EXTRA
     parts = tail_ref[first:, :].astype(F32)
-    parts = jnp.concatenate([parts[:EXTRA], parts[EXTRA:]], axis=1)
+    parts = jnp.concatenate([parts[at * EXTRA : (at + 1) * EXTRA] for at in range(FOLDS)], axis=1)
     gain, bias = (parts[at : at + 1] + (parts[at + 1 : at + 2] + parts[at + 2 : at + 3]) for at in (0, 3))
     return gain, bias, parts[6:7], parts[7:8]
 
 
 def scales(stats_ref, norms_ref, tail_ref, kept):
     chans = norms_ref.shape[1]
+    half = chans // 2
+    spans = stats_ref.shape[0]
     gain, bias, *pivots = peer_vectors(tail_ref)
     norms = [(norms_ref[0:1, :], norms_ref[1:2, :], 0.0), (gain, bias, pivots[kept])]
-    half = chans // 2
     own = lax.axis_index("tensor")
+    seen = stats_ref[...].reshape(4 * spans, stats_ref.shape[3])
+    picked = lax.broadcasted_iota(jnp.int32, (2 * spans, 4 * spans), 0)
+    given = lax.broadcasted_iota(jnp.int32, (2 * spans, 4 * spans), 1)
+    place = jnp.where(picked < spans, 1 - own, own)
+    first = 4 * lax.rem(picked, spans) + 2 * place
+    upper, lower = (given == first).astype(F32), (given == first + 1).astype(F32)
+
+    def pick(rows, lanes):
+        return jnp.dot(rows.astype(BF16), seen[:, lanes], preferred_element_type=F32)
+
+    means = pick(upper + lower, slice(0, chans))
+    counts = pick(upper + lower, slice(chans + half, chans + half + LANES))[:, 0:1]
+    squares = slice(chans, chans + half)
+    squares = jnp.concatenate([pick(upper, squares), pick(lower, squares)], axis=1)
     found = []
-    for shift, place in enumerate((1 - own, own)):
-        seen = stats_ref[:, pl.ds(place, 1), :, :].astype(F32)
-        both = seen[:, :, 0:1, :] + seen[:, :, 1:2, :]
-        means, counts = both[..., :chans], both[..., chans + half : chans + half + 1]
-        squares = jnp.concatenate([seen[:, :, at : at + 1, chans : chans + half] for at in range(2)], axis=-1)
-        count = jnp.sum(counts, axis=0)[0]
-        mean = jnp.sum(means * counts, axis=0)[0] / count
-        off = means - mean
-        var = jnp.sum(squares + counts * off * off, axis=0)[0] / count
-        gain, bias, pivot = norms[shift]
+    for shift, (gain, bias, pivot) in enumerate(norms):
+        rows = slice(shift * spans, (shift + 1) * spans)
+        weight = counts[rows]
+        count = jnp.sum(weight, axis=0, keepdims=True)
+        mean = jnp.sum(means[rows] * weight, axis=0, keepdims=True) / count
+        off = means[rows] - mean
+        var = jnp.sum(squares[rows] + weight * off * off, axis=0, keepdims=True) / count
         found.append((mean - pivot, lax.rsqrt(var + 1e-05) * gain, bias))
     return found
 
@@ -322,8 +341,10 @@
     target = pl.multiple_of(jnp.where(lax.axis_index("tensor") == 0, 0, rows - HALO), HALO)
     peer_ref[:, :wide] = soon_ref[...]
     peer_ref[:, wide:] = tail_ref[0:rows, :]
-    peer_ref[pl.ds(target, HALO), :wide] = tail_ref[rows : rows + HALO, :]
-    peer_ref[pl.ds(target, HALO), wide:] = tail_ref[rows + HALO : rows + 2 * HALO, :]
+    wide = tail_ref.shape[1]
+    for at in range(FOLDS):
+        near = tail_ref[rows + at * HALO : rows + (at + 1) * HALO, :]
+        peer_ref[pl.ds(target, HALO), at * wide : (at + 1) * wide] = near
     found = scales(stats_ref, norms_ref, tail_ref, 0)
     branch = branch_rows(found, conv_ref, peer_ref, weight_ref)
     out_ref[...] = branch.astype(BF16)
@@ -409,8 +430,8 @@
     soon, later, first_sums, held, pivot, store_first = call(
         first_block_kernel,
         (
-            shape((span, chans // 2), BF16),
-            shape((span, chans // 2), BF16),
+            shape((span, chans - chans // FOLDS), BF16),
+            shape((span, chans // FOLDS), BF16),
             reach,
             shape((2, width, chans), BF16),
             shape((1, chans), F32),
@@ -437,7 +458,7 @@
         last_block_kernel,
         (
             shape((span, chans), BF16),
-            shape((span + 2 * HALO + 2 * EXTRA, chans // 2), BF16),
+            shape((span + FOLDS * (HALO + EXTRA), chans // FOLDS), BF16),
             shape((devices, 2, chans + chans // 2 + LANES), BF16),
             store,
         ),

time: 39.2 us -> 39 us (level)
  starting transfers between devices: 12.2 us -> 11.8 us
    all_to_all x1, waiting for transfers between devices: 0.94 us -> 1.89 us  [two_parts(): lax.all_to_all(spread, ('dp', 'tensor'), split_axis=0, concat_axis=0, til...]
    ppermute x5, waiting for transfers between devices: 8.53 us -> 7.9 us  [swap(): return lax.ppermute(value, 'tensor', [(0, 1), (1, 0)])]
  transfers between devices with their start and end apart: 6 -> 6, of which waited for: 5 -> 6; matrix products, arithmetic and copies ran while one was open for 2% -> 2% of each run, Pallas kernels for 29% -> 29%
where the time goes in v8:
time: 39 us; the launch traced here: 38.6 us
  Pallas kernels  12.1 us (31%)
  starting transfers between devices  11.8 us (30%)
  waiting for transfers between devices  9.79 us (25%)
  local copies, waits for them, and re-layouts  3.46 us (9%)
  other arithmetic  0.76 us (2%)
  between operations  0.72 us (2%)
    pallas_call x6, Pallas kernels, call(): pl.pallas_call(kernel, out_shape=tuple(outs), in_specs=list(in_specs), ou...  12.1 us
    ppermute x5, waiting for transfers between devices, swap(): return lax.ppermute(value, 'tensor', [(0, 1), (1, 0)])  7.9 us
    all_to_all x1, starting transfers between devices, two_parts(): lax.all_to_all(spread, ('dp', 'tensor'), split_axis=0, concat_axis=0, til...  6.08 us
    ppermute x5, starting transfers between devices, swap(): return lax.ppermute(value, 'tensor', [(0, 1), (1, 0)])  5.74 us
    unnamed x6, local copies, waits for them, and re-layouts  3.45 us
    all_to_all x1, waiting for transfers between devices, two_parts(): lax.all_to_all(spread, ('dp', 'tensor'), split_axis=0, concat_axis=0, til...  1.89 us
  transfers between devices with their start and end apart: 6, of which 6 were waited for; matrix products, arithmetic and copies ran while one was open for 2% of the time, Pallas kernels for 29%

profile of v8, /device:TPU:0, one launch (start us, length us, event | category | flops | bytes accessed | tf_op | source)
XLA Modules:
  0.0 38.6 jit_solution(9609153986229225386)
XLA Ops:
  0.0 3.0 %collective-permute-start = (bf16[128,1536]{1,0:T(8,128)(2,1)}, bf16[128,1536]{1,0:T(8,128)(2,1)S(1)}, u32[]{:S(2)}, u32[]{:S(2)}) collective-permute-start(bf16[128,1536]{1,0:T(8,128)(2,1)} %bitcast.5), channel_id=1, source_target_pairs={{0,1},{1,0},{2,3},{3,2},{4,5},{5,4},{6,7},{7,6},{8,9},{9,8},{10,11... | collective-permute-start | bytes 1179656 | tf_op jit(solution)/shard_map/ppermute | solution.py:420
  3.6 0.8 %pad_maximum_fusion = f32[4608]{0:T(1024)S(1)} fusion(f32[768]{0:T(1024)} %param.16, f32[768]{0:T(1024)} %param.15, f32[1536]{0:T(1024)} %param.12, f32[1536]{0:T(1024)} %param.11), kind=kLoop, calls=%fused_computation | loop fusion | flops 13824 | bytes 36864 | tf_op jit(solution)/shard_map/concatenate | solution.py:423
  4.4 0.0 copy-start.1
  4.4 1.0 %copy-done.1 = bf16[1,128,1536]{2,1,0:T(8,128)(2,1)S(1)} copy-done((bf16[1,128,1536]{2,1,0:T(8,128)(2,1)S(1)}, bf16[1,128,1536]{2,1,0:T(8,128)(2,1)}, u32[]{:S(2)}) %copy-start.1) | copy-done | bytes 393240
  5.4 0.0 copy-start.2
  5.4 0.8 %copy-done.2 = bf16[32,768]{1,0:T(8,128)(2,1)S(1)} copy-done((bf16[32,768]{1,0:T(8,128)(2,1)S(1)}, bf16[32,768]{1,0:T(8,128)(2,1)}, u32[]{:S(2)}) %copy-start.2) | copy-done | bytes 49176
  6.2 4.7 %first_block.1 = (bf16[128,512]{1,0:T(8,128)(2,1)S(1)}, bf16[128,256]{1,0:T(8,128)(2,1)S(1)}, f32[6,160,128]{2,1,0:T(8,128)S(1)}, bf16[2,1536,768]{2,1,0:T(8,128...) custom-call(s32[1]{0:T(128)S(6)} %copy.12.lengths_ref, bf16[1,128,1536]{2,1,0:T(8,128)(2,1)S(1)} %copy-done.1, ...), custom_call_target="tpu_custom_call" | custom-call | tf_op jit(solution)/shard_map/first_block/pallas_call | solution.py:398
  10.9 0.1 collective-permute-start.1
  11.0 1.3 %collective-permute-done.rows_ref = bf16[128,1536]{1,0:T(8,128)(2,1)S(1)} collective-permute-done((bf16[128,1536]{1,0:T(8,128)(2,1)}, bf16[128,1536]{1,0:T(8,128)(2,1)S(1)}, u32[]{:S(2)}, u32[]{:S(2)}) %collective-permute-start) | collective-permute-done | bytes 393248 | tf_op jit(solution)/shard_map/ppermute | solution.py:420
  12.3 3.3 %last_block.1 = (bf16[128,768]{1,0:T(8,128)(2,1)}, bf16[200,256]{1,0:T(8,128)(2,1)S(1)}, bf16[32,2,1280]{2,1,0:T(2,128)(2,1)}, f32[72,6,128,128]{3,2,1,0:T(8,128)}) custom-call(s32[1]{0:T(128)S(6)} %copy.12.lengths_ref, bf16[128,1536]{1,0:T(8,128)(2,1)S(1)} %collective-permute-done.rows_ref, ...), custom_call_target="tpu_custom_call", output_to_operand_aliasing={{3}: (8, {})} | custom-call | tf_op jit(solution)/shard_map/last_block/pallas_call | solution.py:398
  15.6 0.4 collective-permute-done.1.soon_ref
  15.9 6.1 %all-to-all-start = ((bf16[32,2,1280]{2,1,0:T(2,128)(2,1)}), bf16[32,2,1280]{2,1,0:T(2,128)(2,1)S(1)}, u32[]{:S(2)}, u32[]{:S(2)}) async-start(bf16[32,2,1280]{2,1,0:T(2,128)(2,1)} %get-tuple-element.30), calls=%async_computation | async-start | bytes 327680 | tf_op jit(solution)/shard_map/all_to_all | solution.py:484
  22.0 1.8 %collective-permute-start.3 = (bf16[200,256]{1,0:T(8,128)(2,1)S(1)}, bf16[200,256]{1,0:T(8,128)(2,1)S(1)}, u32[]{:S(2)}, u32[]{:S(2)}) collective-permute-start(bf16[200,256]{1,0:T(8,128)(2,1)S(1)} %get-tuple-element.32), channel_id=1, source_target_pairs={{0,1},{1,0},{2,3},{3,2},{4,5},{5,4},{6,7},{7,6},{8,9},{9,8},{10,11... | collective-permute-start | bytes 307208 | tf_op jit(solution)/shard_map/ppermute | solution.py:420
  23.8 0.3 collective-permute-start.2
  24.1 0.0 copy-start
  24.1 1.7 %copy-done = bf16[768,1536]{1,0:T(8,128)(2,1)S(1)} copy-done((bf16[768,1536]{1,0:T(8,128)(2,1)S(1)}, bf16[768,1536]{1,0:T(8,128)(2,1)}, u32[]{:S(2)}) %copy-start) | copy-done | bytes 2359320
  25.8 1.0 %turn.1 = (bf16[2,768,768]{2,1,0:T(8,128)(2,1)S(1)}, f32[6,128,128]{2,1,0:T(8,128)S(1)}, f32[2,768]{1,0:T(2,128)S(1)}) custom-call(bf16[768,1536]{1,0:T(8,128)(2,1)S(1)} %copy-done, f32[6,768]{1,0:T(8,128)S(1)} %reshape.6.vectors_ref, f32[72,6,128,128]{3,2,1,0:T(8,128)} %get-tuple-element.34.store_ref), custom_call_target="tpu_custom_call" | custom-call | tf_op jit(solution)/shard_map/turn/pallas_call | solution.py:398
  26.8 2.1 %collective-permute-done.3.tail_ref = bf16[200,256]{1,0:T(8,128)(2,1)S(1)} collective-permute-done((bf16[200,256]{1,0:T(8,128)(2,1)S(1)}, bf16[200,256]{1,0:T(8,128)(2,1)S(1)}, u32[]{:S(2)}, u32[]{:S(2)}) %collective-permute-start.3) | collective-permute-done | bytes 102432 | tf_op jit(solution)/shard_map/ppermute | solution.py:420
  28.9 1.9 %all-to-all-done = bf16[32,2,1280]{2,1,0:T(2,128)(2,1)S(1)} async-done(((bf16[32,2,1280]{2,1,0:T(2,128)(2,1)}), bf16[32,2,1280]{2,1,0:T(2,128)(2,1)S(1)}, u32[]{:S(2)}, u32[]{:S(2)}) %all-to-all-start) | async-done | bytes 163872 | tf_op jit(solution)/shard_map/all_to_all | solution.py:484
  30.8 0.7 %branch_sent.1 = bf16[128,768]{1,0:T(8,128)(2,1)S(1)} custom-call(bf16[16,2,2,1280]{3,2,1,0:T(2,128)(2,1)S(1)} %bitcast.3, f32[6,128,128]{2,1,0:T(8,128)S(1)} %get-tuple-element.39.conv_ref, bf16[128,512]{1,0:T(8,128)(2,1)S(1)} %collective-permute-done.1.soon_ref, bf16[200,256]{1,0:T(8,128)(2,1)S(1)} %collective-permute-done.3.tail_ref, ...), custom_call_target="tpu_custom_call" | custom-call | tf_op jit(solution)/shard_map/branch_sent/pallas_call | solution.py:398
  31.5 0.6 %collective-permute-start.4 = (bf16[128,768]{1,0:T(8,128)(2,1)S(1)}, bf16[128,768]{1,0:T(8,128)(2,1)S(1)}, u32[]{:S(2)}, u32[]{:S(2)}) collective-permute-start(bf16[128,768]{1,0:T(8,128)(2,1)S(1)} %branch_sent.1), channel_id=1, source_target_pairs={{0,1},{1,0},{2,3},{3,2},{4,5},{5,4},{6,7},{7,6},{8,9},{9,8},{10,11... | collective-permute-start | bytes 589832 | tf_op jit(solution)/shard_map/ppermute | solution.py:420
  32.2 0.9 %collective-permute-done.2.late_ref = bf16[128,768]{1,0:T(8,128)(2,1)S(1)} collective-permute-done((bf16[128,768]{1,0:T(8,128)(2,1)}, bf16[128,768]{1,0:T(8,128)(2,1)S(1)}, u32[]{:S(2)}, u32[]{:S(2)}) %collective-permute-start.2) | collective-permute-done | bytes 196640 | tf_op jit(solution)/shard_map/ppermute | solution.py:420
  33.1 1.6 %branch_kept.1 = (bf16[128,768]{1,0:T(8,128)(2,1)S(1)}, f32[6,128,128]{2,1,0:T(8,128)S(1)}) custom-call(bf16[16,2,2,1280]{3,2,1,0:T(2,128)(2,1)S(1)} %bitcast.4, bf16[128,768]{1,0:T(8,128)(2,1)S(1)} %collective-permute-done.2.late_ref, bf16[200,256]{1,0:T(8,128)(2,1)S(1)} %collective-permute-done.3.tail_ref, f32[2,768]{1,0:T(2,128)S(1)} %get-tuple-element.35.norms_ref, ...), custom_call_target="tpu_custom_call" | custom-call | tf_op jit(solution)/shard_map/branch_kept/pallas_call | solution.py:398
  34.7 3.2 %collective-permute-done.4.got_ref = bf16[128,768]{1,0:T(8,128)(2,1)S(1)} collective-permute-done((bf16[128,768]{1,0:T(8,128)(2,1)S(1)}, bf16[128,768]{1,0:T(8,128)(2,1)S(1)}, u32[]{:S(2)}, u32[]{:S(2)}) %collective-permute-start.4) | collective-permute-done | bytes 196640 | tf_op jit(solution)/shard_map/ppermute | solution.py:420
  37.8 0.8 %residual.1 = bf16[128,1536]{1,0:T(8,128)(2,1)} custom-call(bf16[128,768]{1,0:T(8,128)(2,1)S(1)} %get-tuple-element.37.mine_ref, f32[6,128,128]{2,1,0:T(8,128)S(1)} %get-tuple-element.38.base_ref, bf16[128,768]{1,0:T(8,128)(2,1)S(1)} %collective-permute-done.4.got_ref), custom_call_target="tpu_custom_call" | custom-call | tf_op jit(solution)/shard_map/residual/pallas_call | solution.py:398
  (1 shorter events, 0.0 us)
Async XLA Ops:
  0.0 12.3 %collective-permute-start = (bf16[128,1536]{1,0:T(8,128)(2,1)}, bf16[128,1536]{1,0:T(8,128)(2,1)S(1)}, u32[]{:S(2)}, u32[]{:S(2)}) collective-permute-start(bf16[128,1536]{1,0:T(8,128)(2,1)} %bitcast.5), channel_id=1, source_target_pairs={{0,1},{1,0},{2,3},{3,2},{4,5},{5,4},{6,7},{7,6},{8,9},{9,8},{10,11... | collective-permute-start | bytes 1179656 | tf_op jit(solution)/shard_map/ppermute | solution.py:420
  4.4 1.0 %copy-start.1 = (bf16[1,128,1536]{2,1,0:T(8,128)(2,1)S(1)}, bf16[1,128,1536]{2,1,0:T(8,128)(2,1)}, u32[]{:S(2)}) copy-start(bf16[1,128,1536]{2,1,0:T(8,128)(2,1)} %frames_ref.1) | copy-start | bytes 1179652
  5.4 0.8 %copy-start.2 = (bf16[32,768]{1,0:T(8,128)(2,1)S(1)}, bf16[32,768]{1,0:T(8,128)(2,1)}, u32[]{:S(2)}) copy-start(bf16[32,768]{1,0:T(8,128)(2,1)} %taps_ref.3) | copy-start | bytes 147460
  10.9 5.0 %collective-permute-start.1 = (bf16[128,512]{1,0:T(8,128)(2,1)S(1)}, bf16[128,512]{1,0:T(8,128)(2,1)S(1)}, u32[]{:S(2)}, u32[]{:S(2)}) collective-permute-start(bf16[128,512]{1,0:T(8,128)(2,1)S(1)} %get-tuple-element.29), channel_id=1, source_target_pairs={{0,1},{1,0},{2,3},{3,2},{4,5},{5,4},{6,7},{7,6},{8,9},{9,8},{10,11... | collective-permute-start | bytes 393224 | tf_op jit(solution)/shard_map/ppermute | solution.py:420
  15.9 14.9 %all-to-all-start = ((bf16[32,2,1280]{2,1,0:T(2,128)(2,1)}), bf16[32,2,1280]{2,1,0:T(2,128)(2,1)S(1)}, u32[]{:S(2)}, u32[]{:S(2)}) async-start(bf16[32,2,1280]{2,1,0:T(2,128)(2,1)} %get-tuple-element.30), calls=%async_computation | async-start | bytes 327680 | tf_op jit(solution)/shard_map/all_to_all | solution.py:484
  22.0 6.9 %collective-permute-start.3 = (bf16[200,256]{1,0:T(8,128)(2,1)S(1)}, bf16[200,256]{1,0:T(8,128)(2,1)S(1)}, u32[]{:S(2)}, u32[]{:S(2)}) collective-permute-start(bf16[200,256]{1,0:T(8,128)(2,1)S(1)} %get-tuple-element.32), channel_id=1, source_target_pairs={{0,1},{1,0},{2,3},{3,2},{4,5},{5,4},{6,7},{7,6},{8,9},{9,8},{10,11... | collective-permute-start | bytes 307208 | tf_op jit(solution)/shard_map/ppermute | solution.py:420
  23.8 9.2 %collective-permute-start.2 = (bf16[128,768]{1,0:T(8,128)(2,1)}, bf16[128,768]{1,0:T(8,128)(2,1)S(1)}, u32[]{:S(2)}, u32[]{:S(2)}) collective-permute-start(bf16[128,768]{1,0:T(8,128)(2,1)} %get-tuple-element.31), channel_id=1, source_target_pairs={{0,1},{1,0},{2,3},{3,2},{4,5},{5,4},{6,7},{7,6},{8,9},{9,8},{10,11... | collective-permute-start | bytes 589832 | tf_op jit(solution)/shard_map/ppermute | solution.py:420
  24.1 1.7 %copy-start = (bf16[768,1536]{1,0:T(8,128)(2,1)S(1)}, bf16[768,1536]{1,0:T(8,128)(2,1)}, u32[]{:S(2)}) copy-start(bf16[768,1536]{1,0:T(8,128)(2,1)} %weight_ref.2) | copy-start | bytes 7077892
  31.5 6.3 %collective-permute-start.4 = (bf16[128,768]{1,0:T(8,128)(2,1)S(1)}, bf16[128,768]{1,0:T(8,128)(2,1)S(1)}, u32[]{:S(2)}, u32[]{:S(2)}) collective-permute-start(bf16[128,768]{1,0:T(8,128)(2,1)S(1)} %branch_sent.1), channel_id=1, source_target_pairs={{0,1},{1,0},{2,3},{3,2},{4,5},{5,4},{6,7},{7,6},{8,9},{9,8},{10,11... | collective-permute-start | bytes 589832 | tf_op jit(solution)/shard_map/ppermute | solution.py:420

commit v9 on v8

--- a/solution.py
+++ b/solution.py
@@ -15,6 +15,7 @@
 KEPT, SENT, HALF, OTHER, BLOCKS = 0, 1, 2, 3, 72
 FOLDS = 3
 EXTRA = 8
+TAIL = 32
 F32 = jnp.float32
 BF16 = jnp.bfloat16
 
@@ -253,7 +254,9 @@
     copies.append(pltpu.make_async_copy(stats_ref, spread_ref, stats_sem))
     copies[-1].start()
     extra = jnp.concatenate(extra + [jnp.concatenate(means, axis=1)])
-    tail_ref[rows + FOLDS * HALO :, :] = folded(extra).astype(BF16)
+    extra = folded(extra)
+    spare = jnp.zeros((TAIL - extra.shape[0], extra.shape[1]), F32)
+    tail_ref[rows + FOLDS * HALO :, :] = jnp.concatenate([extra, spare]).astype(BF16)
     for copy in copies:
         copy.wait()
 
@@ -279,7 +282,7 @@
 
 
 def peer_vectors(tail_ref):
-    first = tail_ref.shape[0] - FOLDS * EXTRA
+    first = tail_ref.shape[0] - TAIL
     parts = tail_ref[first:, :].astype(F32)
     parts = jnp.concatenate([parts[at * EXTRA : (at + 1) * EXTRA] for at in range(FOLDS)], axis=1)
     gain, bias = (parts[at : at + 1] + (parts[at + 1 : at + 2] + parts[at + 2 : at + 3]) for at in (0, 3))
@@ -458,7 +461,7 @@
         last_block_kernel,
         (
             shape((span, chans), BF16),
-            shape((span + FOLDS * (HALO + EXTRA), chans // FOLDS), BF16),
+            shape((span + FOLDS * HALO + TAIL, chans // FOLDS), BF16),
             shape((devices, 2, chans + chans // 2 + LANES), BF16),
             store,
         ),

time: 39 us -> 39 us (level)
  no operation moved by 1% of the time
where the time goes in v9:
time: 39 us; the launch traced here: 38.6 us
  Pallas kernels  12.1 us (31%)
  starting transfers between devices  11.8 us (30%)
  waiting for transfers between devices  9.83 us (25%)
  local copies, waits for them, and re-layouts  3.46 us (9%)
  other arithmetic  0.76 us (2%)
  between operations  0.73 us (2%)
    pallas_call x6, Pallas kernels, call(): pl.pallas_call(kernel, out_shape=tuple(outs), in_specs=list(in_specs), ou...  12.1 us
    ppermute x5, waiting for transfers between devices, swap(): return lax.ppermute(value, 'tensor', [(0, 1), (1, 0)])  8.09 us
    all_to_all x1, starting transfers between devices, two_parts(): lax.all_to_all(spread, ('dp', 'tensor'), split_axis=0, concat_axis=0, til...  6.07 us
    ppermute x5, starting transfers between devices, swap(): return lax.ppermute(value, 'tensor', [(0, 1), (1, 0)])  5.73 us
    unnamed x6, local copies, waits for them, and re-layouts  3.45 us
    all_to_all x1, waiting for transfers between devices, two_parts(): lax.all_to_all(spread, ('dp', 'tensor'), split_axis=0, concat_axis=0, til...  1.73 us
  transfers between devices with their start and end apart: 6, of which 6 were waited for; matrix products, arithmetic and copies ran while one was open for 2% of the time, Pallas kernels for 29%

profile of v9, /device:TPU:0, one launch (start us, length us, event | category | flops | bytes accessed | tf_op | source)
XLA Modules:
  0.0 38.6 jit_solution(18026165925088599196)
XLA Ops:
  0.0 3.0 %collective-permute-start = (bf16[128,1536]{1,0:T(8,128)(2,1)}, bf16[128,1536]{1,0:T(8,128)(2,1)S(1)}, u32[]{:S(2)}, u32[]{:S(2)}) collective-permute-start(bf16[128,1536]{1,0:T(8,128)(2,1)} %bitcast.5), channel_id=1, source_target_pairs={{0,1},{1,0},{2,3},{3,2},{4,5},{5,4},{6,7},{7,6},{8,9},{9,8},{10,11... | collective-permute-start | bytes 1179656 | tf_op jit(solution)/shard_map/ppermute | solution.py:423
  3.6 0.8 %pad_maximum_fusion = f32[4608]{0:T(1024)S(1)} fusion(f32[768]{0:T(1024)} %param.16, f32[768]{0:T(1024)} %param.15, f32[1536]{0:T(1024)} %param.12, f32[1536]{0:T(1024)} %param.11), kind=kLoop, calls=%fused_computation | loop fusion | flops 13824 | bytes 36864 | tf_op jit(solution)/shard_map/concatenate | solution.py:426
  4.4 0.0 copy-start.1
  4.4 1.0 %copy-done.1 = bf16[1,128,1536]{2,1,0:T(8,128)(2,1)S(1)} copy-done((bf16[1,128,1536]{2,1,0:T(8,128)(2,1)S(1)}, bf16[1,128,1536]{2,1,0:T(8,128)(2,1)}, u32[]{:S(2)}) %copy-start.1) | copy-done | bytes 393240
  5.4 0.0 copy-start.2
  5.4 0.8 %copy-done.2 = bf16[32,768]{1,0:T(8,128)(2,1)S(1)} copy-done((bf16[32,768]{1,0:T(8,128)(2,1)S(1)}, bf16[32,768]{1,0:T(8,128)(2,1)}, u32[]{:S(2)}) %copy-start.2) | copy-done | bytes 49176
  6.2 4.7 %first_block.1 = (bf16[128,512]{1,0:T(8,128)(2,1)S(1)}, bf16[128,256]{1,0:T(8,128)(2,1)S(1)}, f32[6,160,128]{2,1,0:T(8,128)S(1)}, bf16[2,1536,768]{2,1,0:T(8,128...) custom-call(s32[1]{0:T(128)S(6)} %copy.12.lengths_ref, bf16[1,128,1536]{2,1,0:T(8,128)(2,1)S(1)} %copy-done.1, ...), custom_call_target="tpu_custom_call" | custom-call | tf_op jit(solution)/shard_map/first_block/pallas_call | solution.py:401
  10.9 0.1 collective-permute-start.1
  11.0 1.3 %collective-permute-done.rows_ref = bf16[128,1536]{1,0:T(8,128)(2,1)S(1)} collective-permute-done((bf16[128,1536]{1,0:T(8,128)(2,1)}, bf16[128,1536]{1,0:T(8,128)(2,1)S(1)}, u32[]{:S(2)}, u32[]{:S(2)}) %collective-permute-start) | collective-permute-done | bytes 393248 | tf_op jit(solution)/shard_map/ppermute | solution.py:423
  12.3 3.3 %last_block.1 = (bf16[128,768]{1,0:T(8,128)(2,1)}, bf16[208,256]{1,0:T(8,128)(2,1)S(1)}, bf16[32,2,1280]{2,1,0:T(2,128)(2,1)}, f32[72,6,128,128]{3,2,1,0:T(8,128)}) custom-call(s32[1]{0:T(128)S(6)} %copy.12.lengths_ref, bf16[128,1536]{1,0:T(8,128)(2,1)S(1)} %collective-permute-done.rows_ref, ...), custom_call_target="tpu_custom_call", output_to_operand_aliasing={{3}: (8, {})} | custom-call | tf_op jit(solution)/shard_map/last_block/pallas_call | solution.py:401
  15.6 0.4 collective-permute-done.1.soon_ref
  15.9 6.1 %all-to-all-start = ((bf16[32,2,1280]{2,1,0:T(2,128)(2,1)}), bf16[32,2,1280]{2,1,0:T(2,128)(2,1)S(1)}, u32[]{:S(2)}, u32[]{:S(2)}) async-start(bf16[32,2,1280]{2,1,0:T(2,128)(2,1)} %get-tuple-element.30), calls=%async_computation | async-start | bytes 327680 | tf_op jit(solution)/shard_map/all_to_all | solution.py:487
  22.0 1.8 %collective-permute-start.3 = (bf16[208,256]{1,0:T(8,128)(2,1)S(1)}, bf16[208,256]{1,0:T(8,128)(2,1)S(1)}, u32[]{:S(2)}, u32[]{:S(2)}) collective-permute-start(bf16[208,256]{1,0:T(8,128)(2,1)S(1)} %get-tuple-element.32), channel_id=1, source_target_pairs={{0,1},{1,0},{2,3},{3,2},{4,5},{5,4},{6,7},{7,6},{8,9},{9,8},{10,11... | collective-permute-start | bytes 319496 | tf_op jit(solution)/shard_map/ppermute | solution.py:423
  23.8 0.3 collective-permute-start.2
  24.1 0.0 copy-start
  24.1 1.7 %copy-done = bf16[768,1536]{1,0:T(8,128)(2,1)S(1)} copy-done((bf16[768,1536]{1,0:T(8,128)(2,1)S(1)}, bf16[768,1536]{1,0:T(8,128)(2,1)}, u32[]{:S(2)}) %copy-start) | copy-done | bytes 2359320
  25.8 1.0 %turn.1 = (bf16[2,768,768]{2,1,0:T(8,128)(2,1)S(1)}, f32[6,128,128]{2,1,0:T(8,128)S(1)}, f32[2,768]{1,0:T(2,128)S(1)}) custom-call(bf16[768,1536]{1,0:T(8,128)(2,1)S(1)} %copy-done, f32[6,768]{1,0:T(8,128)S(1)} %reshape.6.vectors_ref, f32[72,6,128,128]{3,2,1,0:T(8,128)} %get-tuple-element.34.store_ref), custom_call_target="tpu_custom_call" | custom-call | tf_op jit(solution)/shard_map/turn/pallas_call | solution.py:401
  26.8 2.3 %collective-permute-done.3.tail_ref = bf16[208,256]{1,0:T(8,128)(2,1)S(1)} collective-permute-done((bf16[208,256]{1,0:T(8,128)(2,1)S(1)}, bf16[208,256]{1,0:T(8,128)(2,1)S(1)}, u32[]{:S(2)}, u32[]{:S(2)}) %collective-permute-start.3) | collective-permute-done | bytes 106528 | tf_op jit(solution)/shard_map/ppermute | solution.py:423
  29.1 1.7 %all-to-all-done = bf16[32,2,1280]{2,1,0:T(2,128)(2,1)S(1)} async-done(((bf16[32,2,1280]{2,1,0:T(2,128)(2,1)}), bf16[32,2,1280]{2,1,0:T(2,128)(2,1)S(1)}, u32[]{:S(2)}, u32[]{:S(2)}) %all-to-all-start) | async-done | bytes 163872 | tf_op jit(solution)/shard_map/all_to_all | solution.py:487
  30.8 0.8 %branch_sent.1 = bf16[128,768]{1,0:T(8,128)(2,1)S(1)} custom-call(bf16[16,2,2,1280]{3,2,1,0:T(2,128)(2,1)S(1)} %bitcast.3, f32[6,128,128]{2,1,0:T(8,128)S(1)} %get-tuple-element.39.conv_ref, bf16[128,512]{1,0:T(8,128)(2,1)S(1)} %collective-permute-done.1.soon_ref, bf16[208,256]{1,0:T(8,128)(2,1)S(1)} %collective-permute-done.3.tail_ref, ...), custom_call_target="tpu_custom_call" | custom-call | tf_op jit(solution)/shard_map/branch_sent/pallas_call | solution.py:401
  31.6 0.6 %collective-permute-start.4 = (bf16[128,768]{1,0:T(8,128)(2,1)S(1)}, bf16[128,768]{1,0:T(8,128)(2,1)S(1)}, u32[]{:S(2)}, u32[]{:S(2)}) collective-permute-start(bf16[128,768]{1,0:T(8,128)(2,1)S(1)} %branch_sent.1), channel_id=1, source_target_pairs={{0,1},{1,0},{2,3},{3,2},{4,5},{5,4},{6,7},{7,6},{8,9},{9,8},{10,11... | collective-permute-start | bytes 589832 | tf_op jit(solution)/shard_map/ppermute | solution.py:423
  32.2 1.0 %collective-permute-done.2.late_ref = bf16[128,768]{1,0:T(8,128)(2,1)S(1)} collective-permute-done((bf16[128,768]{1,0:T(8,128)(2,1)}, bf16[128,768]{1,0:T(8,128)(2,1)S(1)}, u32[]{:S(2)}, u32[]{:S(2)}) %collective-permute-start.2) | collective-permute-done | bytes 196640 | tf_op jit(solution)/shard_map/ppermute | solution.py:423
  33.2 1.6 %branch_kept.1 = (bf16[128,768]{1,0:T(8,128)(2,1)S(1)}, f32[6,128,128]{2,1,0:T(8,128)S(1)}) custom-call(bf16[16,2,2,1280]{3,2,1,0:T(2,128)(2,1)S(1)} %bitcast.4, bf16[128,768]{1,0:T(8,128)(2,1)S(1)} %collective-permute-done.2.late_ref, bf16[208,256]{1,0:T(8,128)(2,1)S(1)} %collective-permute-done.3.tail_ref, f32[2,768]{1,0:T(2,128)S(1)} %get-tuple-element.35.norms_ref, ...), custom_call_target="tpu_custom_call" | custom-call | tf_op jit(solution)/shard_map/branch_kept/pallas_call | solution.py:401
  34.7 3.1 %collective-permute-done.4.got_ref = bf16[128,768]{1,0:T(8,128)(2,1)S(1)} collective-permute-done((bf16[128,768]{1,0:T(8,128)(2,1)S(1)}, bf16[128,768]{1,0:T(8,128)(2,1)S(1)}, u32[]{:S(2)}, u32[]{:S(2)}) %collective-permute-start.4) | collective-permute-done | bytes 196640 | tf_op jit(solution)/shard_map/ppermute | solution.py:423
  37.9 0.8 %residual.1 = bf16[128,1536]{1,0:T(8,128)(2,1)} custom-call(bf16[128,768]{1,0:T(8,128)(2,1)S(1)} %get-tuple-element.37.mine_ref, f32[6,128,128]{2,1,0:T(8,128)S(1)} %get-tuple-element.38.base_ref, bf16[128,768]{1,0:T(8,128)(2,1)S(1)} %collective-permute-done.4.got_ref), custom_call_target="tpu_custom_call" | custom-call | tf_op jit(solution)/shard_map/residual/pallas_call | solution.py:401
  (1 shorter events, 0.0 us)
Async XLA Ops:
  0.0 12.3 %collective-permute-start = (bf16[128,1536]{1,0:T(8,128)(2,1)}, bf16[128,1536]{1,0:T(8,128)(2,1)S(1)}, u32[]{:S(2)}, u32[]{:S(2)}) collective-permute-start(bf16[128,1536]{1,0:T(8,128)(2,1)} %bitcast.5), channel_id=1, source_target_pairs={{0,1},{1,0},{2,3},{3,2},{4,5},{5,4},{6,7},{7,6},{8,9},{9,8},{10,11... | collective-permute-start | bytes 1179656 | tf_op jit(solution)/shard_map/ppermute | solution.py:423
  4.4 1.0 %copy-start.1 = (bf16[1,128,1536]{2,1,0:T(8,128)(2,1)S(1)}, bf16[1,128,1536]{2,1,0:T(8,128)(2,1)}, u32[]{:S(2)}) copy-start(bf16[1,128,1536]{2,1,0:T(8,128)(2,1)} %frames_ref.1) | copy-start | bytes 1179652
  5.4 0.8 %copy-start.2 = (bf16[32,768]{1,0:T(8,128)(2,1)S(1)}, bf16[32,768]{1,0:T(8,128)(2,1)}, u32[]{:S(2)}) copy-start(bf16[32,768]{1,0:T(8,128)(2,1)} %taps_ref.3) | copy-start | bytes 147460
  10.9 5.0 %collective-permute-start.1 = (bf16[128,512]{1,0:T(8,128)(2,1)S(1)}, bf16[128,512]{1,0:T(8,128)(2,1)S(1)}, u32[]{:S(2)}, u32[]{:S(2)}) collective-permute-start(bf16[128,512]{1,0:T(8,128)(2,1)S(1)} %get-tuple-element.29), channel_id=1, source_target_pairs={{0,1},{1,0},{2,3},{3,2},{4,5},{5,4},{6,7},{7,6},{8,9},{9,8},{10,11... | collective-permute-start | bytes 393224 | tf_op jit(solution)/shard_map/ppermute | solution.py:423
  15.9 14.9 %all-to-all-start = ((bf16[32,2,1280]{2,1,0:T(2,128)(2,1)}), bf16[32,2,1280]{2,1,0:T(2,128)(2,1)S(1)}, u32[]{:S(2)}, u32[]{:S(2)}) async-start(bf16[32,2,1280]{2,1,0:T(2,128)(2,1)} %get-tuple-element.30), calls=%async_computation | async-start | bytes 327680 | tf_op jit(solution)/shard_map/all_to_all | solution.py:487
  22.0 7.0 %collective-permute-start.3 = (bf16[208,256]{1,0:T(8,128)(2,1)S(1)}, bf16[208,256]{1,0:T(8,128)(2,1)S(1)}, u32[]{:S(2)}, u32[]{:S(2)}) collective-permute-start(bf16[208,256]{1,0:T(8,128)(2,1)S(1)} %get-tuple-element.32), channel_id=1, source_target_pairs={{0,1},{1,0},{2,3},{3,2},{4,5},{5,4},{6,7},{7,6},{8,9},{9,8},{10,11... | collective-permute-start | bytes 319496 | tf_op jit(solution)/shard_map/ppermute | solution.py:423
  23.8 9.3 %collective-permute-start.2 = (bf16[128,768]{1,0:T(8,128)(2,1)}, bf16[128,768]{1,0:T(8,128)(2,1)S(1)}, u32[]{:S(2)}, u32[]{:S(2)}) collective-permute-start(bf16[128,768]{1,0:T(8,128)(2,1)} %get-tuple-element.31), channel_id=1, source_target_pairs={{0,1},{1,0},{2,3},{3,2},{4,5},{5,4},{6,7},{7,6},{8,9},{9,8},{10,11... | collective-permute-start | bytes 589832 | tf_op jit(solution)/shard_map/ppermute | solution.py:423
  24.1 1.7 %copy-start = (bf16[768,1536]{1,0:T(8,128)(2,1)S(1)}, bf16[768,1536]{1,0:T(8,128)(2,1)}, u32[]{:S(2)}) copy-start(bf16[768,1536]{1,0:T(8,128)(2,1)} %weight_ref.2) | copy-start | bytes 7077892
  31.6 6.3 %collective-permute-start.4 = (bf16[128,768]{1,0:T(8,128)(2,1)S(1)}, bf16[128,768]{1,0:T(8,128)(2,1)S(1)}, u32[]{:S(2)}, u32[]{:S(2)}) collective-permute-start(bf16[128,768]{1,0:T(8,128)(2,1)S(1)} %branch_sent.1), channel_id=1, source_target_pairs={{0,1},{1,0},{2,3},{3,2},{4,5},{5,4},{6,7},{7,6},{8,9},{9,8},{10,11... | collective-permute-start | bytes 589832 | tf_op jit(solution)/shard_map/ppermute | solution.py:423
